TPU v7x, 32 devices: a whole 2x2x4 slice. The times are simulated.
32 devices in a mesh: expert: 16 (over z, y, core), blk: 2 (over x).
Axes of the slice: x: 2, y: 2, z: 4, core: 2. Of those that a mesh axis runs over, the one named last changes fastest.
Arguments:
- tokens: bfloat16 [2048, 7168], P(('expert', 'blk')), may hold values from -6 to 6
- expert_ids: int32 [2048, 8], P(('expert', 'blk')), may hold values from 0 to 255, all different within a row; in each aligned block of 64 rows (0 to 63, 64 to 127, ...) at most 4 rows name the same one
- gate_weights: bfloat16 [2048, 8], P(('expert', 'blk')), may hold values from 0.099609375 to 1
- w_gate: bfloat16 [16, 7168, 2048], P('expert', None, 'blk'), may hold values from -0.0625 to 0.0625
- w_up: bfloat16 [16, 7168, 2048], P('expert', None, 'blk'), may hold values from -0.0625 to 0.0625
- w_down: bfloat16 [16, 2048, 7168], P('expert', None, 'blk'), may hold values from -0.125 to 0.125
Outputs:
- mixed_out: bfloat16 [2048, 7168], P(('expert', 'blk'))
Inputs may be any that keep to these rules, and one draw needn't show every extreme that they name: `expert_ids`: each row names 8 different experts; among the 64 rows of one device no expert is named more than 4 times, a bound that some block reaches.
All inputs are finite; a program needn't handle non-finite values.
Results may differ from a plain program's by a relative error of at most 0.0057.
Values may be sent and summed in bfloat16 or wider, within the bound.
No kernel may reach another device: no remote copies, remote signals or barrier semaphores. Data moves between devices by JAX's collectives and lax.ppermute only.
A program may use at most 128 MiB of HBM per device.

v0:
```python
import functools

import jax
import jax.numpy as jnp
from jax import lax
from jax.experimental import pallas as pl
from jax.experimental.pallas import tpu as pltpu
from jax.sharding import PartitionSpec as P

CAP = 4
CORE, ROW = 1, 2
MIB = 1 << 20
PARTS = 4
ROOM = 13 * MIB


def exchanged(block, mask, name):
    size = lax.axis_size("expert")
    with jax.named_scope(f"{name}_{mask}"):
        return lax.ppermute(block, "expert", [(i, i ^ mask) for i in range(size)])


def shifted(block, steps, name):
    size = lax.axis_size("blk")
    with jax.named_scope(f"{name}_{steps}"):
        return lax.ppermute(block, "blk", [(i, (i + steps) % size) for i in range(size)])


def matmul(left, right):
    return jnp.dot(left, right, preferred_element_type=jnp.float32)


def tile_of(size, most):
    return max(t for t in range(128, most + 1, 128) if size % t == 0)


def prepare_kernel(levels, place, ids_ref, other_ids_ref, gates_ref, tokens_ref, other_ref, chosen_ref, weights_ref):
    tokens, rows = tokens_ref.shape[0], chosen_ref.shape[0]
    half = rows // 2
    row = lax.broadcasted_iota(jnp.int32, (rows, tokens), 0)
    slot = lax.rem(row, CAP).astype(jnp.float32)
    other_side = lax.rem(row // CAP, 2) == 1
    near = place[0] ^ ((row // half) * ROW + lax.rem(row // (2 * CAP), levels) * (2 * ROW))
    far = near ^ CORE
    earlier = lax.broadcasted_iota(jnp.int32, (tokens, tokens), 0) < lax.broadcasted_iota(jnp.int32, (tokens, tokens), 1)
    earlier = earlier.astype(jnp.float32).astype(jnp.bfloat16)

    def table(ids, labels):
        hits = jnp.zeros((rows, tokens), jnp.float32)
        weights = jnp.zeros((rows, tokens), jnp.float32)
        for j in range(ids.shape[0]):
            match = ids[j:j + 1, :] == labels
            hits = jnp.where(match, 1.0, hits)
            weights = jnp.where(match, gates_ref[j:j + 1, :].astype(jnp.float32), weights)
        before = matmul(hits.astype(jnp.bfloat16), earlier)
        return (hits > 0) & (before == slot), weights

    own, own_weights = table(ids_ref, near)
    other, _ = table(other_ids_ref, near)
    away, away_weights = table(ids_ref, far)
    own_weights = jnp.where(own & ~other_side, own_weights, 0.0)
    away_weights = jnp.where(away & other_side, away_weights, 0.0)
    weights = [own_weights[:half], away_weights[:half], own_weights[half:], away_weights[half:]]
    weights_ref[...] = jnp.concatenate(weights, axis=0).astype(weights_ref.dtype)
    own = jnp.where(own & ~other_side, 1.0, 0.0).astype(jnp.bfloat16)
    other = jnp.where(other & other_side, 1.0, 0.0).astype(jnp.bfloat16)
    tile = tile_of(tokens_ref.shape[1], 1024)
    for n in range(0, tokens_ref.shape[1], tile):
        columns = slice(n, n + tile)
        picked = matmul(own, tokens_ref[:, columns]) + matmul(other, other_ref[:, columns])
        chosen_ref[:, columns] = picked.astype(chosen_ref.dtype)


def prepared(levels, place, ids, other_ids, gates, tokens, other_tokens):
    rows = 4 * levels * CAP
    vmem = pl.BlockSpec(memory_space=pltpu.VMEM)
    return pl.pallas_call(
        functools.partial(prepare_kernel, levels),
        in_specs=[pl.BlockSpec(memory_space=pltpu.SMEM)] + [vmem] * 5,
        out_specs=[vmem, vmem],
        out_shape=[
            jax.ShapeDtypeStruct((rows, tokens.shape[1]), jnp.bfloat16),
            jax.ShapeDtypeStruct((2 * rows, tokens.shape[0]), jnp.bfloat16),
        ],
        compiler_params=pltpu.CompilerParams(vmem_limit_bytes=ROOM),
        cost_estimate=pl.CostEstimate(
            flops=4 * rows * tokens.size, bytes_accessed=4 * (tokens.size + rows * tokens.shape[1]), transcendentals=0
        ),
    )(place, ids, other_ids, gates, tokens, other_tokens)


def parts_of(size, unit):
    return max(p for p in range(1, PARTS + 1) if size % (p * unit) == 0)


def copies_of(source, target, sem, dim):
    count = parts_of(source.shape[dim], 128)
    step = source.shape[dim] // count
    copies = []
    for p in range(count):
        part = (0, pl.ds(p * step, step)) if dim == 1 else (0, slice(None), pl.ds(p * step, step))
        copies.append(pltpu.make_async_copy(source.at[part], target.at[part], sem.at[p]))
    return copies


def load_kernel(source, target, sem):
    copies = copies_of(source, target, sem, 1)
    for copy in copies:
        copy.start()
    for copy in copies:
        copy.wait()


def loaded(weight):
    return pl.pallas_call(
        load_kernel,
        in_specs=[pl.BlockSpec(memory_space=pltpu.HBM)],
        out_specs=pl.BlockSpec(memory_space=pltpu.VMEM),
        out_shape=pltpu.VMEM(weight.shape, weight.dtype),
        scratch_shapes=[pltpu.SemaphoreType.DMA((PARTS,))],
        compiler_params=pltpu.CompilerParams(vmem_limit_bytes=ROOM),
        cost_estimate=pl.CostEstimate(
            flops=0, bytes_accessed=weight.size * weight.dtype.itemsize, transcendentals=0
        ),
    )(pltpu.with_memory_space_constraint(weight, pltpu.HBM))


def in_vmem(weight):
    return pltpu.with_memory_space_constraint(weight, pltpu.VMEM)


def gathered(pieces, ranges, rows_ref):
    rows = [piece[...].astype(jnp.float32)[start:stop] for piece, (start, stop) in zip(pieces, ranges)]
    rows_ref[...] = jnp.concatenate(rows, axis=0).astype(jnp.bfloat16)


def first_hidden_kernel(ranges, *refs):
    count = len(ranges)
    pieces, (gate_ref, up_hbm, out_ref, up_ref, rows_ref, gate_part, sem) = refs[:count], refs[count:]
    copies = copies_of(up_hbm, up_ref, sem, 2)
    for copy in copies:
        copy.start()
    gathered(pieces, ranges, rows_ref)
    tile = out_ref.shape[1] // len(copies)
    parts = [slice(p * tile, (p + 1) * tile) for p in range(len(copies))]
    for columns in parts:
        gate_part[:, columns] = jax.nn.silu(matmul(rows_ref[...], gate_ref[0, :, columns]))
    for columns, copy in zip(parts, copies):
        copy.wait()
        up_part = matmul(rows_ref[...], up_ref[0, :, columns])
        out_ref[:, columns] = (gate_part[:, columns] * up_part).astype(out_ref.dtype)


def hidden_kernel(ranges, *refs):
    count = len(ranges)
    pieces, (gate_ref, up_ref, out_ref, rows_ref) = refs[:count], refs[count:]
    gathered(pieces, ranges, rows_ref)
    tile = tile_of(out_ref.shape[1], 256)

    @pl.loop(0, out_ref.shape[1] // tile)
    def _(n):
        columns = pl.ds(pl.multiple_of(n * tile, tile), tile)
        gate_part = matmul(rows_ref[...], gate_ref[0, :, columns])
        up_part = matmul(rows_ref[...], up_ref[0, :, columns])
        out_ref[:, columns] = (jax.nn.silu(gate_part) * up_part).astype(out_ref.dtype)


def hidden_units(pieces, w_gate, w_up, first):
    depth, units = w_gate.shape[1:]
    ranges = [(start, stop) for _, start, stop in pieces]
    pieces = [piece for piece, _, _ in pieces]
    rows = sum(stop - start for start, stop in ranges)
    vmem = pl.BlockSpec(memory_space=pltpu.VMEM)
    place = pltpu.HBM if first else pltpu.VMEM
    out_shape = [jax.ShapeDtypeStruct((rows, units), jnp.bfloat16)]
    scratch = [pltpu.VMEM((rows, depth), jnp.bfloat16)]
    if first:
        out_shape.append(pltpu.VMEM(w_up.shape, w_up.dtype))
        scratch += [pltpu.VMEM((rows, units), jnp.float32), pltpu.SemaphoreType.DMA((PARTS,))]
    return pl.pallas_call(
        functools.partial(first_hidden_kernel if first else hidden_kernel, ranges),
        in_specs=[vmem] * (len(pieces) + 1) + [pl.BlockSpec(memory_space=place)],
        out_specs=[vmem] * len(out_shape),
        out_shape=out_shape,
        scratch_shapes=scratch,
        compiler_params=pltpu.CompilerParams(vmem_limit_bytes=max(ROOM, 10 * rows * (depth + units) + 2 * MIB)),
        cost_estimate=pl.CostEstimate(
            flops=4 * rows * depth * units,
            bytes_accessed=2 * rows * (depth + units),
            transcendentals=rows * units,
        ),
    )(*pieces, in_vmem(w_gate), pltpu.with_memory_space_constraint(w_up, place))


def down_kernel(half, groups, place, *refs):
    parts, (weight_ref, out_ref) = refs[:-2], refs[-2:]
    size, units = len(parts) // groups, parts[0].shape[1]
    tile = tile_of(out_ref.shape[1], 512)

    @pl.loop(0, out_ref.shape[1] // tile)
    def _(n):
        columns = pl.ds(pl.multiple_of(n * tile, tile), tile)
        total = jnp.zeros((out_ref.shape[0], tile), jnp.float32)
        for k in range(size):
            owner = lax.rem(place[0] + (size - k), size)
            rows = pl.ds(pl.multiple_of(owner * units, units), units)
            left = []
            for part in parts[k::size]:
                left += [part[-k * half:], part[:-k * half]] if k else [part[...]]
            total += matmul(jnp.concatenate(left, axis=0), weight_ref[0, rows, columns])
        out_ref[:, columns] = total.astype(out_ref.dtype)


def down_slices(groups, half, place, w_down):
    units, width = w_down.shape[1:]
    parts = sum(groups, [])
    rows = sum(parts[0].shape[0] for parts in groups)
    vmem = pl.BlockSpec(memory_space=pltpu.VMEM)
    return pl.pallas_call(
        functools.partial(down_kernel, half, len(groups)),
        in_specs=[pl.BlockSpec(memory_space=pltpu.SMEM)] + [vmem] * (len(parts) + 1),
        out_specs=vmem,
        out_shape=jax.ShapeDtypeStruct((rows, width), jnp.bfloat16),
        compiler_params=pltpu.CompilerParams(vmem_limit_bytes=max(ROOM, 8 * rows * (units + width) + 2 * MIB)),
        cost_estimate=pl.CostEstimate(
            flops=2 * rows * units * width,
            bytes_accessed=2 * rows * (units + width),
            transcendentals=0,
        ),
    )(place, *parts, in_vmem(w_down))


def mix_kernel(blocks, *refs):
    place, weights, pieces, out_ref = refs[0], refs[1], refs[2:-1], refs[-1]
    width = out_ref.shape[1] // blocks
    tile = tile_of(width, 512)
    for k in range(blocks):
        start = lax.rem(place[0] + k, blocks) * width
        for n in range(0, width, tile):
            rows = jnp.concatenate([piece[k, :, n:n + tile] for piece in pieces], axis=0)
            columns = pl.ds(pl.multiple_of(start + n, 128), tile)
            total = lax.dot_general(
                weights[...], rows, (((0,), (0,)), ((), ())), preferred_element_type=jnp.float32
            )
            out_ref[:, columns] = total.astype(out_ref.dtype)


def mixed_rows(weights, pieces, place):
    blocks, half, width = pieces[0].shape
    tokens = weights.shape[1]
    return pl.pallas_call(
        functools.partial(mix_kernel, blocks),
        in_specs=[pl.BlockSpec(memory_space=pltpu.SMEM)]
        + [pl.BlockSpec(memory_space=pltpu.VMEM)] * (len(pieces) + 1),
        out_specs=pl.BlockSpec(memory_space=pltpu.VMEM),
        out_shape=jax.ShapeDtypeStruct((tokens, blocks * width), jnp.bfloat16),
        compiler_params=pltpu.CompilerParams(
            vmem_limit_bytes=4 * blocks * width * (len(pieces) * half + tokens) + 2 * MIB
        ),
    )(place, weights, *pieces)


def on_device(tokens, expert_ids, gate_weights, w_gate, w_up, w_down):
    experts, blocks = lax.axis_size("expert"), lax.axis_size("blk")
    me, mine = lax.axis_index("expert"), lax.axis_index("blk")
    levels = experts // 4
    unit = 2 * CAP
    half = levels * unit
    down_mat = w_down[0]

    place = mine.reshape(1).astype(jnp.int32)
    ids = expert_ids.T
    other_ids = exchanged(ids, CORE, "ids")
    other_tokens = exchanged(tokens, CORE, "tokens")
    chosen, weighting = prepared(
        levels, me.reshape(1).astype(jnp.int32), ids, other_ids, gate_weights.T, tokens, other_tokens
    )
    w_gate, place, weighting, chosen = lax.optimization_barrier((w_gate, place, weighting, chosen))

    def split(rows):
        return [rows[z * unit:(z + 1) * unit] for z in range(levels)]

    def over_blk(piece, name):
        return [shifted(piece, k, name) for k in range(1, blocks)]

    stay, leave = split(chosen[:half]), split(chosen[half:])
    first = over_blk(stay[0], "blk_first")
    for z in range(levels - 1, 0, -1):
        stay[z] = exchanged(stay[z], z * 2 * ROW, "go_stay")
    leave[0] = exchanged(leave[0], ROW, "go_leave")
    early = jnp.concatenate([stay[1], leave[0]], axis=0)
    early, w_gate = lax.optimization_barrier((early, w_gate))
    w_gate = loaded(w_gate)
    leave[1:], w_gate = lax.optimization_barrier((leave[1:], w_gate))
    for z in range(levels - 1, 0, -1):
        leave[z] = exchanged(leave[z], z * 2 * ROW + ROW, "go_leave")
    late = jnp.concatenate(stay[2:], axis=0)
    most = jnp.concatenate([leave[1], *leave[3:]], axis=0)
    early_far, late_far = over_blk(early, "blk_early"), over_blk(late, "blk_late")
    most_far, last_far = over_blk(most, "blk_most"), over_blk(leave[2], "blk_last")
    cut = (levels - 2) * unit
    stay = [(stay[0], 0, unit), (early, 0, unit), (late, 0, cut)]
    for k in range(blocks - 1):
        stay += [(first[k], 0, unit), (early_far[k], 0, unit), (late_far[k], 0, cut)]
    order = [1, *range(3, levels)]
    places = [order.index(z) if z != 2 else None for z in range(1, levels)]

    def leaving(head, most, last):
        rows = [(head, unit, 2 * unit)]
        return rows + [(last, 0, unit) if p is None else (most, p * unit, (p + 1) * unit) for p in places]

    leave = sum([leaving(*arrays) for arrays in zip([early, *early_far], [most, *most_far], [leave[2], *last_far])], [])

    hidden, w_up = hidden_units(stay, w_gate, w_up, True)
    stay = [hidden] + over_blk(hidden, "hidden_stay")
    hidden, = hidden_units(leave, w_gate, w_up, False)
    stay, hidden, w_down = lax.optimization_barrier((stay, hidden, w_down))
    leave = [hidden] + over_blk(hidden, "hidden_leave")
    output = down_slices([stay, leave], half, place, loaded(w_down))
    stay, leave = output[:blocks * half], output[blocks * half:]

    def back(pieces, turn, name):
        received = [pieces[:, z * unit:(z + 1) * unit] for z in range(levels)]
        for z in range(levels - 1, -1, -1):
            mask = z * 2 * ROW + turn
            if mask:
                received[z] = exchanged(received[z], mask, name)
        return received

    def to_owners(slices, name):
        return jnp.stack([slices[0]] + [shifted(slices[k], blocks - k, name) for k in range(1, blocks)])

    def by_blk(output):
        return output.reshape(blocks, half, output.shape[1])

    leave = to_owners(by_blk(leave), "own_leave")
    stay = back(by_blk(stay), 0, "back_stay")
    leave = back(leave, ROW, "back_leave")
    stay = jnp.concatenate(stay, axis=1)
    stay, leave[-1] = lax.optimization_barrier((stay, leave[-1]))
    stay = to_owners(stay, "own_stay")
    leave = jnp.concatenate(leave, axis=1)
    returned = [stay, exchanged(stay, CORE, "pair_stay"), leave, exchanged(leave, CORE, "pair_leave")]
    return mixed_rows(weighting, returned, place)


def solution(mesh):
    return jax.shard_map(
        on_device,
        mesh=mesh,
        in_specs=(
            P(("expert", "blk"), None),
            P(("expert", "blk"), None),
            P(("expert", "blk"), None),
            P("expert", None, "blk"),
            P("expert", None, "blk"),
            P("expert", None, "blk"),
        ),
        out_specs=P(("expert", "blk"), None),
        check_vma=False,
    )
```

profile of v0, /device:TPU:0, one launch (start us, length us, event | category | flops | bytes accessed | tf_op | source)
XLA Modules:
  0.0 92.0 jit_solution(4420096530131538575)
XLA Ops:
  0.5 2.3 %collective-permute-done.other_ids_ref = s32[8,64]{1,0:T(8,128)S(1)} collective-permute-done((s32[8,64]{1,0:T(8,128)}, s32[8,64]{1,0:T(8,128)S(1)}, u32[]{:S(2)}, u32[]{:S(2)}) %collective-permute-start) | collective-permute-done | bytes 2080 | tf_op jit(solution)/shard_map/ids_1/ppermute | solution.py:20
  2.8 1.2 %copy-done = bf16[64,7168]{1,0:T(8,128)(2,1)S(1)} copy-done((bf16[64,7168]{1,0:T(8,128)(2,1)S(1)}, bf16[64,7168]{1,0:T(8,128)(2,1)}, u32[]{:S(2)}) %copy-start) | copy-done | bytes 917528
  6.2 3.0 %collective-permute-start.3 = (bf16[8,7168]{1,0:T(8,128)(2,1)S(1)}, bf16[8,7168]{1,0:T(8,128)(2,1)S(1)}, u32[]{:S(2)}, u32[]{:S(2)}) collective-permute-start(bf16[8,7168]{1,0:T(8,128)(2,1)S(1)} %get-tuple-element.52), channel_id=1, source_target_pairs={{0,4},{2,6},{4,0},{6,2},{8,12},{10,14},{12,8},{14,10},{16,20},{18,... | collective-permute-start | bytes 344072 | tf_op jit(solution)/shard_map/go_leave_2/ppermute | solution.py:20
  9.1 1.6 %collective-permute-start.2 = (bf16[8,7168]{1,0:T(8,128)(2,1)S(1)}, bf16[8,7168]{1,0:T(8,128)(2,1)S(1)}, u32[]{:S(2)}, u32[]{:S(2)}) collective-permute-start(bf16[8,7168]{1,0:T(8,128)(2,1)S(1)} %get-tuple-element.53), channel_id=1, source_target_pairs={{0,8},{2,10},{4,12},{6,14},{8,0},{10,2},{12,4},{14,6},{16,24},{18,... | collective-permute-start | bytes 344072 | tf_op jit(solution)/shard_map/go_stay_4/ppermute | solution.py:20
  10.7 2.6 %collective-permute-start.4 = (bf16[8,7168]{1,0:T(8,128)(2,1)S(1)}, bf16[8,7168]{1,0:T(8,128)(2,1)S(1)}, u32[]{:S(2)}, u32[]{:S(2)}) collective-permute-start(bf16[8,7168]{1,0:T(8,128)(2,1)S(1)} %get-tuple-element.51), channel_id=1, source_target_pairs={{0,16},{2,18},{4,20},{6,22},{8,24},{10,26},{12,28},{14,30},{16,0},... | collective-permute-start | bytes 344072 | tf_op jit(solution)/shard_map/go_stay_8/ppermute | solution.py:20
  13.5 1.5 %collective-permute-start.6 = (bf16[8,7168]{1,0:T(8,128)(2,1)S(1)}, bf16[8,7168]{1,0:T(8,128)(2,1)S(1)}, u32[]{:S(2)}, u32[]{:S(2)}) collective-permute-start(bf16[8,7168]{1,0:T(8,128)(2,1)S(1)} %get-tuple-element.54.refs_0_), channel_id=1, source_target_pairs={{0,1},{1,0},{2,3},{3,2},{4,5},{5,4},{6,7},{7,6},{8,9},{9,8},{10,11... | collective-permute-start | bytes 344072 | tf_op jit(solution)/shard_map/blk_first_1/ppermute | solution.py:26
  15.3 1.6 %collective-permute-start.7 = (bf16[16,7168]{1,0:T(8,128)(2,1)S(1)}, bf16[16,7168]{1,0:T(8,128)(2,1)S(1)}, u32[]{:S(2)}, u32[]{:S(2)}) collective-permute-start(bf16[16,7168]{1,0:T(8,128)(2,1)S(1)} %pad_maximum_fusion.2.refs_1_.refs_0_), channel_id=1, source_target_pairs={{0,1},{1,0},{2,3},{3,2},{4,5},{5,4},{6,7},{7,6},{8,9},{9,8},{10,11... | collective-permute-start | bytes 688136 | tf_op jit(solution)/shard_map/blk_early_1/ppermute | solution.py:26
  16.8 5.3 %shard_map.65.refs_6_.refs_8_ = bf16[1,7168,1024]{2,1,0:T(8,128)(2,1)S(1)} custom-call(bf16[1,7168,1024]{2,1,0:T(8,128)(2,1)} %source), custom_call_target="tpu_custom_call" | custom-call | bytes 14680064 | tf_op jit(solution)/shard_map/pallas_call | solution.py:115
  22.6 1.4 %collective-permute-start.8 = (bf16[16,7168]{1,0:T(8,128)(2,1)S(1)}, bf16[16,7168]{1,0:T(8,128)(2,1)S(1)}, u32[]{:S(2)}, u32[]{:S(2)}) collective-permute-start(bf16[16,7168]{1,0:T(8,128)(2,1)S(1)} %constant_dynamic-update-slice_fusion.refs_2_), channel_id=1, source_target_pairs={{0,1},{1,0},{2,3},{3,2},{4,5},{5,4},{6,7},{7,6},{8,9},{9,8},{10,11... | collective-permute-start | bytes 688136 | tf_op jit(solution)/shard_map/blk_late_1/ppermute | solution.py:26
  24.0 3.7 %collective-permute-start.11 = (bf16[8,7168]{1,0:T(8,128)(2,1)S(1)}, bf16[8,7168]{1,0:T(8,128)(2,1)S(1)}, u32[]{:S(2)}, u32[]{:S(2)}) collective-permute-start(bf16[8,7168]{1,0:T(8,128)(2,1)S(1)} %get-tuple-element.36), channel_id=1, source_target_pairs={{0,28},{2,30},{4,24},{6,26},{8,20},{10,22},{12,16},{14,18},{16,12}... | collective-permute-start | bytes 344072 | tf_op jit(solution)/shard_map/go_leave_14/ppermute | solution.py:20
  27.7 1.4 %collective-permute-done.10 = bf16[8,7168]{1,0:T(8,128)(2,1)S(1)} collective-permute-done((bf16[8,7168]{1,0:T(8,128)(2,1)S(1)}, bf16[8,7168]{1,0:T(8,128)(2,1)S(1)}, u32[]{:S(2)}, u32[]{:S(2)}) %collective-permute-start.10) | collective-permute-done | bytes 114720 | tf_op jit(solution)/shard_map/go_leave_6/ppermute | solution.py:20
  29.1 1.7 %collective-permute-start.12 = (bf16[8,7168]{1,0:T(8,128)(2,1)S(1)}, bf16[8,7168]{1,0:T(8,128)(2,1)S(1)}, u32[]{:S(2)}, u32[]{:S(2)}) collective-permute-start(bf16[8,7168]{1,0:T(8,128)(2,1)S(1)} %get-tuple-element.37), channel_id=1, source_target_pairs={{0,20},{2,22},{4,16},{6,18},{8,28},{10,30},{12,24},{14,26},{16,4},... | collective-permute-start | bytes 344072 | tf_op jit(solution)/shard_map/go_leave_10/ppermute | solution.py:20
  30.8 1.9 %collective-permute-done.11 = bf16[8,7168]{1,0:T(8,128)(2,1)S(1)} collective-permute-done((bf16[8,7168]{1,0:T(8,128)(2,1)S(1)}, bf16[8,7168]{1,0:T(8,128)(2,1)S(1)}, u32[]{:S(2)}, u32[]{:S(2)}) %collective-permute-start.11) | collective-permute-done | bytes 114720 | tf_op jit(solution)/shard_map/go_leave_14/ppermute | solution.py:20
  33.0 3.6 %collective-permute-done.12.refs_2_ = bf16[8,7168]{1,0:T(8,128)(2,1)S(1)} collective-permute-done((bf16[8,7168]{1,0:T(8,128)(2,1)S(1)}, bf16[8,7168]{1,0:T(8,128)(2,1)S(1)}, u32[]{:S(2)}, u32[]{:S(2)}) %collective-permute-start.12) | collective-permute-done | bytes 114720 | tf_op jit(solution)/shard_map/go_leave_10/ppermute | solution.py:20
  36.6 1.4 %collective-permute-start.14 = (bf16[8,7168]{1,0:T(8,128)(2,1)S(1)}, bf16[8,7168]{1,0:T(8,128)(2,1)S(1)}, u32[]{:S(2)}, u32[]{:S(2)}) collective-permute-start(bf16[8,7168]{1,0:T(8,128)(2,1)S(1)} %collective-permute-done.12.refs_2_), channel_id=1, source_target_pairs={{0,1},{1,0},{2,3},{3,2},{4,5},{5,4},{6,7},{7,6},{8,9},{9,8},{10,11... | collective-permute-start | bytes 344072 | tf_op jit(solution)/shard_map/blk_last_1/ppermute | solution.py:26
  38.0 7.4 %shard_map.66 = (bf16[64,1024]{1,0:T(8,128)(2,1)S(1)}, bf16[1,7168,1024]{2,1,0:T(8,128)(2,1)S(1)}) custom-call(bf16[8,7168]{1,0:T(8,128)(2,1)S(1)} %get-tuple-element.54.refs_0_, bf16[16,7168]{1,0:T(8,128)(2,1)S(1)} %pad_maximum_fusion.2.refs_1_.refs_0_, bf16[16,7168]{1,0:T(8,128)(2,1)S(1)} %constant_dynamic-update-slice_fusion.refs_2_, ...), custom_call_target="tpu_custom_call" | custom-call | flops 1879048192 | bytes 1048576 | tf_op jit(solution)/shard_map/pallas_call | solution.py:180
  46.1 5.8 %shard_map.67.refs_2_ = bf16[64,1024]{1,0:T(8,128)(2,1)S(1)} custom-call(bf16[16,7168]{1,0:T(8,128)(2,1)S(1)} %pad_maximum_fusion.2.refs_1_.refs_0_, bf16[16,7168]{1,0:T(8,128)(2,1)S(1)} %constant_dynamic-update-slice_fusion.2.refs_1_.refs_3_, bf16[8,7168]{1,0:T(8,128)(2,1)S(1)} %collective-permute-done.12.refs_2_, ...), custom_call_target="tpu_custom_call" | custom-call | flops 1879048192 | bytes 1048576 | tf_op jit(solution)/shard_map/pallas_call | solution.py:180
  51.9 1.5 %collective-permute-start.15 = (bf16[64,1024]{1,0:T(8,128)(2,1)S(1)}, bf16[64,1024]{1,0:T(8,128)(2,1)S(1)}, u32[]{:S(2)}, u32[]{:S(2)}) collective-permute-start(bf16[64,1024]{1,0:T(8,128)(2,1)S(1)} %shard_map.67.refs_2_), channel_id=1, source_target_pairs={{0,1},{1,0},{2,3},{3,2},{4,5},{5,4},{6,7},{7,6},{8,9},{9,8},{10,11... | collective-permute-start | bytes 393224 | tf_op jit(solution)/shard_map/hidden_leave_1/ppermute | solution.py:26
  53.4 5.3 %shard_map.68.refs_4_ = bf16[1,2048,3584]{2,1,0:T(8,128)(2,1)S(1)} custom-call(bf16[1,2048,3584]{2,1,0:T(8,128)(2,1)} %source.1), custom_call_target="tpu_custom_call" | custom-call | bytes 14680064 | tf_op jit(solution)/shard_map/pallas_call | solution.py:115
  58.7 3.2 %shard_map.69 = bf16[128,3584]{1,0:T(8,128)(2,1)S(1)} custom-call(s32[1]{0:T(128)} %bitcast.place.refs_0_, bf16[64,1024]{1,0:T(8,128)(2,1)S(1)} %get-tuple-element.39.refs_0_, bf16[64,1024]{1,0:T(8,128)(2,1)S(1)} %collective-permute-done.9.refs_1_, bf16[64,1024]{1,0:T(8,128)(2,1)S(1)} %shard_map.67.refs_2_, ...), custom_call_target="tpu_custom_call" | custom-call | flops 1879048192 | bytes 1441792 | tf_op jit(solution)/shard_map/pallas_call | solution.py:219
  62.8 3.1 %collective-permute-start.18 = (bf16[2,8,3584]{2,1,0:T(8,128)(2,1)S(1)}, bf16[2,8,3584]{2,1,0:T(8,128)(2,1)S(1)}, u32[]{:S(2)}, u32[]{:S(2)}) collective-permute-start(bf16[2,8,3584]{2,1,0:T(8,128)(2,1)S(1)} %get-tuple-element.62), channel_id=1, source_target_pairs={{0,24},{2,26},{4,28},{6,30},{8,16},{10,18},{12,20},{14,22},{16,8},... | collective-permute-start | bytes 344072 | tf_op jit(solution)/shard_map/back_stay_12/ppermute | solution.py:20
  65.8 1.4 %collective-permute-start.16 = (bf16[2,8,3584]{2,1,0:T(8,128)(2,1)S(1)}, bf16[2,8,3584]{2,1,0:T(8,128)(2,1)S(1)}, u32[]{:S(2)}, u32[]{:S(2)}) collective-permute-start(bf16[2,8,3584]{2,1,0:T(8,128)(2,1)S(1)} %get-tuple-element.64), channel_id=1, source_target_pairs={{0,8},{2,10},{4,12},{6,14},{8,0},{10,2},{12,4},{14,6},{16,24},{18,... | collective-permute-start | bytes 344072 | tf_op jit(solution)/shard_map/back_stay_4/ppermute | solution.py:20
  67.2 0.9 collective-permute-done.19
  68.2 3.5 %collective-permute-start.20 = (bf16[2,8,3584]{2,1,0:T(8,128)(2,1)S(1)}, bf16[2,8,3584]{2,1,0:T(8,128)(2,1)S(1)}, u32[]{:S(2)}, u32[]{:S(2)}) collective-permute-start(bf16[2,8,3584]{2,1,0:T(8,128)(2,1)S(1)} %get-tuple-element.56), channel_id=1, source_target_pairs={{0,28},{2,30},{4,24},{6,26},{8,20},{10,22},{12,16},{14,18},{16,12}... | collective-permute-start | bytes 344072 | tf_op jit(solution)/shard_map/back_leave_14/ppermute | solution.py:20
  71.7 5.1 %collective-permute-done.17 = bf16[2,8,3584]{2,1,0:T(8,128)(2,1)S(1)} collective-permute-done((bf16[2,8,3584]{2,1,0:T(8,128)(2,1)S(1)}, bf16[2,8,3584]{2,1,0:T(8,128)(2,1)S(1)}, u32[]{:S(2)}, u32[]{:S(2)}) %collective-permute-start.17) | collective-permute-done | bytes 114720 | tf_op jit(solution)/shard_map/back_stay_8/ppermute | solution.py:20
  76.8 1.6 %collective-permute-start.23 = (bf16[2,8,3584]{2,1,0:T(8,128)(2,1)S(1)}, bf16[2,8,3584]{2,1,0:T(8,128)(2,1)S(1)}, u32[]{:S(2)}, u32[]{:S(2)}) collective-permute-start(bf16[2,8,3584]{2,1,0:T(8,128)(2,1)S(1)} %get-tuple-element.57), channel_id=1, source_target_pairs={{0,4},{2,6},{4,0},{6,2},{8,12},{10,14},{12,8},{14,10},{16,20},{18,... | collective-permute-start | bytes 344072 | tf_op jit(solution)/shard_map/back_leave_2/ppermute | solution.py:20
  78.4 4.1 %collective-permute-start.25 = (bf16[2,8,3584]{2,1,0:T(8,128)(2,1)S(1)}, bf16[2,8,3584]{2,1,0:T(8,128)(2,1)S(1)}, u32[]{:S(2)}, u32[]{:S(2)}) collective-permute-start(bf16[2,8,3584]{2,1,0:T(8,128)(2,1)S(1)} %get-tuple-element.55), channel_id=1, source_target_pairs={{0,20},{2,22},{4,16},{6,18},{8,28},{10,30},{12,24},{14,26},{16,4},... | collective-permute-start | bytes 344072 | tf_op jit(solution)/shard_map/back_leave_10/ppermute | solution.py:20
  82.6 1.8 %collective-permute-start.21 = (bf16[32,3584]{1,0:T(8,128)(2,1)S(1)}, bf16[32,3584]{1,0:T(8,128)(2,1)S(1)}, u32[]{:S(2)}, u32[]{:S(2)}) collective-permute-start(bf16[32,3584]{1,0:T(8,128)(2,1)S(1)} %get-tuple-element.60), channel_id=1, source_target_pairs={{0,1},{1,0},{2,3},{3,2},{4,5},{5,4},{6,7},{7,6},{8,9},{9,8},{10,11... | collective-permute-start | bytes 688136 | tf_op jit(solution)/shard_map/own_stay_1/ppermute | solution.py:26
  84.4 2.1 %collective-permute-done.25 = bf16[2,8,3584]{2,1,0:T(8,128)(2,1)S(1)} collective-permute-done((bf16[2,8,3584]{2,1,0:T(8,128)(2,1)S(1)}, bf16[2,8,3584]{2,1,0:T(8,128)(2,1)S(1)}, u32[]{:S(2)}, u32[]{:S(2)}) %collective-permute-start.25) | collective-permute-done | bytes 114720 | tf_op jit(solution)/shard_map/back_leave_10/ppermute | solution.py:20
  86.6 2.0 %collective-permute-done.21 = bf16[32,3584]{1,0:T(8,128)(2,1)S(1)} collective-permute-done((bf16[32,3584]{1,0:T(8,128)(2,1)S(1)}, bf16[32,3584]{1,0:T(8,128)(2,1)S(1)}, u32[]{:S(2)}, u32[]{:S(2)}) %collective-permute-start.21) | collective-permute-done | bytes 229408 | tf_op jit(solution)/shard_map/own_stay_1/ppermute | solution.py:26
  88.8 1.8 %collective-permute-done.22.refs_3_ = bf16[2,32,3584]{2,1,0:T(8,128)(2,1)S(1)} collective-permute-done((bf16[2,32,3584]{2,1,0:T(8,128)(2,1)S(1)}, bf16[2,32,3584]{2,1,0:T(8,128)(2,1)S(1)}, u32[]{:S(2)}, u32[]{:S(2)}) %collective-permute-start.22) | collective-permute-done | bytes 458784 | tf_op jit(solution)/shard_map/pair_stay_1/ppermute | solution.py:20
  90.6 1.4 %shard_map.70 = bf16[64,7168]{1,0:T(8,128)(2,1)} custom-call(s32[1]{0:T(128)} %bitcast.place.refs_0_, bf16[128,64]{1,0:T(8,128)(2,1)S(1)} %get-tuple-element.28.refs_1_, bf16[2,32,3584]{2,1,0:T(8,128)(2,1)S(1)} %pad_maximum_fusion.1.refs_2_, bf16[2,32,3584]{2,1,0:T(8,128)(2,1)S(1)} %collective-permute-done.22.refs_3_, ...), custom_call_target="tpu_custom_call" | custom-call | tf_op jit(solution)/shard_map/pallas_call | solution.py:251
  (52 shorter events, 5.8 us)
Async XLA Ops:
  0.0 2.8 %collective-permute-start.1 = (bf16[64,7168]{1,0:T(8,128)(2,1)}, bf16[64,7168]{1,0:T(8,128)(2,1)S(1)}, u32[]{:S(2)}, u32[]{:S(2)}) collective-permute-start(bf16[64,7168]{1,0:T(8,128)(2,1)} %tokens_ref.1), channel_id=1, source_target_pairs={{0,2},{2,0},{4,6},{6,4},{8,10},{10,8},{12,14},{14,12},{16,18},{18,... | collective-permute-start | bytes 2752520 | tf_op jit(solution)/shard_map/tokens_1/ppermute | solution.py:20
  0.5 2.3 %collective-permute-start = (s32[8,64]{1,0:T(8,128)}, s32[8,64]{1,0:T(8,128)S(1)}, u32[]{:S(2)}, u32[]{:S(2)}) collective-permute-start(s32[8,64]{1,0:T(8,128)} %bitcast.11), channel_id=1, source_target_pairs={{0,2},{2,0},{4,6},{6,4},{8,10},{10,8},{12,14},{14,12},{16,18},{18,... | collective-permute-start | bytes 6152 | tf_op jit(solution)/shard_map/ids_1/ppermute | solution.py:20
  2.8 1.2 %copy-start = (bf16[64,7168]{1,0:T(8,128)(2,1)S(1)}, bf16[64,7168]{1,0:T(8,128)(2,1)}, u32[]{:S(2)}) copy-start(bf16[64,7168]{1,0:T(8,128)(2,1)} %tokens_ref.1) | copy-start | bytes 2752516
  4.0 0.7 copy-start.1
  4.6 0.7 copy-start.2
  6.2 8.8 %collective-permute-start.3 = (bf16[8,7168]{1,0:T(8,128)(2,1)S(1)}, bf16[8,7168]{1,0:T(8,128)(2,1)S(1)}, u32[]{:S(2)}, u32[]{:S(2)}) collective-permute-start(bf16[8,7168]{1,0:T(8,128)(2,1)S(1)} %get-tuple-element.52), channel_id=1, source_target_pairs={{0,4},{2,6},{4,0},{6,2},{8,12},{10,14},{12,8},{14,10},{16,20},{18,... | collective-permute-start | bytes 344072 | tf_op jit(solution)/shard_map/go_leave_2/ppermute | solution.py:20
  9.1 6.1 %collective-permute-start.2 = (bf16[8,7168]{1,0:T(8,128)(2,1)S(1)}, bf16[8,7168]{1,0:T(8,128)(2,1)S(1)}, u32[]{:S(2)}, u32[]{:S(2)}) collective-permute-start(bf16[8,7168]{1,0:T(8,128)(2,1)S(1)} %get-tuple-element.53), channel_id=1, source_target_pairs={{0,8},{2,10},{4,12},{6,14},{8,0},{10,2},{12,4},{14,6},{16,24},{18,... | collective-permute-start | bytes 344072 | tf_op jit(solution)/shard_map/go_stay_4/ppermute | solution.py:20
  10.7 11.9 %collective-permute-start.4 = (bf16[8,7168]{1,0:T(8,128)(2,1)S(1)}, bf16[8,7168]{1,0:T(8,128)(2,1)S(1)}, u32[]{:S(2)}, u32[]{:S(2)}) collective-permute-start(bf16[8,7168]{1,0:T(8,128)(2,1)S(1)} %get-tuple-element.51), channel_id=1, source_target_pairs={{0,16},{2,18},{4,20},{6,22},{8,24},{10,26},{12,28},{14,30},{16,0},... | collective-permute-start | bytes 344072 | tf_op jit(solution)/shard_map/go_stay_8/ppermute | solution.py:20
  13.3 9.3 %collective-permute-start.5 = (bf16[8,7168]{1,0:T(8,128)(2,1)S(1)}, bf16[8,7168]{1,0:T(8,128)(2,1)S(1)}, u32[]{:S(2)}, u32[]{:S(2)}) collective-permute-start(bf16[8,7168]{1,0:T(8,128)(2,1)S(1)} %get-tuple-element.50), channel_id=1, source_target_pairs={{0,24},{2,26},{4,28},{6,30},{8,16},{10,18},{12,20},{14,22},{16,8},... | collective-permute-start | bytes 344072 | tf_op jit(solution)/shard_map/go_stay_12/ppermute | solution.py:20
  13.5 24.5 %collective-permute-start.6 = (bf16[8,7168]{1,0:T(8,128)(2,1)S(1)}, bf16[8,7168]{1,0:T(8,128)(2,1)S(1)}, u32[]{:S(2)}, u32[]{:S(2)}) collective-permute-start(bf16[8,7168]{1,0:T(8,128)(2,1)S(1)} %get-tuple-element.54.refs_0_), channel_id=1, source_target_pairs={{0,1},{1,0},{2,3},{3,2},{4,5},{5,4},{6,7},{7,6},{8,9},{9,8},{10,11... | collective-permute-start | bytes 344072 | tf_op jit(solution)/shard_map/blk_first_1/ppermute | solution.py:26
  15.3 22.7 %collective-permute-start.7 = (bf16[16,7168]{1,0:T(8,128)(2,1)S(1)}, bf16[16,7168]{1,0:T(8,128)(2,1)S(1)}, u32[]{:S(2)}, u32[]{:S(2)}) collective-permute-start(bf16[16,7168]{1,0:T(8,128)(2,1)S(1)} %pad_maximum_fusion.2.refs_1_.refs_0_), channel_id=1, source_target_pairs={{0,1},{1,0},{2,3},{3,2},{4,5},{5,4},{6,7},{7,6},{8,9},{9,8},{10,11... | collective-permute-start | bytes 688136 | tf_op jit(solution)/shard_map/blk_early_1/ppermute | solution.py:26
  22.1 7.0 %collective-permute-start.10 = (bf16[8,7168]{1,0:T(8,128)(2,1)S(1)}, bf16[8,7168]{1,0:T(8,128)(2,1)S(1)}, u32[]{:S(2)}, u32[]{:S(2)}) collective-permute-start(bf16[8,7168]{1,0:T(8,128)(2,1)S(1)} %get-tuple-element.35), channel_id=1, source_target_pairs={{0,12},{2,14},{4,8},{6,10},{8,4},{10,6},{12,0},{14,2},{16,28},{18,... | collective-permute-start | bytes 344072 | tf_op jit(solution)/shard_map/go_leave_6/ppermute | solution.py:20
  22.6 15.4 %collective-permute-start.8 = (bf16[16,7168]{1,0:T(8,128)(2,1)S(1)}, bf16[16,7168]{1,0:T(8,128)(2,1)S(1)}, u32[]{:S(2)}, u32[]{:S(2)}) collective-permute-start(bf16[16,7168]{1,0:T(8,128)(2,1)S(1)} %constant_dynamic-update-slice_fusion.refs_2_), channel_id=1, source_target_pairs={{0,1},{1,0},{2,3},{3,2},{4,5},{5,4},{6,7},{7,6},{8,9},{9,8},{10,11... | collective-permute-start | bytes 688136 | tf_op jit(solution)/shard_map/blk_late_1/ppermute | solution.py:26
  24.0 8.7 %collective-permute-start.11 = (bf16[8,7168]{1,0:T(8,128)(2,1)S(1)}, bf16[8,7168]{1,0:T(8,128)(2,1)S(1)}, u32[]{:S(2)}, u32[]{:S(2)}) collective-permute-start(bf16[8,7168]{1,0:T(8,128)(2,1)S(1)} %get-tuple-element.36), channel_id=1, source_target_pairs={{0,28},{2,30},{4,24},{6,26},{8,20},{10,22},{12,16},{14,18},{16,12}... | collective-permute-start | bytes 344072 | tf_op jit(solution)/shard_map/go_leave_14/ppermute | solution.py:20
  29.1 7.5 %collective-permute-start.12 = (bf16[8,7168]{1,0:T(8,128)(2,1)S(1)}, bf16[8,7168]{1,0:T(8,128)(2,1)S(1)}, u32[]{:S(2)}, u32[]{:S(2)}) collective-permute-start(bf16[8,7168]{1,0:T(8,128)(2,1)S(1)} %get-tuple-element.37), channel_id=1, source_target_pairs={{0,20},{2,22},{4,16},{6,18},{8,28},{10,30},{12,24},{14,26},{16,4},... | collective-permute-start | bytes 344072 | tf_op jit(solution)/shard_map/go_leave_10/ppermute | solution.py:20
  32.7 13.4 %collective-permute-start.13 = (bf16[16,7168]{1,0:T(8,128)(2,1)S(1)}, bf16[16,7168]{1,0:T(8,128)(2,1)S(1)}, u32[]{:S(2)}, u32[]{:S(2)}) collective-permute-start(bf16[16,7168]{1,0:T(8,128)(2,1)S(1)} %constant_dynamic-update-slice_fusion.2.refs_1_.refs_3_), channel_id=1, source_target_pairs={{0,1},{1,0},{2,3},{3,2},{4,5},{5,4},{6,7},{7,6},{8,9},{9,8},{10,11... | collective-permute-start | bytes 688136 | tf_op jit(solution)/shard_map/blk_most_1/ppermute | solution.py:26
  36.6 9.5 %collective-permute-start.14 = (bf16[8,7168]{1,0:T(8,128)(2,1)S(1)}, bf16[8,7168]{1,0:T(8,128)(2,1)S(1)}, u32[]{:S(2)}, u32[]{:S(2)}) collective-permute-start(bf16[8,7168]{1,0:T(8,128)(2,1)S(1)} %collective-permute-done.12.refs_2_), channel_id=1, source_target_pairs={{0,1},{1,0},{2,3},{3,2},{4,5},{5,4},{6,7},{7,6},{8,9},{9,8},{10,11... | collective-permute-start | bytes 344072 | tf_op jit(solution)/shard_map/blk_last_1/ppermute | solution.py:26
  45.4 6.5 %collective-permute-start.9 = (bf16[64,1024]{1,0:T(8,128)(2,1)S(1)}, bf16[64,1024]{1,0:T(8,128)(2,1)S(1)}, u32[]{:S(2)}, u32[]{:S(2)}) collective-permute-start(bf16[64,1024]{1,0:T(8,128)(2,1)S(1)} %get-tuple-element.39.refs_0_), channel_id=1, source_target_pairs={{0,1},{1,0},{2,3},{3,2},{4,5},{5,4},{6,7},{7,6},{8,9},{9,8},{10,11... | collective-permute-start | bytes 393224 | tf_op jit(solution)/shard_map/hidden_stay_1/ppermute | solution.py:26
  51.9 6.8 %collective-permute-start.15 = (bf16[64,1024]{1,0:T(8,128)(2,1)S(1)}, bf16[64,1024]{1,0:T(8,128)(2,1)S(1)}, u32[]{:S(2)}, u32[]{:S(2)}) collective-permute-start(bf16[64,1024]{1,0:T(8,128)(2,1)S(1)} %shard_map.67.refs_2_), channel_id=1, source_target_pairs={{0,1},{1,0},{2,3},{3,2},{4,5},{5,4},{6,7},{7,6},{8,9},{9,8},{10,11... | collective-permute-start | bytes 393224 | tf_op jit(solution)/shard_map/hidden_leave_1/ppermute | solution.py:26
  62.0 6.1 %collective-permute-start.19 = (bf16[32,3584]{1,0:T(8,128)(2,1)S(1)}, bf16[32,3584]{1,0:T(8,128)(2,1)S(1)}, u32[]{:S(2)}, u32[]{:S(2)}) collective-permute-start(bf16[32,3584]{1,0:T(8,128)(2,1)S(1)} %get-tuple-element.45), channel_id=1, source_target_pairs={{0,1},{1,0},{2,3},{3,2},{4,5},{5,4},{6,7},{7,6},{8,9},{9,8},{10,11... | collective-permute-start | bytes 688136 | tf_op jit(solution)/shard_map/own_leave_1/ppermute | solution.py:26
  62.8 8.9 %collective-permute-start.18 = (bf16[2,8,3584]{2,1,0:T(8,128)(2,1)S(1)}, bf16[2,8,3584]{2,1,0:T(8,128)(2,1)S(1)}, u32[]{:S(2)}, u32[]{:S(2)}) collective-permute-start(bf16[2,8,3584]{2,1,0:T(8,128)(2,1)S(1)} %get-tuple-element.62), channel_id=1, source_target_pairs={{0,24},{2,26},{4,28},{6,30},{8,16},{10,18},{12,20},{14,22},{16,8},... | collective-permute-start | bytes 344072 | tf_op jit(solution)/shard_map/back_stay_12/ppermute | solution.py:20
  65.8 11.0 %collective-permute-start.17 = (bf16[2,8,3584]{2,1,0:T(8,128)(2,1)S(1)}, bf16[2,8,3584]{2,1,0:T(8,128)(2,1)S(1)}, u32[]{:S(2)}, u32[]{:S(2)}) collective-permute-start(bf16[2,8,3584]{2,1,0:T(8,128)(2,1)S(1)} %get-tuple-element.63), channel_id=1, source_target_pairs={{0,16},{2,18},{4,20},{6,22},{8,24},{10,26},{12,28},{14,30},{16,0},... | collective-permute-start | bytes 344072 | tf_op jit(solution)/shard_map/back_stay_8/ppermute | solution.py:20
  65.8 11.0 %collective-permute-start.16 = (bf16[2,8,3584]{2,1,0:T(8,128)(2,1)S(1)}, bf16[2,8,3584]{2,1,0:T(8,128)(2,1)S(1)}, u32[]{:S(2)}, u32[]{:S(2)}) collective-permute-start(bf16[2,8,3584]{2,1,0:T(8,128)(2,1)S(1)} %get-tuple-element.64), channel_id=1, source_target_pairs={{0,8},{2,10},{4,12},{6,14},{8,0},{10,2},{12,4},{14,6},{16,24},{18,... | collective-permute-start | bytes 344072 | tf_op jit(solution)/shard_map/back_stay_4/ppermute | solution.py:20
  68.2 14.4 %collective-permute-start.20 = (bf16[2,8,3584]{2,1,0:T(8,128)(2,1)S(1)}, bf16[2,8,3584]{2,1,0:T(8,128)(2,1)S(1)}, u32[]{:S(2)}, u32[]{:S(2)}) collective-permute-start(bf16[2,8,3584]{2,1,0:T(8,128)(2,1)S(1)} %get-tuple-element.56), channel_id=1, source_target_pairs={{0,28},{2,30},{4,24},{6,26},{8,20},{10,22},{12,16},{14,18},{16,12}... | collective-permute-start | bytes 344072 | tf_op jit(solution)/shard_map/back_leave_14/ppermute | solution.py:20
  76.8 7.6 %collective-permute-start.23 = (bf16[2,8,3584]{2,1,0:T(8,128)(2,1)S(1)}, bf16[2,8,3584]{2,1,0:T(8,128)(2,1)S(1)}, u32[]{:S(2)}, u32[]{:S(2)}) collective-permute-start(bf16[2,8,3584]{2,1,0:T(8,128)(2,1)S(1)} %get-tuple-element.57), channel_id=1, source_target_pairs={{0,4},{2,6},{4,0},{6,2},{8,12},{10,14},{12,8},{14,10},{16,20},{18,... | collective-permute-start | bytes 344072 | tf_op jit(solution)/shard_map/back_leave_2/ppermute | solution.py:20
  78.4 6.0 %collective-permute-start.24 = (bf16[2,8,3584]{2,1,0:T(8,128)(2,1)S(1)}, bf16[2,8,3584]{2,1,0:T(8,128)(2,1)S(1)}, u32[]{:S(2)}, u32[]{:S(2)}) collective-permute-start(bf16[2,8,3584]{2,1,0:T(8,128)(2,1)S(1)} %get-tuple-element.58), channel_id=1, source_target_pairs={{0,12},{2,14},{4,8},{6,10},{8,4},{10,6},{12,0},{14,2},{16,28},{18,... | collective-permute-start | bytes 344072 | tf_op jit(solution)/shard_map/back_leave_6/ppermute | solution.py:20
  78.4 8.1 %collective-permute-start.25 = (bf16[2,8,3584]{2,1,0:T(8,128)(2,1)S(1)}, bf16[2,8,3584]{2,1,0:T(8,128)(2,1)S(1)}, u32[]{:S(2)}, u32[]{:S(2)}) collective-permute-start(bf16[2,8,3584]{2,1,0:T(8,128)(2,1)S(1)} %get-tuple-element.55), channel_id=1, source_target_pairs={{0,20},{2,22},{4,16},{6,18},{8,28},{10,30},{12,24},{14,26},{16,4},... | collective-permute-start | bytes 344072 | tf_op jit(solution)/shard_map/back_leave_10/ppermute | solution.py:20
  82.6 6.1 %collective-permute-start.21 = (bf16[32,3584]{1,0:T(8,128)(2,1)S(1)}, bf16[32,3584]{1,0:T(8,128)(2,1)S(1)}, u32[]{:S(2)}, u32[]{:S(2)}) collective-permute-start(bf16[32,3584]{1,0:T(8,128)(2,1)S(1)} %get-tuple-element.60), channel_id=1, source_target_pairs={{0,1},{1,0},{2,3},{3,2},{4,5},{5,4},{6,7},{7,6},{8,9},{9,8},{10,11... | collective-permute-start | bytes 688136 | tf_op jit(solution)/shard_map/own_stay_1/ppermute | solution.py:26
  86.6 2.2 %collective-permute-start.26 = (bf16[2,32,3584]{2,1,0:T(8,128)(2,1)S(1)}, bf16[2,32,3584]{2,1,0:T(8,128)(2,1)S(1)}, u32[]{:S(2)}, u32[]{:S(2)}) collective-permute-start(bf16[2,32,3584]{2,1,0:T(8,128)(2,1)S(1)} %constant_dynamic-update-slice_fusion.4.refs_4_), channel_id=1, source_target_pairs={{0,2},{2,0},{4,6},{6,4},{8,10},{10,8},{12,14},{14,12},{16,18},{18,... | collective-permute-start | bytes 1376264 | tf_op jit(solution)/shard_map/pair_leave_1/ppermute | solution.py:20
  88.7 1.9 %collective-permute-start.22 = (bf16[2,32,3584]{2,1,0:T(8,128)(2,1)S(1)}, bf16[2,32,3584]{2,1,0:T(8,128)(2,1)S(1)}, u32[]{:S(2)}, u32[]{:S(2)}) collective-permute-start(bf16[2,32,3584]{2,1,0:T(8,128)(2,1)S(1)} %pad_maximum_fusion.1.refs_2_), channel_id=1, source_target_pairs={{0,2},{2,0},{4,6},{6,4},{8,10},{10,8},{12,14},{14,12},{16,18},{18,... | collective-permute-start | bytes 1376264 | tf_op jit(solution)/shard_map/pair_stay_1/ppermute | solution.py:20
where the time goes:
time: 92.2 us; the launch traced here: 92 us
  starting transfers between devices  38.3 us (42%)
  Pallas kernels  29.2 us (32%)
  waiting for transfers between devices  21.4 us (23%)
  local copies, waits for them, and re-layouts  2.81 us (3%)
    ppermute x18, starting transfers between devices, exchanged(): return lax.ppermute(block, 'expert', [(i, i ^ mask) for i in range(size)])  27.5 us
    ppermute x18, waiting for transfers between devices, exchanged(): return lax.ppermute(block, 'expert', [(i, i ^ mask) for i in range(size)])  18.4 us
    pallas_call x2, Pallas kernels, hidden_units(): pl.pallas_call(functools.partial(first_hidden_kernel if first else hidden...  13.2 us
    ppermute x9, starting transfers between devices, shifted(): lax.ppermute(block, 'blk', [(i, (i + steps) % size) for i in range(size)])  10.8 us
    pallas_call x2, Pallas kernels, loaded(): pl.pallas_call(load_kernel, in_specs=[pl.BlockSpec(memory_space=pltpu.HBM...  10.6 us
    pallas_call x1, Pallas kernels, down_slices(): pl.pallas_call(functools.partial(down_kernel, half, len(groups)), in_spec...  3.25 us
    ppermute x9, waiting for transfers between devices, shifted(): lax.ppermute(block, 'blk', [(i, (i + steps) % size) for i in range(size)])  2.96 us
    unnamed x11, local copies, waits for them, and re-layouts  2.59 us
  transfers between devices with their start and end apart: 27, of which 10 were waited for; matrix products, arithmetic and copies ran while one was open for 0% of the time, Pallas kernels for 26%

commit v1 on v0

--- a/solution.py
+++ b/solution.py
@@ -103,26 +103,33 @@
     return copies
 
 
-def load_kernel(source, target, sem):
-    copies = copies_of(source, target, sem, 1)
+def load_kernel(count, *refs):
+    sources, targets, sem = refs[:count], refs[count:-1], refs[-1]
+    copies = []
+    for number, (source, target) in enumerate(zip(sources, targets)):
+        if len(source.shape) == 2:
+            copies.append(pltpu.make_async_copy(source, target, sem.at[number, 0]))
+        else:
+            copies += copies_of(source, target, sem.at[number], 1)
     for copy in copies:
         copy.start()
     for copy in copies:
         copy.wait()
 
 
-def loaded(weight):
-    return pl.pallas_call(
-        load_kernel,
-        in_specs=[pl.BlockSpec(memory_space=pltpu.HBM)],
-        out_specs=pl.BlockSpec(memory_space=pltpu.VMEM),
-        out_shape=pltpu.VMEM(weight.shape, weight.dtype),
-        scratch_shapes=[pltpu.SemaphoreType.DMA((PARTS,))],
+def loaded(*arrays):
+    count = len(arrays)
+    return pl.pallas_call(
+        functools.partial(load_kernel, count),
+        in_specs=[pl.BlockSpec(memory_space=pltpu.HBM)] * count,
+        out_specs=[pl.BlockSpec(memory_space=pltpu.VMEM)] * count,
+        out_shape=[pltpu.VMEM(array.shape, array.dtype) for array in arrays],
+        scratch_shapes=[pltpu.SemaphoreType.DMA((count, PARTS))],
         compiler_params=pltpu.CompilerParams(vmem_limit_bytes=ROOM),
         cost_estimate=pl.CostEstimate(
-            flops=0, bytes_accessed=weight.size * weight.dtype.itemsize, transcendentals=0
-        ),
-    )(pltpu.with_memory_space_constraint(weight, pltpu.HBM))
+            flops=0, bytes_accessed=sum(a.size * a.dtype.itemsize for a in arrays), transcendentals=0
+        ),
+    )(*[pltpu.with_memory_space_constraint(array, pltpu.HBM) for array in arrays])
 
 
 def in_vmem(weight):
@@ -272,8 +279,9 @@
     ids = expert_ids.T
     other_ids = exchanged(ids, CORE, "ids")
     other_tokens = exchanged(tokens, CORE, "tokens")
+    near_ids, near_gates, near_tokens = loaded(ids, gate_weights.T, tokens)
     chosen, weighting = prepared(
-        levels, me.reshape(1).astype(jnp.int32), ids, other_ids, gate_weights.T, tokens, other_tokens
+        levels, me.reshape(1).astype(jnp.int32), near_ids, other_ids, near_gates, near_tokens, other_tokens
     )
     w_gate, place, weighting, chosen = lax.optimization_barrier((w_gate, place, weighting, chosen))
 
@@ -284,39 +292,38 @@
         return [shifted(piece, k, name) for k in range(1, blocks)]
 
     stay, leave = split(chosen[:half]), split(chosen[half:])
-    first = over_blk(stay[0], "blk_first")
     for z in range(levels - 1, 0, -1):
         stay[z] = exchanged(stay[z], z * 2 * ROW, "go_stay")
     leave[0] = exchanged(leave[0], ROW, "go_leave")
-    early = jnp.concatenate([stay[1], leave[0]], axis=0)
-    early, w_gate = lax.optimization_barrier((early, w_gate))
-    w_gate = loaded(w_gate)
-    leave[1:], w_gate = lax.optimization_barrier((leave[1:], w_gate))
+    early = jnp.concatenate([stay[0], stay[1], leave[0]], axis=0)
+    late = jnp.concatenate(stay[2:], axis=0)
+    early, leave[1:] = lax.optimization_barrier((early, leave[1:]))
+    early_far, late_far = over_blk(early, "blk_early"), over_blk(late, "blk_late")
+    early_far, leave[2] = lax.optimization_barrier((early_far, leave[2]))
     for z in range(levels - 1, 0, -1):
         leave[z] = exchanged(leave[z], z * 2 * ROW + ROW, "go_leave")
-    late = jnp.concatenate(stay[2:], axis=0)
-    most = jnp.concatenate([leave[1], *leave[3:]], axis=0)
-    early_far, late_far = over_blk(early, "blk_early"), over_blk(late, "blk_late")
-    most_far, last_far = over_blk(most, "blk_most"), over_blk(leave[2], "blk_last")
+    late, w_gate = lax.optimization_barrier((late, w_gate))
+    w_gate, = loaded(w_gate)
+    order = [*range(levels - 1, 1, -1)]
+    most = jnp.concatenate([leave[z] for z in order], axis=0)
+    most, w_gate = lax.optimization_barrier((most, w_gate))
+    most_far, last_far = over_blk(most, "blk_most"), over_blk(leave[1], "blk_last")
     cut = (levels - 2) * unit
-    stay = [(stay[0], 0, unit), (early, 0, unit), (late, 0, cut)]
-    for k in range(blocks - 1):
-        stay += [(first[k], 0, unit), (early_far[k], 0, unit), (late_far[k], 0, cut)]
-    order = [1, *range(3, levels)]
-    places = [order.index(z) if z != 2 else None for z in range(1, levels)]
+    stay = sum([[(a, 0, 2 * unit), (b, 0, cut)] for a, b in zip([early, *early_far], [late, *late_far])], [])
+    places = [order.index(z) if z != 1 else None for z in range(1, levels)]
 
     def leaving(head, most, last):
-        rows = [(head, unit, 2 * unit)]
+        rows = [(head, 2 * unit, 3 * unit)]
         return rows + [(last, 0, unit) if p is None else (most, p * unit, (p + 1) * unit) for p in places]
 
-    leave = sum([leaving(*arrays) for arrays in zip([early, *early_far], [most, *most_far], [leave[2], *last_far])], [])
+    leave = sum([leaving(*arrays) for arrays in zip([early, *early_far], [most, *most_far], [leave[1], *last_far])], [])
 
     hidden, w_up = hidden_units(stay, w_gate, w_up, True)
     stay = [hidden] + over_blk(hidden, "hidden_stay")
     hidden, = hidden_units(leave, w_gate, w_up, False)
     stay, hidden, w_down = lax.optimization_barrier((stay, hidden, w_down))
     leave = [hidden] + over_blk(hidden, "hidden_leave")
-    output = down_slices([stay, leave], half, place, loaded(w_down))
+    output = down_slices([stay, leave], half, place, loaded(w_down)[0])
     stay, leave = output[:blocks * half], output[blocks * half:]
 
     def back(pieces, turn, name):
@@ -337,7 +344,7 @@
     stay = back(by_blk(stay), 0, "back_stay")
     leave = back(leave, ROW, "back_leave")
     stay = jnp.concatenate(stay, axis=1)
-    stay, leave[-1] = lax.optimization_barrier((stay, leave[-1]))
+    stay, leave[0] = lax.optimization_barrier((stay, leave[0]))
     stay = to_owners(stay, "own_stay")
     leave = jnp.concatenate(leave, axis=1)
     returned = [stay, exchanged(stay, CORE, "pair_stay"), leave, exchanged(leave, CORE, "pair_leave")]

time: 92.2 us -> 92.5 us (level)
  local copies, waits for them, and re-layouts: 2.81 us -> 0.24 us
  Pallas kernels: 29.2 us -> 30.5 us
  waiting for transfers between devices: 21.4 us -> 22.4 us
    ppermute x18, waiting for transfers between devices: 18.4 us -> 22.4 us  [exchanged(): return lax.ppermute(block, 'expert', [(i, i ^ mask) for i in range(size)])]
    ppermute x9 -> x8, waiting for transfers between devices: 2.96 us -> 0.02 us  [shifted(): lax.ppermute(block, 'blk', [(i, (i + steps) % size) for i in range(size)])]
    ppermute x18, starting transfers between devices: 27.5 us -> 30.2 us  [exchanged(): return lax.ppermute(block, 'expert', [(i, i ^ mask) for i in range(size)])]
    unnamed x11 -> x4, local copies, waits for them, and re-layouts: 2.59 us -> 0.03 us
    ppermute x9 -> x8, starting transfers between devices: 10.8 us -> 8.66 us  [shifted(): lax.ppermute(block, 'blk', [(i, (i + steps) % size) for i in range(size)])]
    pallas_call x2 -> x3, Pallas kernels: 10.6 us -> 11.9 us  [loaded(): pl.pallas_call(functools.partial(load_kernel, count), in_specs=[pl.BlockS...]
  transfers between devices with their start and end apart: 27 -> 26, of which waited for: 10 -> 10; matrix products, arithmetic and copies ran while one was open for 0% -> 0% of each run, Pallas kernels for 26% -> 27%
where the time goes in v1:
time: 92.5 us; the launch traced here: 92.3 us
  starting transfers between devices  38.9 us (42%)
  Pallas kernels  30.5 us (33%)
  waiting for transfers between devices  22.4 us (24%)
    ppermute x18, starting transfers between devices, exchanged(): return lax.ppermute(block, 'expert', [(i, i ^ mask) for i in range(size)])  30.2 us
    ppermute x18, waiting for transfers between devices, exchanged(): return lax.ppermute(block, 'expert', [(i, i ^ mask) for i in range(size)])  22.4 us
    pallas_call x2, Pallas kernels, hidden_units(): pl.pallas_call(functools.partial(first_hidden_kernel if first else hidden...  13.2 us
    pallas_call x3, Pallas kernels, loaded(): pl.pallas_call(functools.partial(load_kernel, count), in_specs=[pl.BlockS...  11.9 us
    ppermute x8, starting transfers between devices, shifted(): lax.ppermute(block, 'blk', [(i, (i + steps) % size) for i in range(size)])  8.66 us
    pallas_call x1, Pallas kernels, down_slices(): pl.pallas_call(functools.partial(down_kernel, half, len(groups)), in_spec...  3.24 us
  transfers between devices with their start and end apart: 26, of which 10 were waited for; matrix products, arithmetic and copies ran while one was open for 0% of the time, Pallas kernels for 27%

profile of v1, /device:TPU:0, one launch (start us, length us, event | category | flops | bytes accessed | tf_op | source)
XLA Modules:
  0.0 92.3 jit_solution(15013302360726538354)
XLA Ops:
  0.5 1.3 %shard_map.64 = (s32[8,64]{1,0:T(8,128)S(1)}, bf16[8,64]{1,0:T(8,128)(2,1)S(1)}, bf16[64,7168]{1,0:T(8,128)(2,1)S(1)}) custom-call(s32[8,64]{1,0:T(8,128)} %bitcast.15, bf16[8,64]{1,0:T(8,128)(2,1)} %bitcast.16, bf16[64,7168]{1,0:T(8,128)(2,1)} %refs_2_.1), custom_call_target="tpu_custom_call" | custom-call | bytes 920576 | tf_op jit(solution)/shard_map/pallas_call | solution.py:122
  1.8 0.9 %collective-permute-done.other_ids_ref = s32[8,64]{1,0:T(8,128)S(1)} collective-permute-done((s32[8,64]{1,0:T(8,128)}, s32[8,64]{1,0:T(8,128)S(1)}, u32[]{:S(2)}, u32[]{:S(2)}) %collective-permute-start) | collective-permute-done | bytes 2080 | tf_op jit(solution)/shard_map/ids_1/ppermute | solution.py:20
  2.8 0.8 shard_map.65
  3.6 3.0 %collective-permute-start.2 = (bf16[8,7168]{1,0:T(8,128)(2,1)S(1)}, bf16[8,7168]{1,0:T(8,128)(2,1)S(1)}, u32[]{:S(2)}, u32[]{:S(2)}) collective-permute-start(bf16[8,7168]{1,0:T(8,128)(2,1)S(1)} %get-tuple-element.67), channel_id=1, source_target_pairs={{0,8},{2,10},{4,12},{6,14},{8,0},{10,2},{12,4},{14,6},{16,24},{18,... | collective-permute-start | bytes 344072 | tf_op jit(solution)/shard_map/go_stay_4/ppermute | solution.py:20
  6.6 1.5 %collective-permute-start.3 = (bf16[8,7168]{1,0:T(8,128)(2,1)S(1)}, bf16[8,7168]{1,0:T(8,128)(2,1)S(1)}, u32[]{:S(2)}, u32[]{:S(2)}) collective-permute-start(bf16[8,7168]{1,0:T(8,128)(2,1)S(1)} %get-tuple-element.66), channel_id=1, source_target_pairs={{0,4},{2,6},{4,0},{6,2},{8,12},{10,14},{12,8},{14,10},{16,20},{18,... | collective-permute-start | bytes 344072 | tf_op jit(solution)/shard_map/go_leave_2/ppermute | solution.py:20
  8.1 2.6 %collective-permute-start.4 = (bf16[8,7168]{1,0:T(8,128)(2,1)S(1)}, bf16[8,7168]{1,0:T(8,128)(2,1)S(1)}, u32[]{:S(2)}, u32[]{:S(2)}) collective-permute-start(bf16[8,7168]{1,0:T(8,128)(2,1)S(1)} %get-tuple-element.62), channel_id=1, source_target_pairs={{0,16},{2,18},{4,20},{6,22},{8,24},{10,26},{12,28},{14,30},{16,0},... | collective-permute-start | bytes 344072 | tf_op jit(solution)/shard_map/go_stay_8/ppermute | solution.py:20
  11.6 1.6 %collective-permute-start.6 = (bf16[24,7168]{1,0:T(8,128)(2,1)S(1)}, bf16[24,7168]{1,0:T(8,128)(2,1)S(1)}, u32[]{:S(2)}, u32[]{:S(2)}) collective-permute-start(bf16[24,7168]{1,0:T(8,128)(2,1)S(1)} %pad_maximum_fusion.2.refs_0_), channel_id=1, source_target_pairs={{0,1},{1,0},{2,3},{3,2},{4,5},{5,4},{6,7},{7,6},{8,9},{9,8},{10,11... | collective-permute-start | bytes 1032200 | tf_op jit(solution)/shard_map/blk_early_1/ppermute | solution.py:26
  13.1 4.3 %collective-permute-start.8 = (bf16[8,7168]{1,0:T(8,128)(2,1)S(1)}, bf16[8,7168]{1,0:T(8,128)(2,1)S(1)}, u32[]{:S(2)}, u32[]{:S(2)}) collective-permute-start(bf16[8,7168]{1,0:T(8,128)(2,1)S(1)} %get-tuple-element.45), channel_id=1, source_target_pairs={{0,28},{2,30},{4,24},{6,26},{8,20},{10,22},{12,16},{14,18},{16,12}... | collective-permute-start | bytes 344072 | tf_op jit(solution)/shard_map/go_leave_14/ppermute | solution.py:20
  17.4 4.5 %collective-permute-done.4 = bf16[8,7168]{1,0:T(8,128)(2,1)S(1)} collective-permute-done((bf16[8,7168]{1,0:T(8,128)(2,1)S(1)}, bf16[8,7168]{1,0:T(8,128)(2,1)S(1)}, u32[]{:S(2)}, u32[]{:S(2)}) %collective-permute-start.4) | collective-permute-done | bytes 114720 | tf_op jit(solution)/shard_map/go_stay_8/ppermute | solution.py:20
  21.9 2.2 %collective-permute-start.9 = (bf16[8,7168]{1,0:T(8,128)(2,1)S(1)}, bf16[8,7168]{1,0:T(8,128)(2,1)S(1)}, u32[]{:S(2)}, u32[]{:S(2)}) collective-permute-start(bf16[8,7168]{1,0:T(8,128)(2,1)S(1)} %get-tuple-element.46), channel_id=1, source_target_pairs={{0,20},{2,22},{4,16},{6,18},{8,28},{10,30},{12,24},{14,26},{16,4},... | collective-permute-start | bytes 344072 | tf_op jit(solution)/shard_map/go_leave_10/ppermute | solution.py:20
  24.1 1.6 %collective-permute-start.7 = (bf16[16,7168]{1,0:T(8,128)(2,1)S(1)}, bf16[16,7168]{1,0:T(8,128)(2,1)S(1)}, u32[]{:S(2)}, u32[]{:S(2)}) collective-permute-start(bf16[16,7168]{1,0:T(8,128)(2,1)S(1)} %constant_dynamic-update-slice_fusion.refs_1_), channel_id=1, source_target_pairs={{0,1},{1,0},{2,3},{3,2},{4,5},{5,4},{6,7},{7,6},{8,9},{9,8},{10,11... | collective-permute-start | bytes 688136 | tf_op jit(solution)/shard_map/blk_late_1/ppermute | solution.py:26
  25.7 5.3 %shard_map.66.refs_4_.refs_8_ = bf16[1,7168,1024]{2,1,0:T(8,128)(2,1)S(1)} custom-call(bf16[1,7168,1024]{2,1,0:T(8,128)(2,1)} %refs_0_), custom_call_target="tpu_custom_call" | custom-call | bytes 14680064 | tf_op jit(solution)/shard_map/pallas_call | solution.py:122
  31.0 2.5 %collective-permute-start.11 = (bf16[8,7168]{1,0:T(8,128)(2,1)S(1)}, bf16[8,7168]{1,0:T(8,128)(2,1)S(1)}, u32[]{:S(2)}, u32[]{:S(2)}) collective-permute-start(bf16[8,7168]{1,0:T(8,128)(2,1)S(1)} %get-tuple-element.50), channel_id=1, source_target_pairs={{0,12},{2,14},{4,8},{6,10},{8,4},{10,6},{12,0},{14,2},{16,28},{18,... | collective-permute-start | bytes 344072 | tf_op jit(solution)/shard_map/go_leave_6/ppermute | solution.py:20
  34.1 2.6 %collective-permute-done.11.refs_1_ = bf16[8,7168]{1,0:T(8,128)(2,1)S(1)} collective-permute-done((bf16[8,7168]{1,0:T(8,128)(2,1)S(1)}, bf16[8,7168]{1,0:T(8,128)(2,1)S(1)}, u32[]{:S(2)}, u32[]{:S(2)}) %collective-permute-start.11) | collective-permute-done | bytes 114720 | tf_op jit(solution)/shard_map/go_leave_6/ppermute | solution.py:20
  37.3 7.4 %shard_map.67 = (bf16[64,1024]{1,0:T(8,128)(2,1)S(1)}, bf16[1,7168,1024]{2,1,0:T(8,128)(2,1)S(1)}) custom-call(bf16[24,7168]{1,0:T(8,128)(2,1)S(1)} %pad_maximum_fusion.2.refs_0_, bf16[16,7168]{1,0:T(8,128)(2,1)S(1)} %constant_dynamic-update-slice_fusion.refs_1_, bf16[24,7168]{1,0:T(8,128)(2,1)S(1)} %collective-permute-done.6.refs_2_.refs_4_, ...), custom_call_target="tpu_custom_call" | custom-call | flops 1879048192 | bytes 1048576 | tf_op jit(solution)/shard_map/pallas_call | solution.py:187
  44.7 1.6 %collective-permute-start.10 = (bf16[64,1024]{1,0:T(8,128)(2,1)S(1)}, bf16[64,1024]{1,0:T(8,128)(2,1)S(1)}, u32[]{:S(2)}, u32[]{:S(2)}) collective-permute-start(bf16[64,1024]{1,0:T(8,128)(2,1)S(1)} %get-tuple-element.53.refs_0_), channel_id=1, source_target_pairs={{0,1},{1,0},{2,3},{3,2},{4,5},{5,4},{6,7},{7,6},{8,9},{9,8},{10,11... | collective-permute-start | bytes 393224 | tf_op jit(solution)/shard_map/hidden_stay_1/ppermute | solution.py:26
  46.2 5.8 %shard_map.68.refs_2_ = bf16[64,1024]{1,0:T(8,128)(2,1)S(1)} custom-call(bf16[24,7168]{1,0:T(8,128)(2,1)S(1)} %pad_maximum_fusion.2.refs_0_, bf16[8,7168]{1,0:T(8,128)(2,1)S(1)} %collective-permute-done.11.refs_1_, bf16[16,7168]{1,0:T(8,128)(2,1)S(1)} %pad_maximum_fusion.3.refs_2_.refs_3_, bf16[16,7168]{1,0:T(8,128)(2,1)S(1)} %pad_maximum_fusion.3.refs_2_.refs_3_, ...), custom_call_target="tpu_custom_call" | custom-call | flops 1879048192 | bytes 1048576 | tf_op jit(solution)/shard_map/pallas_call | solution.py:187
  52.7 5.3 %shard_map.69.refs_4_ = bf16[1,2048,3584]{2,1,0:T(8,128)(2,1)S(1)} custom-call(bf16[1,2048,3584]{2,1,0:T(8,128)(2,1)} %refs_0_.1), custom_call_target="tpu_custom_call" | custom-call | bytes 14680064 | tf_op jit(solution)/shard_map/pallas_call | solution.py:122
  58.0 3.2 %shard_map.70 = bf16[128,3584]{1,0:T(8,128)(2,1)S(1)} custom-call(s32[1]{0:T(128)} %bitcast.place.refs_0_, bf16[64,1024]{1,0:T(8,128)(2,1)S(1)} %get-tuple-element.53.refs_0_, bf16[64,1024]{1,0:T(8,128)(2,1)S(1)} %collective-permute-done.10.refs_1_, bf16[64,1024]{1,0:T(8,128)(2,1)S(1)} %shard_map.68.refs_2_, ...), custom_call_target="tpu_custom_call" | custom-call | flops 1879048192 | bytes 1441792 | tf_op jit(solution)/shard_map/pallas_call | solution.py:226
  61.3 1.6 %collective-permute-start.18 = (bf16[32,3584]{1,0:T(8,128)(2,1)S(1)}, bf16[32,3584]{1,0:T(8,128)(2,1)S(1)}, u32[]{:S(2)}, u32[]{:S(2)}) collective-permute-start(bf16[32,3584]{1,0:T(8,128)(2,1)S(1)} %get-tuple-element.59), channel_id=1, source_target_pairs={{0,1},{1,0},{2,3},{3,2},{4,5},{5,4},{6,7},{7,6},{8,9},{9,8},{10,11... | collective-permute-start | bytes 688136 | tf_op jit(solution)/shard_map/own_leave_1/ppermute | solution.py:26
  62.9 2.1 %collective-permute-start.15 = (bf16[2,8,3584]{2,1,0:T(8,128)(2,1)S(1)}, bf16[2,8,3584]{2,1,0:T(8,128)(2,1)S(1)}, u32[]{:S(2)}, u32[]{:S(2)}) collective-permute-start(bf16[2,8,3584]{2,1,0:T(8,128)(2,1)S(1)} %get-tuple-element.78), channel_id=1, source_target_pairs={{0,8},{2,10},{4,12},{6,14},{8,0},{10,2},{12,4},{14,6},{16,24},{18,... | collective-permute-start | bytes 344072 | tf_op jit(solution)/shard_map/back_stay_4/ppermute | solution.py:20
  65.0 1.4 %collective-permute-start.16 = (bf16[2,8,3584]{2,1,0:T(8,128)(2,1)S(1)}, bf16[2,8,3584]{2,1,0:T(8,128)(2,1)S(1)}, u32[]{:S(2)}, u32[]{:S(2)}) collective-permute-start(bf16[2,8,3584]{2,1,0:T(8,128)(2,1)S(1)} %get-tuple-element.77), channel_id=1, source_target_pairs={{0,16},{2,18},{4,20},{6,22},{8,24},{10,26},{12,28},{14,30},{16,0},... | collective-permute-start | bytes 344072 | tf_op jit(solution)/shard_map/back_stay_8/ppermute | solution.py:20
  66.4 1.4 %collective-permute-start.17 = (bf16[2,8,3584]{2,1,0:T(8,128)(2,1)S(1)}, bf16[2,8,3584]{2,1,0:T(8,128)(2,1)S(1)}, u32[]{:S(2)}, u32[]{:S(2)}) collective-permute-start(bf16[2,8,3584]{2,1,0:T(8,128)(2,1)S(1)} %get-tuple-element.76), channel_id=1, source_target_pairs={{0,24},{2,26},{4,28},{6,30},{8,16},{10,18},{12,20},{14,22},{16,8},... | collective-permute-start | bytes 344072 | tf_op jit(solution)/shard_map/back_stay_12/ppermute | solution.py:20
  68.5 3.2 %collective-permute-done.16 = bf16[2,8,3584]{2,1,0:T(8,128)(2,1)S(1)} collective-permute-done((bf16[2,8,3584]{2,1,0:T(8,128)(2,1)S(1)}, bf16[2,8,3584]{2,1,0:T(8,128)(2,1)S(1)}, u32[]{:S(2)}, u32[]{:S(2)}) %collective-permute-start.16) | collective-permute-done | bytes 114720 | tf_op jit(solution)/shard_map/back_stay_8/ppermute | solution.py:20
  71.7 2.9 %collective-permute-done.17 = bf16[2,8,3584]{2,1,0:T(8,128)(2,1)S(1)} collective-permute-done((bf16[2,8,3584]{2,1,0:T(8,128)(2,1)S(1)}, bf16[2,8,3584]{2,1,0:T(8,128)(2,1)S(1)}, u32[]{:S(2)}, u32[]{:S(2)}) %collective-permute-start.17) | collective-permute-done | bytes 114720 | tf_op jit(solution)/shard_map/back_stay_12/ppermute | solution.py:20
  74.7 4.9 %collective-permute-start.22 = (bf16[2,8,3584]{2,1,0:T(8,128)(2,1)S(1)}, bf16[2,8,3584]{2,1,0:T(8,128)(2,1)S(1)}, u32[]{:S(2)}, u32[]{:S(2)}) collective-permute-start(bf16[2,8,3584]{2,1,0:T(8,128)(2,1)S(1)} %get-tuple-element.71), channel_id=1, source_target_pairs={{0,12},{2,14},{4,8},{6,10},{8,4},{10,6},{12,0},{14,2},{16,28},{18,... | collective-permute-start | bytes 344072 | tf_op jit(solution)/shard_map/back_leave_6/ppermute | solution.py:20
  79.6 1.2 %collective-permute-start.23 = (bf16[2,8,3584]{2,1,0:T(8,128)(2,1)S(1)}, bf16[2,8,3584]{2,1,0:T(8,128)(2,1)S(1)}, u32[]{:S(2)}, u32[]{:S(2)}) collective-permute-start(bf16[2,8,3584]{2,1,0:T(8,128)(2,1)S(1)} %get-tuple-element.72), channel_id=1, source_target_pairs={{0,20},{2,22},{4,16},{6,18},{8,28},{10,30},{12,24},{14,26},{16,4},... | collective-permute-start | bytes 344072 | tf_op jit(solution)/shard_map/back_leave_10/ppermute | solution.py:20
  80.8 1.0 %collective-permute-start.24 = (bf16[2,8,3584]{2,1,0:T(8,128)(2,1)S(1)}, bf16[2,8,3584]{2,1,0:T(8,128)(2,1)S(1)}, u32[]{:S(2)}, u32[]{:S(2)}) collective-permute-start(bf16[2,8,3584]{2,1,0:T(8,128)(2,1)S(1)} %get-tuple-element.69), channel_id=1, source_target_pairs={{0,28},{2,30},{4,24},{6,26},{8,20},{10,22},{12,16},{14,18},{16,12}... | collective-permute-start | bytes 344072 | tf_op jit(solution)/shard_map/back_leave_14/ppermute | solution.py:20
  82.6 4.5 %collective-permute-done.23 = bf16[2,8,3584]{2,1,0:T(8,128)(2,1)S(1)} collective-permute-done((bf16[2,8,3584]{2,1,0:T(8,128)(2,1)S(1)}, bf16[2,8,3584]{2,1,0:T(8,128)(2,1)S(1)}, u32[]{:S(2)}, u32[]{:S(2)}) %collective-permute-start.23) | collective-permute-done | bytes 114720 | tf_op jit(solution)/shard_map/back_leave_10/ppermute | solution.py:20
  87.1 1.3 %collective-permute-done.24 = bf16[2,8,3584]{2,1,0:T(8,128)(2,1)S(1)} collective-permute-done((bf16[2,8,3584]{2,1,0:T(8,128)(2,1)S(1)}, bf16[2,8,3584]{2,1,0:T(8,128)(2,1)S(1)}, u32[]{:S(2)}, u32[]{:S(2)}) %collective-permute-start.24) | collective-permute-done | bytes 114720 | tf_op jit(solution)/shard_map/back_leave_14/ppermute | solution.py:20
  89.1 1.2 %collective-permute-done.25.refs_5_ = bf16[2,32,3584]{2,1,0:T(8,128)(2,1)S(1)} collective-permute-done((bf16[2,32,3584]{2,1,0:T(8,128)(2,1)S(1)}, bf16[2,32,3584]{2,1,0:T(8,128)(2,1)S(1)}, u32[]{:S(2)}, u32[]{:S(2)}) %collective-permute-start.25) | collective-permute-done | bytes 458784 | tf_op jit(solution)/shard_map/pair_leave_1/ppermute | solution.py:20
  91.0 1.4 %shard_map.71 = bf16[64,7168]{1,0:T(8,128)(2,1)} custom-call(s32[1]{0:T(128)} %bitcast.place.refs_0_, bf16[128,64]{1,0:T(8,128)(2,1)S(1)} %get-tuple-element.38.refs_1_, bf16[2,32,3584]{2,1,0:T(8,128)(2,1)S(1)} %pad_maximum_fusion.1.refs_2_, bf16[2,32,3584]{2,1,0:T(8,128)(2,1)S(1)} %collective-permute-done.21.refs_3_, ...), custom_call_target="tpu_custom_call" | custom-call | tf_op jit(solution)/shard_map/pallas_call | solution.py:258
  (44 shorter events, 6.1 us)
Async XLA Ops:
  0.0 2.8 %collective-permute-start.1 = (bf16[64,7168]{1,0:T(8,128)(2,1)}, bf16[64,7168]{1,0:T(8,128)(2,1)S(1)}, u32[]{:S(2)}, u32[]{:S(2)}) collective-permute-start(bf16[64,7168]{1,0:T(8,128)(2,1)} %refs_2_.1), channel_id=1, source_target_pairs={{0,2},{2,0},{4,6},{6,4},{8,10},{10,8},{12,14},{14,12},{16,18},{18,... | collective-permute-start | bytes 2752520 | tf_op jit(solution)/shard_map/tokens_1/ppermute | solution.py:20
  0.5 2.3 %collective-permute-start = (s32[8,64]{1,0:T(8,128)}, s32[8,64]{1,0:T(8,128)S(1)}, u32[]{:S(2)}, u32[]{:S(2)}) collective-permute-start(s32[8,64]{1,0:T(8,128)} %bitcast.14), channel_id=1, source_target_pairs={{0,2},{2,0},{4,6},{6,4},{8,10},{10,8},{12,14},{14,12},{16,18},{18,... | collective-permute-start | bytes 6152 | tf_op jit(solution)/shard_map/ids_1/ppermute | solution.py:20
  3.6 7.3 %collective-permute-start.2 = (bf16[8,7168]{1,0:T(8,128)(2,1)S(1)}, bf16[8,7168]{1,0:T(8,128)(2,1)S(1)}, u32[]{:S(2)}, u32[]{:S(2)}) collective-permute-start(bf16[8,7168]{1,0:T(8,128)(2,1)S(1)} %get-tuple-element.67), channel_id=1, source_target_pairs={{0,8},{2,10},{4,12},{6,14},{8,0},{10,2},{12,4},{14,6},{16,24},{18,... | collective-permute-start | bytes 344072 | tf_op jit(solution)/shard_map/go_stay_4/ppermute | solution.py:20
  6.6 4.9 %collective-permute-start.3 = (bf16[8,7168]{1,0:T(8,128)(2,1)S(1)}, bf16[8,7168]{1,0:T(8,128)(2,1)S(1)}, u32[]{:S(2)}, u32[]{:S(2)}) collective-permute-start(bf16[8,7168]{1,0:T(8,128)(2,1)S(1)} %get-tuple-element.66), channel_id=1, source_target_pairs={{0,4},{2,6},{4,0},{6,2},{8,12},{10,14},{12,8},{14,10},{16,20},{18,... | collective-permute-start | bytes 344072 | tf_op jit(solution)/shard_map/go_leave_2/ppermute | solution.py:20
  8.1 13.8 %collective-permute-start.4 = (bf16[8,7168]{1,0:T(8,128)(2,1)S(1)}, bf16[8,7168]{1,0:T(8,128)(2,1)S(1)}, u32[]{:S(2)}, u32[]{:S(2)}) collective-permute-start(bf16[8,7168]{1,0:T(8,128)(2,1)S(1)} %get-tuple-element.62), channel_id=1, source_target_pairs={{0,16},{2,18},{4,20},{6,22},{8,24},{10,26},{12,28},{14,30},{16,0},... | collective-permute-start | bytes 344072 | tf_op jit(solution)/shard_map/go_stay_8/ppermute | solution.py:20
  10.7 13.4 %collective-permute-start.5 = (bf16[8,7168]{1,0:T(8,128)(2,1)S(1)}, bf16[8,7168]{1,0:T(8,128)(2,1)S(1)}, u32[]{:S(2)}, u32[]{:S(2)}) collective-permute-start(bf16[8,7168]{1,0:T(8,128)(2,1)S(1)} %get-tuple-element.61), channel_id=1, source_target_pairs={{0,24},{2,26},{4,28},{6,30},{8,16},{10,18},{12,20},{14,22},{16,8},... | collective-permute-start | bytes 344072 | tf_op jit(solution)/shard_map/go_stay_12/ppermute | solution.py:20
  11.6 10.4 %collective-permute-start.6 = (bf16[24,7168]{1,0:T(8,128)(2,1)S(1)}, bf16[24,7168]{1,0:T(8,128)(2,1)S(1)}, u32[]{:S(2)}, u32[]{:S(2)}) collective-permute-start(bf16[24,7168]{1,0:T(8,128)(2,1)S(1)} %pad_maximum_fusion.2.refs_0_), channel_id=1, source_target_pairs={{0,1},{1,0},{2,3},{3,2},{4,5},{5,4},{6,7},{7,6},{8,9},{9,8},{10,11... | collective-permute-start | bytes 1032200 | tf_op jit(solution)/shard_map/blk_early_1/ppermute | solution.py:26
  13.1 20.4 %collective-permute-start.8 = (bf16[8,7168]{1,0:T(8,128)(2,1)S(1)}, bf16[8,7168]{1,0:T(8,128)(2,1)S(1)}, u32[]{:S(2)}, u32[]{:S(2)}) collective-permute-start(bf16[8,7168]{1,0:T(8,128)(2,1)S(1)} %get-tuple-element.45), channel_id=1, source_target_pairs={{0,28},{2,30},{4,24},{6,26},{8,20},{10,22},{12,16},{14,18},{16,12}... | collective-permute-start | bytes 344072 | tf_op jit(solution)/shard_map/go_leave_14/ppermute | solution.py:20
  21.9 11.6 %collective-permute-start.9 = (bf16[8,7168]{1,0:T(8,128)(2,1)S(1)}, bf16[8,7168]{1,0:T(8,128)(2,1)S(1)}, u32[]{:S(2)}, u32[]{:S(2)}) collective-permute-start(bf16[8,7168]{1,0:T(8,128)(2,1)S(1)} %get-tuple-element.46), channel_id=1, source_target_pairs={{0,20},{2,22},{4,16},{6,18},{8,28},{10,30},{12,24},{14,26},{16,4},... | collective-permute-start | bytes 344072 | tf_op jit(solution)/shard_map/go_leave_10/ppermute | solution.py:20
  24.1 13.1 %collective-permute-start.7 = (bf16[16,7168]{1,0:T(8,128)(2,1)S(1)}, bf16[16,7168]{1,0:T(8,128)(2,1)S(1)}, u32[]{:S(2)}, u32[]{:S(2)}) collective-permute-start(bf16[16,7168]{1,0:T(8,128)(2,1)S(1)} %constant_dynamic-update-slice_fusion.refs_1_), channel_id=1, source_target_pairs={{0,1},{1,0},{2,3},{3,2},{4,5},{5,4},{6,7},{7,6},{8,9},{9,8},{10,11... | collective-permute-start | bytes 688136 | tf_op jit(solution)/shard_map/blk_late_1/ppermute | solution.py:26
  31.0 5.8 %collective-permute-start.11 = (bf16[8,7168]{1,0:T(8,128)(2,1)S(1)}, bf16[8,7168]{1,0:T(8,128)(2,1)S(1)}, u32[]{:S(2)}, u32[]{:S(2)}) collective-permute-start(bf16[8,7168]{1,0:T(8,128)(2,1)S(1)} %get-tuple-element.50), channel_id=1, source_target_pairs={{0,12},{2,14},{4,8},{6,10},{8,4},{10,6},{12,0},{14,2},{16,28},{18,... | collective-permute-start | bytes 344072 | tf_op jit(solution)/shard_map/go_leave_6/ppermute | solution.py:20
  33.5 12.7 %collective-permute-start.13 = (bf16[16,7168]{1,0:T(8,128)(2,1)S(1)}, bf16[16,7168]{1,0:T(8,128)(2,1)S(1)}, u32[]{:S(2)}, u32[]{:S(2)}) collective-permute-start(bf16[16,7168]{1,0:T(8,128)(2,1)S(1)} %pad_maximum_fusion.3.refs_2_.refs_3_), channel_id=1, source_target_pairs={{0,1},{1,0},{2,3},{3,2},{4,5},{5,4},{6,7},{7,6},{8,9},{9,8},{10,11... | collective-permute-start | bytes 688136 | tf_op jit(solution)/shard_map/blk_most_1/ppermute | solution.py:26
  36.7 9.5 %collective-permute-start.12 = (bf16[8,7168]{1,0:T(8,128)(2,1)S(1)}, bf16[8,7168]{1,0:T(8,128)(2,1)S(1)}, u32[]{:S(2)}, u32[]{:S(2)}) collective-permute-start(bf16[8,7168]{1,0:T(8,128)(2,1)S(1)} %collective-permute-done.11.refs_1_), channel_id=1, source_target_pairs={{0,1},{1,0},{2,3},{3,2},{4,5},{5,4},{6,7},{7,6},{8,9},{9,8},{10,11... | collective-permute-start | bytes 344072 | tf_op jit(solution)/shard_map/blk_last_1/ppermute | solution.py:26
  44.7 7.4 %collective-permute-start.10 = (bf16[64,1024]{1,0:T(8,128)(2,1)S(1)}, bf16[64,1024]{1,0:T(8,128)(2,1)S(1)}, u32[]{:S(2)}, u32[]{:S(2)}) collective-permute-start(bf16[64,1024]{1,0:T(8,128)(2,1)S(1)} %get-tuple-element.53.refs_0_), channel_id=1, source_target_pairs={{0,1},{1,0},{2,3},{3,2},{4,5},{5,4},{6,7},{7,6},{8,9},{9,8},{10,11... | collective-permute-start | bytes 393224 | tf_op jit(solution)/shard_map/hidden_stay_1/ppermute | solution.py:26
  52.1 5.9 %collective-permute-start.14 = (bf16[64,1024]{1,0:T(8,128)(2,1)S(1)}, bf16[64,1024]{1,0:T(8,128)(2,1)S(1)}, u32[]{:S(2)}, u32[]{:S(2)}) collective-permute-start(bf16[64,1024]{1,0:T(8,128)(2,1)S(1)} %shard_map.68.refs_2_), channel_id=1, source_target_pairs={{0,1},{1,0},{2,3},{3,2},{4,5},{5,4},{6,7},{7,6},{8,9},{9,8},{10,11... | collective-permute-start | bytes 393224 | tf_op jit(solution)/shard_map/hidden_leave_1/ppermute | solution.py:26
  61.3 6.5 %collective-permute-start.18 = (bf16[32,3584]{1,0:T(8,128)(2,1)S(1)}, bf16[32,3584]{1,0:T(8,128)(2,1)S(1)}, u32[]{:S(2)}, u32[]{:S(2)}) collective-permute-start(bf16[32,3584]{1,0:T(8,128)(2,1)S(1)} %get-tuple-element.59), channel_id=1, source_target_pairs={{0,1},{1,0},{2,3},{3,2},{4,5},{5,4},{6,7},{7,6},{8,9},{9,8},{10,11... | collective-permute-start | bytes 688136 | tf_op jit(solution)/shard_map/own_leave_1/ppermute | solution.py:26
  62.9 5.6 %collective-permute-start.15 = (bf16[2,8,3584]{2,1,0:T(8,128)(2,1)S(1)}, bf16[2,8,3584]{2,1,0:T(8,128)(2,1)S(1)}, u32[]{:S(2)}, u32[]{:S(2)}) collective-permute-start(bf16[2,8,3584]{2,1,0:T(8,128)(2,1)S(1)} %get-tuple-element.78), channel_id=1, source_target_pairs={{0,8},{2,10},{4,12},{6,14},{8,0},{10,2},{12,4},{14,6},{16,24},{18,... | collective-permute-start | bytes 344072 | tf_op jit(solution)/shard_map/back_stay_4/ppermute | solution.py:20
  65.0 6.7 %collective-permute-start.16 = (bf16[2,8,3584]{2,1,0:T(8,128)(2,1)S(1)}, bf16[2,8,3584]{2,1,0:T(8,128)(2,1)S(1)}, u32[]{:S(2)}, u32[]{:S(2)}) collective-permute-start(bf16[2,8,3584]{2,1,0:T(8,128)(2,1)S(1)} %get-tuple-element.77), channel_id=1, source_target_pairs={{0,16},{2,18},{4,20},{6,22},{8,24},{10,26},{12,28},{14,30},{16,0},... | collective-permute-start | bytes 344072 | tf_op jit(solution)/shard_map/back_stay_8/ppermute | solution.py:20
  66.4 8.2 %collective-permute-start.17 = (bf16[2,8,3584]{2,1,0:T(8,128)(2,1)S(1)}, bf16[2,8,3584]{2,1,0:T(8,128)(2,1)S(1)}, u32[]{:S(2)}, u32[]{:S(2)}) collective-permute-start(bf16[2,8,3584]{2,1,0:T(8,128)(2,1)S(1)} %get-tuple-element.76), channel_id=1, source_target_pairs={{0,24},{2,26},{4,28},{6,30},{8,16},{10,18},{12,20},{14,22},{16,8},... | collective-permute-start | bytes 344072 | tf_op jit(solution)/shard_map/back_stay_12/ppermute | solution.py:20
  67.8 14.0 %collective-permute-start.19 = (bf16[2,8,3584]{2,1,0:T(8,128)(2,1)S(1)}, bf16[2,8,3584]{2,1,0:T(8,128)(2,1)S(1)}, u32[]{:S(2)}, u32[]{:S(2)}) collective-permute-start(bf16[2,8,3584]{2,1,0:T(8,128)(2,1)S(1)} %get-tuple-element.70), channel_id=1, source_target_pairs={{0,4},{2,6},{4,0},{6,2},{8,12},{10,14},{12,8},{14,10},{16,20},{18,... | collective-permute-start | bytes 344072 | tf_op jit(solution)/shard_map/back_leave_2/ppermute | solution.py:20
  74.7 7.9 %collective-permute-start.22 = (bf16[2,8,3584]{2,1,0:T(8,128)(2,1)S(1)}, bf16[2,8,3584]{2,1,0:T(8,128)(2,1)S(1)}, u32[]{:S(2)}, u32[]{:S(2)}) collective-permute-start(bf16[2,8,3584]{2,1,0:T(8,128)(2,1)S(1)} %get-tuple-element.71), channel_id=1, source_target_pairs={{0,12},{2,14},{4,8},{6,10},{8,4},{10,6},{12,0},{14,2},{16,28},{18,... | collective-permute-start | bytes 344072 | tf_op jit(solution)/shard_map/back_leave_6/ppermute | solution.py:20
  79.6 7.5 %collective-permute-start.23 = (bf16[2,8,3584]{2,1,0:T(8,128)(2,1)S(1)}, bf16[2,8,3584]{2,1,0:T(8,128)(2,1)S(1)}, u32[]{:S(2)}, u32[]{:S(2)}) collective-permute-start(bf16[2,8,3584]{2,1,0:T(8,128)(2,1)S(1)} %get-tuple-element.72), channel_id=1, source_target_pairs={{0,20},{2,22},{4,16},{6,18},{8,28},{10,30},{12,24},{14,26},{16,4},... | collective-permute-start | bytes 344072 | tf_op jit(solution)/shard_map/back_leave_10/ppermute | solution.py:20
  80.8 7.6 %collective-permute-start.24 = (bf16[2,8,3584]{2,1,0:T(8,128)(2,1)S(1)}, bf16[2,8,3584]{2,1,0:T(8,128)(2,1)S(1)}, u32[]{:S(2)}, u32[]{:S(2)}) collective-permute-start(bf16[2,8,3584]{2,1,0:T(8,128)(2,1)S(1)} %get-tuple-element.69), channel_id=1, source_target_pairs={{0,28},{2,30},{4,24},{6,26},{8,20},{10,22},{12,16},{14,18},{16,12}... | collective-permute-start | bytes 344072 | tf_op jit(solution)/shard_map/back_leave_14/ppermute | solution.py:20
  81.9 6.6 %collective-permute-start.20 = (bf16[32,3584]{1,0:T(8,128)(2,1)S(1)}, bf16[32,3584]{1,0:T(8,128)(2,1)S(1)}, u32[]{:S(2)}, u32[]{:S(2)}) collective-permute-start(bf16[32,3584]{1,0:T(8,128)(2,1)S(1)} %get-tuple-element.74), channel_id=1, source_target_pairs={{0,1},{1,0},{2,3},{3,2},{4,5},{5,4},{6,7},{7,6},{8,9},{9,8},{10,11... | collective-permute-start | bytes 688136 | tf_op jit(solution)/shard_map/own_stay_1/ppermute | solution.py:26
  88.4 1.9 %collective-permute-start.25 = (bf16[2,32,3584]{2,1,0:T(8,128)(2,1)S(1)}, bf16[2,32,3584]{2,1,0:T(8,128)(2,1)S(1)}, u32[]{:S(2)}, u32[]{:S(2)}) collective-permute-start(bf16[2,32,3584]{2,1,0:T(8,128)(2,1)S(1)} %constant_dynamic-update-slice_fusion.2.refs_4_), channel_id=1, source_target_pairs={{0,2},{2,0},{4,6},{6,4},{8,10},{10,8},{12,14},{14,12},{16,18},{18,... | collective-permute-start | bytes 1376264 | tf_op jit(solution)/shard_map/pair_leave_1/ppermute | solution.py:20
  88.6 2.4 %collective-permute-start.21 = (bf16[2,32,3584]{2,1,0:T(8,128)(2,1)S(1)}, bf16[2,32,3584]{2,1,0:T(8,128)(2,1)S(1)}, u32[]{:S(2)}, u32[]{:S(2)}) collective-permute-start(bf16[2,32,3584]{2,1,0:T(8,128)(2,1)S(1)} %pad_maximum_fusion.1.refs_2_), channel_id=1, source_target_pairs={{0,2},{2,0},{4,6},{6,4},{8,10},{10,8},{12,14},{14,12},{16,18},{18,... | collective-permute-start | bytes 1376264 | tf_op jit(solution)/shard_map/pair_stay_1/ppermute | solution.py:20

commit v2 on v1

--- a/solution.py
+++ b/solution.py
@@ -299,9 +299,10 @@
     late = jnp.concatenate(stay[2:], axis=0)
     early, leave[1:] = lax.optimization_barrier((early, leave[1:]))
     early_far, late_far = over_blk(early, "blk_early"), over_blk(late, "blk_late")
-    early_far, leave[2] = lax.optimization_barrier((early_far, leave[2]))
-    for z in range(levels - 1, 0, -1):
+    for z in [1, *range(levels - 1, 2, -1)]:
         leave[z] = exchanged(leave[z], z * 2 * ROW + ROW, "go_leave")
+    early_far, leave[1], leave[2] = lax.optimization_barrier((early_far, leave[1], leave[2]))
+    leave[2] = exchanged(leave[2], 2 * 2 * ROW + ROW, "go_leave")
     late, w_gate = lax.optimization_barrier((late, w_gate))
     w_gate, = loaded(w_gate)
     order = [*range(levels - 1, 1, -1)]
@@ -344,7 +345,6 @@
     stay = back(by_blk(stay), 0, "back_stay")
     leave = back(leave, ROW, "back_leave")
     stay = jnp.concatenate(stay, axis=1)
-    stay, leave[0] = lax.optimization_barrier((stay, leave[0]))
     stay = to_owners(stay, "own_stay")
     leave = jnp.concatenate(leave, axis=1)
     returned = [stay, exchanged(stay, CORE, "pair_stay"), leave, exchanged(leave, CORE, "pair_leave")]

time: 92.5 us -> 88.4 us (0.956)
  starting transfers between devices: 38.9 us -> 35.4 us
    ppermute x18, starting transfers between devices: 30.2 us -> 26.1 us  [exchanged(): return lax.ppermute(block, 'expert', [(i, i ^ mask) for i in range(size)])]
  transfers between devices with their start and end apart: 26 -> 26, of which waited for: 10 -> 9; matrix products, arithmetic and copies ran while one was open for 0% -> 0% of each run, Pallas kernels for 27% -> 28%
where the time goes in v2:
time: 88.4 us; the launch traced here: 88.2 us
  starting transfers between devices  35.4 us (40%)
  Pallas kernels  30.5 us (35%)
  waiting for transfers between devices  21.7 us (25%)
    ppermute x18, starting transfers between devices, exchanged(): return lax.ppermute(block, 'expert', [(i, i ^ mask) for i in range(size)])  26.1 us
    ppermute x18, waiting for transfers between devices, exchanged(): return lax.ppermute(block, 'expert', [(i, i ^ mask) for i in range(size)])  21.7 us
    pallas_call x2, Pallas kernels, hidden_units(): pl.pallas_call(functools.partial(first_hidden_kernel if first else hidden...  13.2 us
    pallas_call x3, Pallas kernels, loaded(): pl.pallas_call(functools.partial(load_kernel, count), in_specs=[pl.BlockS...  11.9 us
    ppermute x8, starting transfers between devices, shifted(): lax.ppermute(block, 'blk', [(i, (i + steps) % size) for i in range(size)])  9.35 us
    pallas_call x1, Pallas kernels, down_slices(): pl.pallas_call(functools.partial(down_kernel, half, len(groups)), in_spec...  3.24 us
  transfers between devices with their start and end apart: 26, of which 9 were waited for; matrix products, arithmetic and copies ran while one was open for 0% of the time, Pallas kernels for 28%

profile of v2, /device:TPU:0, one launch (start us, length us, event | category | flops | bytes accessed | tf_op | source)
XLA Modules:
  0.0 88.2 jit_solution(3099046123025147074)
XLA Ops:
  0.5 1.3 %shard_map.64 = (s32[8,64]{1,0:T(8,128)S(1)}, bf16[8,64]{1,0:T(8,128)(2,1)S(1)}, bf16[64,7168]{1,0:T(8,128)(2,1)S(1)}) custom-call(s32[8,64]{1,0:T(8,128)} %bitcast.15, bf16[8,64]{1,0:T(8,128)(2,1)} %bitcast.16, bf16[64,7168]{1,0:T(8,128)(2,1)} %refs_2_.1), custom_call_target="tpu_custom_call" | custom-call | bytes 920576 | tf_op jit(solution)/shard_map/pallas_call | solution.py:122
  1.8 0.9 %collective-permute-done.other_ids_ref = s32[8,64]{1,0:T(8,128)S(1)} collective-permute-done((s32[8,64]{1,0:T(8,128)}, s32[8,64]{1,0:T(8,128)S(1)}, u32[]{:S(2)}, u32[]{:S(2)}) %collective-permute-start) | collective-permute-done | bytes 2080 | tf_op jit(solution)/shard_map/ids_1/ppermute | solution.py:20
  3.6 3.0 %collective-permute-start.2 = (bf16[8,7168]{1,0:T(8,128)(2,1)S(1)}, bf16[8,7168]{1,0:T(8,128)(2,1)S(1)}, u32[]{:S(2)}, u32[]{:S(2)}) collective-permute-start(bf16[8,7168]{1,0:T(8,128)(2,1)S(1)} %get-tuple-element.65), channel_id=1, source_target_pairs={{0,8},{2,10},{4,12},{6,14},{8,0},{10,2},{12,4},{14,6},{16,24},{18,... | collective-permute-start | bytes 344072 | tf_op jit(solution)/shard_map/go_stay_4/ppermute | solution.py:20
  6.6 1.5 %collective-permute-start.3 = (bf16[8,7168]{1,0:T(8,128)(2,1)S(1)}, bf16[8,7168]{1,0:T(8,128)(2,1)S(1)}, u32[]{:S(2)}, u32[]{:S(2)}) collective-permute-start(bf16[8,7168]{1,0:T(8,128)(2,1)S(1)} %get-tuple-element.64), channel_id=1, source_target_pairs={{0,4},{2,6},{4,0},{6,2},{8,12},{10,14},{12,8},{14,10},{16,20},{18,... | collective-permute-start | bytes 344072 | tf_op jit(solution)/shard_map/go_leave_2/ppermute | solution.py:20
  8.1 2.6 %collective-permute-start.4 = (bf16[8,7168]{1,0:T(8,128)(2,1)S(1)}, bf16[8,7168]{1,0:T(8,128)(2,1)S(1)}, u32[]{:S(2)}, u32[]{:S(2)}) collective-permute-start(bf16[8,7168]{1,0:T(8,128)(2,1)S(1)} %get-tuple-element.60), channel_id=1, source_target_pairs={{0,16},{2,18},{4,20},{6,22},{8,24},{10,26},{12,28},{14,30},{16,0},... | collective-permute-start | bytes 344072 | tf_op jit(solution)/shard_map/go_stay_8/ppermute | solution.py:20
  11.6 1.6 %collective-permute-start.6 = (bf16[24,7168]{1,0:T(8,128)(2,1)S(1)}, bf16[24,7168]{1,0:T(8,128)(2,1)S(1)}, u32[]{:S(2)}, u32[]{:S(2)}) collective-permute-start(bf16[24,7168]{1,0:T(8,128)(2,1)S(1)} %pad_maximum_fusion.2.refs_0_), channel_id=1, source_target_pairs={{0,1},{1,0},{2,3},{3,2},{4,5},{5,4},{6,7},{7,6},{8,9},{9,8},{10,11... | collective-permute-start | bytes 1032200 | tf_op jit(solution)/shard_map/blk_early_1/ppermute | solution.py:26
  13.1 1.4 %collective-permute-start.7 = (bf16[8,7168]{1,0:T(8,128)(2,1)S(1)}, bf16[8,7168]{1,0:T(8,128)(2,1)S(1)}, u32[]{:S(2)}, u32[]{:S(2)}) collective-permute-start(bf16[8,7168]{1,0:T(8,128)(2,1)S(1)} %get-tuple-element.42), channel_id=1, source_target_pairs={{0,12},{2,14},{4,8},{6,10},{8,4},{10,6},{12,0},{14,2},{16,28},{18,... | collective-permute-start | bytes 344072 | tf_op jit(solution)/shard_map/go_leave_6/ppermute | solution.py:20
  14.5 3.5 %collective-permute-start.9 = (bf16[8,7168]{1,0:T(8,128)(2,1)S(1)}, bf16[8,7168]{1,0:T(8,128)(2,1)S(1)}, u32[]{:S(2)}, u32[]{:S(2)}) collective-permute-start(bf16[8,7168]{1,0:T(8,128)(2,1)S(1)} %get-tuple-element.45), channel_id=1, source_target_pairs={{0,28},{2,30},{4,24},{6,26},{8,20},{10,22},{12,16},{14,18},{16,12}... | collective-permute-start | bytes 344072 | tf_op jit(solution)/shard_map/go_leave_14/ppermute | solution.py:20
  18.1 2.7 %collective-permute-done.4 = bf16[8,7168]{1,0:T(8,128)(2,1)S(1)} collective-permute-done((bf16[8,7168]{1,0:T(8,128)(2,1)S(1)}, bf16[8,7168]{1,0:T(8,128)(2,1)S(1)}, u32[]{:S(2)}, u32[]{:S(2)}) %collective-permute-start.4) | collective-permute-done | bytes 114720 | tf_op jit(solution)/shard_map/go_stay_8/ppermute | solution.py:20
  20.7 2.6 %collective-permute-done.7.refs_1_ = bf16[8,7168]{1,0:T(8,128)(2,1)S(1)} collective-permute-done((bf16[8,7168]{1,0:T(8,128)(2,1)S(1)}, bf16[8,7168]{1,0:T(8,128)(2,1)S(1)}, u32[]{:S(2)}, u32[]{:S(2)}) %collective-permute-start.7) | collective-permute-done | bytes 114720 | tf_op jit(solution)/shard_map/go_leave_6/ppermute | solution.py:20
  23.3 0.8 collective-permute-start.10
  24.1 1.6 %collective-permute-start.8 = (bf16[16,7168]{1,0:T(8,128)(2,1)S(1)}, bf16[16,7168]{1,0:T(8,128)(2,1)S(1)}, u32[]{:S(2)}, u32[]{:S(2)}) collective-permute-start(bf16[16,7168]{1,0:T(8,128)(2,1)S(1)} %constant_dynamic-update-slice_fusion.refs_1_), channel_id=1, source_target_pairs={{0,1},{1,0},{2,3},{3,2},{4,5},{5,4},{6,7},{7,6},{8,9},{9,8},{10,11... | collective-permute-start | bytes 688136 | tf_op jit(solution)/shard_map/blk_late_1/ppermute | solution.py:26
  25.7 5.3 %shard_map.66.refs_4_.refs_8_ = bf16[1,7168,1024]{2,1,0:T(8,128)(2,1)S(1)} custom-call(bf16[1,7168,1024]{2,1,0:T(8,128)(2,1)} %refs_0_), custom_call_target="tpu_custom_call" | custom-call | bytes 14680064 | tf_op jit(solution)/shard_map/pallas_call | solution.py:122
  31.1 1.3 %collective-permute-start.13 = (bf16[16,7168]{1,0:T(8,128)(2,1)S(1)}, bf16[16,7168]{1,0:T(8,128)(2,1)S(1)}, u32[]{:S(2)}, u32[]{:S(2)}) collective-permute-start(bf16[16,7168]{1,0:T(8,128)(2,1)S(1)} %pad_maximum_fusion.3.refs_2_.refs_3_), channel_id=1, source_target_pairs={{0,1},{1,0},{2,3},{3,2},{4,5},{5,4},{6,7},{7,6},{8,9},{9,8},{10,11... | collective-permute-start | bytes 688136 | tf_op jit(solution)/shard_map/blk_most_1/ppermute | solution.py:26
  33.2 7.4 %shard_map.67 = (bf16[64,1024]{1,0:T(8,128)(2,1)S(1)}, bf16[1,7168,1024]{2,1,0:T(8,128)(2,1)S(1)}) custom-call(bf16[24,7168]{1,0:T(8,128)(2,1)S(1)} %pad_maximum_fusion.2.refs_0_, bf16[16,7168]{1,0:T(8,128)(2,1)S(1)} %constant_dynamic-update-slice_fusion.refs_1_, bf16[24,7168]{1,0:T(8,128)(2,1)S(1)} %collective-permute-done.6.refs_2_.refs_4_, ...), custom_call_target="tpu_custom_call" | custom-call | flops 1879048192 | bytes 1048576 | tf_op jit(solution)/shard_map/pallas_call | solution.py:187
  40.6 1.3 %collective-permute-start.11 = (bf16[64,1024]{1,0:T(8,128)(2,1)S(1)}, bf16[64,1024]{1,0:T(8,128)(2,1)S(1)}, u32[]{:S(2)}, u32[]{:S(2)}) collective-permute-start(bf16[64,1024]{1,0:T(8,128)(2,1)S(1)} %get-tuple-element.53.refs_0_), channel_id=1, source_target_pairs={{0,1},{1,0},{2,3},{3,2},{4,5},{5,4},{6,7},{7,6},{8,9},{9,8},{10,11... | collective-permute-start | bytes 393224 | tf_op jit(solution)/shard_map/hidden_stay_1/ppermute | solution.py:26
  41.9 5.8 %shard_map.68.refs_2_ = bf16[64,1024]{1,0:T(8,128)(2,1)S(1)} custom-call(bf16[24,7168]{1,0:T(8,128)(2,1)S(1)} %pad_maximum_fusion.2.refs_0_, bf16[8,7168]{1,0:T(8,128)(2,1)S(1)} %collective-permute-done.7.refs_1_, bf16[16,7168]{1,0:T(8,128)(2,1)S(1)} %pad_maximum_fusion.3.refs_2_.refs_3_, bf16[16,7168]{1,0:T(8,128)(2,1)S(1)} %pad_maximum_fusion.3.refs_2_.refs_3_, ...), custom_call_target="tpu_custom_call" | custom-call | flops 1879048192 | bytes 1048576 | tf_op jit(solution)/shard_map/pallas_call | solution.py:187
  47.8 0.8 collective-permute-start.14
  48.6 5.3 %shard_map.69.refs_4_ = bf16[1,2048,3584]{2,1,0:T(8,128)(2,1)S(1)} custom-call(bf16[1,2048,3584]{2,1,0:T(8,128)(2,1)} %refs_0_.1), custom_call_target="tpu_custom_call" | custom-call | bytes 14680064 | tf_op jit(solution)/shard_map/pallas_call | solution.py:122
  53.9 3.2 %shard_map.70 = bf16[128,3584]{1,0:T(8,128)(2,1)S(1)} custom-call(s32[1]{0:T(128)} %bitcast.place.refs_0_, bf16[64,1024]{1,0:T(8,128)(2,1)S(1)} %get-tuple-element.53.refs_0_, bf16[64,1024]{1,0:T(8,128)(2,1)S(1)} %collective-permute-done.11.refs_1_, bf16[64,1024]{1,0:T(8,128)(2,1)S(1)} %shard_map.68.refs_2_, ...), custom_call_target="tpu_custom_call" | custom-call | flops 1879048192 | bytes 1441792 | tf_op jit(solution)/shard_map/pallas_call | solution.py:226
  57.2 3.1 %collective-permute-start.15 = (bf16[2,8,3584]{2,1,0:T(8,128)(2,1)S(1)}, bf16[2,8,3584]{2,1,0:T(8,128)(2,1)S(1)}, u32[]{:S(2)}, u32[]{:S(2)}) collective-permute-start(bf16[2,8,3584]{2,1,0:T(8,128)(2,1)S(1)} %get-tuple-element.76), channel_id=1, source_target_pairs={{0,8},{2,10},{4,12},{6,14},{8,0},{10,2},{12,4},{14,6},{16,24},{18,... | collective-permute-start | bytes 344072 | tf_op jit(solution)/shard_map/back_stay_4/ppermute | solution.py:20
  60.7 2.1 %collective-permute-start.17 = (bf16[2,8,3584]{2,1,0:T(8,128)(2,1)S(1)}, bf16[2,8,3584]{2,1,0:T(8,128)(2,1)S(1)}, u32[]{:S(2)}, u32[]{:S(2)}) collective-permute-start(bf16[2,8,3584]{2,1,0:T(8,128)(2,1)S(1)} %get-tuple-element.74), channel_id=1, source_target_pairs={{0,24},{2,26},{4,28},{6,30},{8,16},{10,18},{12,20},{14,22},{16,8},... | collective-permute-start | bytes 344072 | tf_op jit(solution)/shard_map/back_stay_12/ppermute | solution.py:20
  62.8 0.9 %collective-permute-start.20 = (bf16[32,3584]{1,0:T(8,128)(2,1)S(1)}, bf16[32,3584]{1,0:T(8,128)(2,1)S(1)}, u32[]{:S(2)}, u32[]{:S(2)}) collective-permute-start(bf16[32,3584]{1,0:T(8,128)(2,1)S(1)} %get-tuple-element.57), channel_id=1, source_target_pairs={{0,1},{1,0},{2,3},{3,2},{4,5},{5,4},{6,7},{7,6},{8,9},{9,8},{10,11... | collective-permute-start | bytes 688136 | tf_op jit(solution)/shard_map/own_leave_1/ppermute | solution.py:26
  63.7 1.9 %collective-permute-done.15 = bf16[2,8,3584]{2,1,0:T(8,128)(2,1)S(1)} collective-permute-done((bf16[2,8,3584]{2,1,0:T(8,128)(2,1)S(1)}, bf16[2,8,3584]{2,1,0:T(8,128)(2,1)S(1)}, u32[]{:S(2)}, u32[]{:S(2)}) %collective-permute-start.15) | collective-permute-done | bytes 114720 | tf_op jit(solution)/shard_map/back_stay_4/ppermute | solution.py:20
  65.6 4.2 %collective-permute-done.16 = bf16[2,8,3584]{2,1,0:T(8,128)(2,1)S(1)} collective-permute-done((bf16[2,8,3584]{2,1,0:T(8,128)(2,1)S(1)}, bf16[2,8,3584]{2,1,0:T(8,128)(2,1)S(1)}, u32[]{:S(2)}, u32[]{:S(2)}) %collective-permute-start.16) | collective-permute-done | bytes 114720 | tf_op jit(solution)/shard_map/back_stay_8/ppermute | solution.py:20
  69.9 1.1 %collective-permute-start.18 = (bf16[32,3584]{1,0:T(8,128)(2,1)S(1)}, bf16[32,3584]{1,0:T(8,128)(2,1)S(1)}, u32[]{:S(2)}, u32[]{:S(2)}) collective-permute-start(bf16[32,3584]{1,0:T(8,128)(2,1)S(1)} %get-tuple-element.72), channel_id=1, source_target_pairs={{0,1},{1,0},{2,3},{3,2},{4,5},{5,4},{6,7},{7,6},{8,9},{9,8},{10,11... | collective-permute-start | bytes 688136 | tf_op jit(solution)/shard_map/own_stay_1/ppermute | solution.py:26
  71.4 3.0 %collective-permute-start.22 = (bf16[2,8,3584]{2,1,0:T(8,128)(2,1)S(1)}, bf16[2,8,3584]{2,1,0:T(8,128)(2,1)S(1)}, u32[]{:S(2)}, u32[]{:S(2)}) collective-permute-start(bf16[2,8,3584]{2,1,0:T(8,128)(2,1)S(1)} %get-tuple-element.69), channel_id=1, source_target_pairs={{0,12},{2,14},{4,8},{6,10},{8,4},{10,6},{12,0},{14,2},{16,28},{18,... | collective-permute-start | bytes 344072 | tf_op jit(solution)/shard_map/back_leave_6/ppermute | solution.py:20
  74.4 0.9 %collective-permute-start.23 = (bf16[2,8,3584]{2,1,0:T(8,128)(2,1)S(1)}, bf16[2,8,3584]{2,1,0:T(8,128)(2,1)S(1)}, u32[]{:S(2)}, u32[]{:S(2)}) collective-permute-start(bf16[2,8,3584]{2,1,0:T(8,128)(2,1)S(1)} %get-tuple-element.70), channel_id=1, source_target_pairs={{0,20},{2,22},{4,16},{6,18},{8,28},{10,30},{12,24},{14,26},{16,4},... | collective-permute-start | bytes 344072 | tf_op jit(solution)/shard_map/back_leave_10/ppermute | solution.py:20
  75.3 2.5 %collective-permute-start.24 = (bf16[2,8,3584]{2,1,0:T(8,128)(2,1)S(1)}, bf16[2,8,3584]{2,1,0:T(8,128)(2,1)S(1)}, u32[]{:S(2)}, u32[]{:S(2)}) collective-permute-start(bf16[2,8,3584]{2,1,0:T(8,128)(2,1)S(1)} %get-tuple-element.67), channel_id=1, source_target_pairs={{0,28},{2,30},{4,24},{6,26},{8,20},{10,22},{12,16},{14,18},{16,12}... | collective-permute-start | bytes 344072 | tf_op jit(solution)/shard_map/back_leave_14/ppermute | solution.py:20
  78.0 7.0 %collective-permute-done.23 = bf16[2,8,3584]{2,1,0:T(8,128)(2,1)S(1)} collective-permute-done((bf16[2,8,3584]{2,1,0:T(8,128)(2,1)S(1)}, bf16[2,8,3584]{2,1,0:T(8,128)(2,1)S(1)}, u32[]{:S(2)}, u32[]{:S(2)}) %collective-permute-start.23) | collective-permute-done | bytes 114720 | tf_op jit(solution)/shard_map/back_leave_10/ppermute | solution.py:20
  85.1 1.8 %collective-permute-done.25.refs_5_ = bf16[2,32,3584]{2,1,0:T(8,128)(2,1)S(1)} collective-permute-done((bf16[2,32,3584]{2,1,0:T(8,128)(2,1)S(1)}, bf16[2,32,3584]{2,1,0:T(8,128)(2,1)S(1)}, u32[]{:S(2)}, u32[]{:S(2)}) %collective-permute-start.25) | collective-permute-done | bytes 458784 | tf_op jit(solution)/shard_map/pair_leave_1/ppermute | solution.py:20
  86.9 1.4 %shard_map.71 = bf16[64,7168]{1,0:T(8,128)(2,1)} custom-call(s32[1]{0:T(128)} %bitcast.place.refs_0_, bf16[128,64]{1,0:T(8,128)(2,1)S(1)} %get-tuple-element.37.refs_1_, bf16[2,32,3584]{2,1,0:T(8,128)(2,1)S(1)} %pad_maximum_fusion.1.refs_2_, bf16[2,32,3584]{2,1,0:T(8,128)(2,1)S(1)} %collective-permute-done.19.refs_3_, ...), custom_call_target="tpu_custom_call" | custom-call | tf_op jit(solution)/shard_map/pallas_call | solution.py:258
  (44 shorter events, 4.3 us)
Async XLA Ops:
  0.0 2.8 %collective-permute-start.1 = (bf16[64,7168]{1,0:T(8,128)(2,1)}, bf16[64,7168]{1,0:T(8,128)(2,1)S(1)}, u32[]{:S(2)}, u32[]{:S(2)}) collective-permute-start(bf16[64,7168]{1,0:T(8,128)(2,1)} %refs_2_.1), channel_id=1, source_target_pairs={{0,2},{2,0},{4,6},{6,4},{8,10},{10,8},{12,14},{14,12},{16,18},{18,... | collective-permute-start | bytes 2752520 | tf_op jit(solution)/shard_map/tokens_1/ppermute | solution.py:20
  0.5 2.3 %collective-permute-start = (s32[8,64]{1,0:T(8,128)}, s32[8,64]{1,0:T(8,128)S(1)}, u32[]{:S(2)}, u32[]{:S(2)}) collective-permute-start(s32[8,64]{1,0:T(8,128)} %bitcast.14), channel_id=1, source_target_pairs={{0,2},{2,0},{4,6},{6,4},{8,10},{10,8},{12,14},{14,12},{16,18},{18,... | collective-permute-start | bytes 6152 | tf_op jit(solution)/shard_map/ids_1/ppermute | solution.py:20
  3.6 7.3 %collective-permute-start.2 = (bf16[8,7168]{1,0:T(8,128)(2,1)S(1)}, bf16[8,7168]{1,0:T(8,128)(2,1)S(1)}, u32[]{:S(2)}, u32[]{:S(2)}) collective-permute-start(bf16[8,7168]{1,0:T(8,128)(2,1)S(1)} %get-tuple-element.65), channel_id=1, source_target_pairs={{0,8},{2,10},{4,12},{6,14},{8,0},{10,2},{12,4},{14,6},{16,24},{18,... | collective-permute-start | bytes 344072 | tf_op jit(solution)/shard_map/go_stay_4/ppermute | solution.py:20
  6.6 4.9 %collective-permute-start.3 = (bf16[8,7168]{1,0:T(8,128)(2,1)S(1)}, bf16[8,7168]{1,0:T(8,128)(2,1)S(1)}, u32[]{:S(2)}, u32[]{:S(2)}) collective-permute-start(bf16[8,7168]{1,0:T(8,128)(2,1)S(1)} %get-tuple-element.64), channel_id=1, source_target_pairs={{0,4},{2,6},{4,0},{6,2},{8,12},{10,14},{12,8},{14,10},{16,20},{18,... | collective-permute-start | bytes 344072 | tf_op jit(solution)/shard_map/go_leave_2/ppermute | solution.py:20
  8.1 12.6 %collective-permute-start.4 = (bf16[8,7168]{1,0:T(8,128)(2,1)S(1)}, bf16[8,7168]{1,0:T(8,128)(2,1)S(1)}, u32[]{:S(2)}, u32[]{:S(2)}) collective-permute-start(bf16[8,7168]{1,0:T(8,128)(2,1)S(1)} %get-tuple-element.60), channel_id=1, source_target_pairs={{0,16},{2,18},{4,20},{6,22},{8,24},{10,26},{12,28},{14,30},{16,0},... | collective-permute-start | bytes 344072 | tf_op jit(solution)/shard_map/go_stay_8/ppermute | solution.py:20
  10.7 13.4 %collective-permute-start.5 = (bf16[8,7168]{1,0:T(8,128)(2,1)S(1)}, bf16[8,7168]{1,0:T(8,128)(2,1)S(1)}, u32[]{:S(2)}, u32[]{:S(2)}) collective-permute-start(bf16[8,7168]{1,0:T(8,128)(2,1)S(1)} %get-tuple-element.59), channel_id=1, source_target_pairs={{0,24},{2,26},{4,28},{6,30},{8,16},{10,18},{12,20},{14,22},{16,8},... | collective-permute-start | bytes 344072 | tf_op jit(solution)/shard_map/go_stay_12/ppermute | solution.py:20
  11.6 11.8 %collective-permute-start.6 = (bf16[24,7168]{1,0:T(8,128)(2,1)S(1)}, bf16[24,7168]{1,0:T(8,128)(2,1)S(1)}, u32[]{:S(2)}, u32[]{:S(2)}) collective-permute-start(bf16[24,7168]{1,0:T(8,128)(2,1)S(1)} %pad_maximum_fusion.2.refs_0_), channel_id=1, source_target_pairs={{0,1},{1,0},{2,3},{3,2},{4,5},{5,4},{6,7},{7,6},{8,9},{9,8},{10,11... | collective-permute-start | bytes 1032200 | tf_op jit(solution)/shard_map/blk_early_1/ppermute | solution.py:26
  13.1 10.2 %collective-permute-start.7 = (bf16[8,7168]{1,0:T(8,128)(2,1)S(1)}, bf16[8,7168]{1,0:T(8,128)(2,1)S(1)}, u32[]{:S(2)}, u32[]{:S(2)}) collective-permute-start(bf16[8,7168]{1,0:T(8,128)(2,1)S(1)} %get-tuple-element.42), channel_id=1, source_target_pairs={{0,12},{2,14},{4,8},{6,10},{8,4},{10,6},{12,0},{14,2},{16,28},{18,... | collective-permute-start | bytes 344072 | tf_op jit(solution)/shard_map/go_leave_6/ppermute | solution.py:20
  14.5 16.5 %collective-permute-start.9 = (bf16[8,7168]{1,0:T(8,128)(2,1)S(1)}, bf16[8,7168]{1,0:T(8,128)(2,1)S(1)}, u32[]{:S(2)}, u32[]{:S(2)}) collective-permute-start(bf16[8,7168]{1,0:T(8,128)(2,1)S(1)} %get-tuple-element.45), channel_id=1, source_target_pairs={{0,28},{2,30},{4,24},{6,26},{8,20},{10,22},{12,16},{14,18},{16,12}... | collective-permute-start | bytes 344072 | tf_op jit(solution)/shard_map/go_leave_14/ppermute | solution.py:20
  23.3 7.8 %collective-permute-start.10 = (bf16[8,7168]{1,0:T(8,128)(2,1)S(1)}, bf16[8,7168]{1,0:T(8,128)(2,1)S(1)}, u32[]{:S(2)}, u32[]{:S(2)}) collective-permute-start(bf16[8,7168]{1,0:T(8,128)(2,1)S(1)} %get-tuple-element.46), channel_id=1, source_target_pairs={{0,20},{2,22},{4,16},{6,18},{8,28},{10,30},{12,24},{14,26},{16,4},... | collective-permute-start | bytes 344072 | tf_op jit(solution)/shard_map/go_leave_10/ppermute | solution.py:20
  24.1 9.1 %collective-permute-start.8 = (bf16[16,7168]{1,0:T(8,128)(2,1)S(1)}, bf16[16,7168]{1,0:T(8,128)(2,1)S(1)}, u32[]{:S(2)}, u32[]{:S(2)}) collective-permute-start(bf16[16,7168]{1,0:T(8,128)(2,1)S(1)} %constant_dynamic-update-slice_fusion.refs_1_), channel_id=1, source_target_pairs={{0,1},{1,0},{2,3},{3,2},{4,5},{5,4},{6,7},{7,6},{8,9},{9,8},{10,11... | collective-permute-start | bytes 688136 | tf_op jit(solution)/shard_map/blk_late_1/ppermute | solution.py:26
  31.1 10.8 %collective-permute-start.13 = (bf16[16,7168]{1,0:T(8,128)(2,1)S(1)}, bf16[16,7168]{1,0:T(8,128)(2,1)S(1)}, u32[]{:S(2)}, u32[]{:S(2)}) collective-permute-start(bf16[16,7168]{1,0:T(8,128)(2,1)S(1)} %pad_maximum_fusion.3.refs_2_.refs_3_), channel_id=1, source_target_pairs={{0,1},{1,0},{2,3},{3,2},{4,5},{5,4},{6,7},{7,6},{8,9},{9,8},{10,11... | collective-permute-start | bytes 688136 | tf_op jit(solution)/shard_map/blk_most_1/ppermute | solution.py:26
  32.4 9.5 %collective-permute-start.12 = (bf16[8,7168]{1,0:T(8,128)(2,1)S(1)}, bf16[8,7168]{1,0:T(8,128)(2,1)S(1)}, u32[]{:S(2)}, u32[]{:S(2)}) collective-permute-start(bf16[8,7168]{1,0:T(8,128)(2,1)S(1)} %collective-permute-done.7.refs_1_), channel_id=1, source_target_pairs={{0,1},{1,0},{2,3},{3,2},{4,5},{5,4},{6,7},{7,6},{8,9},{9,8},{10,11... | collective-permute-start | bytes 344072 | tf_op jit(solution)/shard_map/blk_last_1/ppermute | solution.py:26
  40.6 7.2 %collective-permute-start.11 = (bf16[64,1024]{1,0:T(8,128)(2,1)S(1)}, bf16[64,1024]{1,0:T(8,128)(2,1)S(1)}, u32[]{:S(2)}, u32[]{:S(2)}) collective-permute-start(bf16[64,1024]{1,0:T(8,128)(2,1)S(1)} %get-tuple-element.53.refs_0_), channel_id=1, source_target_pairs={{0,1},{1,0},{2,3},{3,2},{4,5},{5,4},{6,7},{7,6},{8,9},{9,8},{10,11... | collective-permute-start | bytes 393224 | tf_op jit(solution)/shard_map/hidden_stay_1/ppermute | solution.py:26
  47.8 6.1 %collective-permute-start.14 = (bf16[64,1024]{1,0:T(8,128)(2,1)S(1)}, bf16[64,1024]{1,0:T(8,128)(2,1)S(1)}, u32[]{:S(2)}, u32[]{:S(2)}) collective-permute-start(bf16[64,1024]{1,0:T(8,128)(2,1)S(1)} %shard_map.68.refs_2_), channel_id=1, source_target_pairs={{0,1},{1,0},{2,3},{3,2},{4,5},{5,4},{6,7},{7,6},{8,9},{9,8},{10,11... | collective-permute-start | bytes 393224 | tf_op jit(solution)/shard_map/hidden_leave_1/ppermute | solution.py:26
  57.2 8.3 %collective-permute-start.15 = (bf16[2,8,3584]{2,1,0:T(8,128)(2,1)S(1)}, bf16[2,8,3584]{2,1,0:T(8,128)(2,1)S(1)}, u32[]{:S(2)}, u32[]{:S(2)}) collective-permute-start(bf16[2,8,3584]{2,1,0:T(8,128)(2,1)S(1)} %get-tuple-element.76), channel_id=1, source_target_pairs={{0,8},{2,10},{4,12},{6,14},{8,0},{10,2},{12,4},{14,6},{16,24},{18,... | collective-permute-start | bytes 344072 | tf_op jit(solution)/shard_map/back_stay_4/ppermute | solution.py:20
  60.3 9.4 %collective-permute-start.16 = (bf16[2,8,3584]{2,1,0:T(8,128)(2,1)S(1)}, bf16[2,8,3584]{2,1,0:T(8,128)(2,1)S(1)}, u32[]{:S(2)}, u32[]{:S(2)}) collective-permute-start(bf16[2,8,3584]{2,1,0:T(8,128)(2,1)S(1)} %get-tuple-element.75), channel_id=1, source_target_pairs={{0,16},{2,18},{4,20},{6,22},{8,24},{10,26},{12,28},{14,30},{16,0},... | collective-permute-start | bytes 344072 | tf_op jit(solution)/shard_map/back_stay_8/ppermute | solution.py:20
  60.7 9.1 %collective-permute-start.17 = (bf16[2,8,3584]{2,1,0:T(8,128)(2,1)S(1)}, bf16[2,8,3584]{2,1,0:T(8,128)(2,1)S(1)}, u32[]{:S(2)}, u32[]{:S(2)}) collective-permute-start(bf16[2,8,3584]{2,1,0:T(8,128)(2,1)S(1)} %get-tuple-element.74), channel_id=1, source_target_pairs={{0,24},{2,26},{4,28},{6,30},{8,16},{10,18},{12,20},{14,22},{16,8},... | collective-permute-start | bytes 344072 | tf_op jit(solution)/shard_map/back_stay_12/ppermute | solution.py:20
  62.8 8.1 %collective-permute-start.20 = (bf16[32,3584]{1,0:T(8,128)(2,1)S(1)}, bf16[32,3584]{1,0:T(8,128)(2,1)S(1)}, u32[]{:S(2)}, u32[]{:S(2)}) collective-permute-start(bf16[32,3584]{1,0:T(8,128)(2,1)S(1)} %get-tuple-element.57), channel_id=1, source_target_pairs={{0,1},{1,0},{2,3},{3,2},{4,5},{5,4},{6,7},{7,6},{8,9},{9,8},{10,11... | collective-permute-start | bytes 688136 | tf_op jit(solution)/shard_map/own_leave_1/ppermute | solution.py:26
  69.9 7.9 %collective-permute-start.18 = (bf16[32,3584]{1,0:T(8,128)(2,1)S(1)}, bf16[32,3584]{1,0:T(8,128)(2,1)S(1)}, u32[]{:S(2)}, u32[]{:S(2)}) collective-permute-start(bf16[32,3584]{1,0:T(8,128)(2,1)S(1)} %get-tuple-element.72), channel_id=1, source_target_pairs={{0,1},{1,0},{2,3},{3,2},{4,5},{5,4},{6,7},{7,6},{8,9},{9,8},{10,11... | collective-permute-start | bytes 688136 | tf_op jit(solution)/shard_map/own_stay_1/ppermute | solution.py:26
  71.0 6.9 %collective-permute-start.21 = (bf16[2,8,3584]{2,1,0:T(8,128)(2,1)S(1)}, bf16[2,8,3584]{2,1,0:T(8,128)(2,1)S(1)}, u32[]{:S(2)}, u32[]{:S(2)}) collective-permute-start(bf16[2,8,3584]{2,1,0:T(8,128)(2,1)S(1)} %get-tuple-element.68), channel_id=1, source_target_pairs={{0,4},{2,6},{4,0},{6,2},{8,12},{10,14},{12,8},{14,10},{16,20},{18,... | collective-permute-start | bytes 344072 | tf_op jit(solution)/shard_map/back_leave_2/ppermute | solution.py:20
  71.4 6.6 %collective-permute-start.22 = (bf16[2,8,3584]{2,1,0:T(8,128)(2,1)S(1)}, bf16[2,8,3584]{2,1,0:T(8,128)(2,1)S(1)}, u32[]{:S(2)}, u32[]{:S(2)}) collective-permute-start(bf16[2,8,3584]{2,1,0:T(8,128)(2,1)S(1)} %get-tuple-element.69), channel_id=1, source_target_pairs={{0,12},{2,14},{4,8},{6,10},{8,4},{10,6},{12,0},{14,2},{16,28},{18,... | collective-permute-start | bytes 344072 | tf_op jit(solution)/shard_map/back_leave_6/ppermute | solution.py:20
  74.4 10.5 %collective-permute-start.23 = (bf16[2,8,3584]{2,1,0:T(8,128)(2,1)S(1)}, bf16[2,8,3584]{2,1,0:T(8,128)(2,1)S(1)}, u32[]{:S(2)}, u32[]{:S(2)}) collective-permute-start(bf16[2,8,3584]{2,1,0:T(8,128)(2,1)S(1)} %get-tuple-element.70), channel_id=1, source_target_pairs={{0,20},{2,22},{4,16},{6,18},{8,28},{10,30},{12,24},{14,26},{16,4},... | collective-permute-start | bytes 344072 | tf_op jit(solution)/shard_map/back_leave_10/ppermute | solution.py:20
  75.3 9.6 %collective-permute-start.24 = (bf16[2,8,3584]{2,1,0:T(8,128)(2,1)S(1)}, bf16[2,8,3584]{2,1,0:T(8,128)(2,1)S(1)}, u32[]{:S(2)}, u32[]{:S(2)}) collective-permute-start(bf16[2,8,3584]{2,1,0:T(8,128)(2,1)S(1)} %get-tuple-element.67), channel_id=1, source_target_pairs={{0,28},{2,30},{4,24},{6,26},{8,20},{10,22},{12,16},{14,18},{16,12}... | collective-permute-start | bytes 344072 | tf_op jit(solution)/shard_map/back_leave_14/ppermute | solution.py:20
  77.8 7.2 %collective-permute-start.19 = (bf16[2,32,3584]{2,1,0:T(8,128)(2,1)S(1)}, bf16[2,32,3584]{2,1,0:T(8,128)(2,1)S(1)}, u32[]{:S(2)}, u32[]{:S(2)}) collective-permute-start(bf16[2,32,3584]{2,1,0:T(8,128)(2,1)S(1)} %pad_maximum_fusion.1.refs_2_), channel_id=1, source_target_pairs={{0,2},{2,0},{4,6},{6,4},{8,10},{10,8},{12,14},{14,12},{16,18},{18,... | collective-permute-start | bytes 1376264 | tf_op jit(solution)/shard_map/pair_stay_1/ppermute | solution.py:20
  85.0 1.9 %collective-permute-start.25 = (bf16[2,32,3584]{2,1,0:T(8,128)(2,1)S(1)}, bf16[2,32,3584]{2,1,0:T(8,128)(2,1)S(1)}, u32[]{:S(2)}, u32[]{:S(2)}) collective-permute-start(bf16[2,32,3584]{2,1,0:T(8,128)(2,1)S(1)} %constant_dynamic-update-slice_fusion.2.refs_4_), channel_id=1, source_target_pairs={{0,2},{2,0},{4,6},{6,4},{8,10},{10,8},{12,14},{14,12},{16,18},{18,... | collective-permute-start | bytes 1376264 | tf_op jit(solution)/shard_map/pair_leave_1/ppermute | solution.py:20

commit v3 on v2

--- a/solution.py
+++ b/solution.py
@@ -341,12 +341,16 @@
     def by_blk(output):
         return output.reshape(blocks, half, output.shape[1])
 
-    leave = to_owners(by_blk(leave), "own_leave")
-    stay = back(by_blk(stay), 0, "back_stay")
-    leave = back(leave, ROW, "back_leave")
+    stay = to_owners(by_blk(stay), "own_stay")
+    leave = back(by_blk(leave), ROW, "back_leave")
+    stay = [stay[:, z * unit:(z + 1) * unit] for z in range(levels)]
+    leave[0], stay[2] = lax.optimization_barrier((leave[0], stay[2]))
+    leave[1], stay[-1] = lax.optimization_barrier((leave[1], stay[-1]))
+    for z in range(levels - 1, 0, -1):
+        stay[z] = exchanged(stay[z], z * 2 * ROW, "back_stay")
+    leave = jnp.concatenate(leave, axis=1)
+    leave = to_owners(leave, "own_leave")
     stay = jnp.concatenate(stay, axis=1)
-    stay = to_owners(stay, "own_stay")
-    leave = jnp.concatenate(leave, axis=1)
     returned = [stay, exchanged(stay, CORE, "pair_stay"), leave, exchanged(leave, CORE, "pair_leave")]
     return mixed_rows(weighting, returned, place)
 

time: 88.4 us -> 88.1 us (level)
    ppermute x18, waiting for transfers between devices: 21.7 us -> 18.3 us  [exchanged(): return lax.ppermute(block, 'expert', [(i, i ^ mask) for i in range(size)])]
    ppermute x8, waiting for transfers between devices: 0.02 us -> 2.82 us  [shifted(): lax.ppermute(block, 'blk', [(i, (i + steps) % size) for i in range(size)])]
  transfers between devices with their start and end apart: 26 -> 26, of which waited for: 9 -> 10; matrix products, arithmetic and copies ran while one was open for 0% -> 0% of each run, Pallas kernels for 28% -> 29%
where the time goes in v3:
time: 88.1 us; the launch traced here: 87.7 us
  starting transfers between devices  35.6 us (40%)
  Pallas kernels  30.5 us (35%)
  waiting for transfers between devices  21.1 us (24%)
    ppermute x18, starting transfers between devices, exchanged(): return lax.ppermute(block, 'expert', [(i, i ^ mask) for i in range(size)])  26 us
    ppermute x18, waiting for transfers between devices, exchanged(): return lax.ppermute(block, 'expert', [(i, i ^ mask) for i in range(size)])  18.3 us
    pallas_call x2, Pallas kernels, hidden_units(): pl.pallas_call(functools.partial(first_hidden_kernel if first else hidden...  13.2 us
    pallas_call x3, Pallas kernels, loaded(): pl.pallas_call(functools.partial(load_kernel, count), in_specs=[pl.BlockS...  11.9 us
    ppermute x8, starting transfers between devices, shifted(): lax.ppermute(block, 'blk', [(i, (i + steps) % size) for i in range(size)])  9.6 us
    pallas_call x1, Pallas kernels, down_slices(): pl.pallas_call(functools.partial(down_kernel, half, len(groups)), in_spec...  3.24 us
    ppermute x8, waiting for transfers between devices, shifted(): lax.ppermute(block, 'blk', [(i, (i + steps) % size) for i in range(size)])  2.82 us
  transfers between devices with their start and end apart: 26, of which 10 were waited for; matrix products, arithmetic and copies ran while one was open for 0% of the time, Pallas kernels for 29%

profile of v3, /device:TPU:0, one launch (start us, length us, event | category | flops | bytes accessed | tf_op | source)
XLA Modules:
  0.0 87.7 jit_solution(6786107516289621323)
XLA Ops:
  0.5 1.3 %shard_map.64 = (s32[8,64]{1,0:T(8,128)S(1)}, bf16[8,64]{1,0:T(8,128)(2,1)S(1)}, bf16[64,7168]{1,0:T(8,128)(2,1)S(1)}) custom-call(s32[8,64]{1,0:T(8,128)} %bitcast.15, bf16[8,64]{1,0:T(8,128)(2,1)} %bitcast.16, bf16[64,7168]{1,0:T(8,128)(2,1)} %refs_2_.1), custom_call_target="tpu_custom_call" | custom-call | bytes 920576 | tf_op jit(solution)/shard_map/pallas_call | solution.py:122
  1.8 0.9 %collective-permute-done.other_ids_ref = s32[8,64]{1,0:T(8,128)S(1)} collective-permute-done((s32[8,64]{1,0:T(8,128)}, s32[8,64]{1,0:T(8,128)S(1)}, u32[]{:S(2)}, u32[]{:S(2)}) %collective-permute-start) | collective-permute-done | bytes 2080 | tf_op jit(solution)/shard_map/ids_1/ppermute | solution.py:20
  3.6 3.0 %collective-permute-start.2 = (bf16[8,7168]{1,0:T(8,128)(2,1)S(1)}, bf16[8,7168]{1,0:T(8,128)(2,1)S(1)}, u32[]{:S(2)}, u32[]{:S(2)}) collective-permute-start(bf16[8,7168]{1,0:T(8,128)(2,1)S(1)} %get-tuple-element.73), channel_id=1, source_target_pairs={{0,8},{2,10},{4,12},{6,14},{8,0},{10,2},{12,4},{14,6},{16,24},{18,... | collective-permute-start | bytes 344072 | tf_op jit(solution)/shard_map/go_stay_4/ppermute | solution.py:20
  6.6 1.5 %collective-permute-start.3 = (bf16[8,7168]{1,0:T(8,128)(2,1)S(1)}, bf16[8,7168]{1,0:T(8,128)(2,1)S(1)}, u32[]{:S(2)}, u32[]{:S(2)}) collective-permute-start(bf16[8,7168]{1,0:T(8,128)(2,1)S(1)} %get-tuple-element.72), channel_id=1, source_target_pairs={{0,4},{2,6},{4,0},{6,2},{8,12},{10,14},{12,8},{14,10},{16,20},{18,... | collective-permute-start | bytes 344072 | tf_op jit(solution)/shard_map/go_leave_2/ppermute | solution.py:20
  8.1 2.6 %collective-permute-start.4 = (bf16[8,7168]{1,0:T(8,128)(2,1)S(1)}, bf16[8,7168]{1,0:T(8,128)(2,1)S(1)}, u32[]{:S(2)}, u32[]{:S(2)}) collective-permute-start(bf16[8,7168]{1,0:T(8,128)(2,1)S(1)} %get-tuple-element.68), channel_id=1, source_target_pairs={{0,16},{2,18},{4,20},{6,22},{8,24},{10,26},{12,28},{14,30},{16,0},... | collective-permute-start | bytes 344072 | tf_op jit(solution)/shard_map/go_stay_8/ppermute | solution.py:20
  11.6 1.6 %collective-permute-start.6 = (bf16[24,7168]{1,0:T(8,128)(2,1)S(1)}, bf16[24,7168]{1,0:T(8,128)(2,1)S(1)}, u32[]{:S(2)}, u32[]{:S(2)}) collective-permute-start(bf16[24,7168]{1,0:T(8,128)(2,1)S(1)} %pad_maximum_fusion.2.refs_0_), channel_id=1, source_target_pairs={{0,1},{1,0},{2,3},{3,2},{4,5},{5,4},{6,7},{7,6},{8,9},{9,8},{10,11... | collective-permute-start | bytes 1032200 | tf_op jit(solution)/shard_map/blk_early_1/ppermute | solution.py:26
  13.1 1.4 %collective-permute-start.7 = (bf16[8,7168]{1,0:T(8,128)(2,1)S(1)}, bf16[8,7168]{1,0:T(8,128)(2,1)S(1)}, u32[]{:S(2)}, u32[]{:S(2)}) collective-permute-start(bf16[8,7168]{1,0:T(8,128)(2,1)S(1)} %get-tuple-element.46), channel_id=1, source_target_pairs={{0,12},{2,14},{4,8},{6,10},{8,4},{10,6},{12,0},{14,2},{16,28},{18,... | collective-permute-start | bytes 344072 | tf_op jit(solution)/shard_map/go_leave_6/ppermute | solution.py:20
  14.5 3.5 %collective-permute-start.9 = (bf16[8,7168]{1,0:T(8,128)(2,1)S(1)}, bf16[8,7168]{1,0:T(8,128)(2,1)S(1)}, u32[]{:S(2)}, u32[]{:S(2)}) collective-permute-start(bf16[8,7168]{1,0:T(8,128)(2,1)S(1)} %get-tuple-element.49), channel_id=1, source_target_pairs={{0,28},{2,30},{4,24},{6,26},{8,20},{10,22},{12,16},{14,18},{16,12}... | collective-permute-start | bytes 344072 | tf_op jit(solution)/shard_map/go_leave_14/ppermute | solution.py:20
  18.1 2.7 %collective-permute-done.4 = bf16[8,7168]{1,0:T(8,128)(2,1)S(1)} collective-permute-done((bf16[8,7168]{1,0:T(8,128)(2,1)S(1)}, bf16[8,7168]{1,0:T(8,128)(2,1)S(1)}, u32[]{:S(2)}, u32[]{:S(2)}) %collective-permute-start.4) | collective-permute-done | bytes 114720 | tf_op jit(solution)/shard_map/go_stay_8/ppermute | solution.py:20
  20.7 2.6 %collective-permute-done.7.refs_1_ = bf16[8,7168]{1,0:T(8,128)(2,1)S(1)} collective-permute-done((bf16[8,7168]{1,0:T(8,128)(2,1)S(1)}, bf16[8,7168]{1,0:T(8,128)(2,1)S(1)}, u32[]{:S(2)}, u32[]{:S(2)}) %collective-permute-start.7) | collective-permute-done | bytes 114720 | tf_op jit(solution)/shard_map/go_leave_6/ppermute | solution.py:20
  24.1 1.6 %collective-permute-start.8 = (bf16[16,7168]{1,0:T(8,128)(2,1)S(1)}, bf16[16,7168]{1,0:T(8,128)(2,1)S(1)}, u32[]{:S(2)}, u32[]{:S(2)}) collective-permute-start(bf16[16,7168]{1,0:T(8,128)(2,1)S(1)} %constant_dynamic-update-slice_fusion.refs_1_), channel_id=1, source_target_pairs={{0,1},{1,0},{2,3},{3,2},{4,5},{5,4},{6,7},{7,6},{8,9},{9,8},{10,11... | collective-permute-start | bytes 688136 | tf_op jit(solution)/shard_map/blk_late_1/ppermute | solution.py:26
  25.7 5.3 %shard_map.66.refs_4_.refs_8_ = bf16[1,7168,1024]{2,1,0:T(8,128)(2,1)S(1)} custom-call(bf16[1,7168,1024]{2,1,0:T(8,128)(2,1)} %refs_0_), custom_call_target="tpu_custom_call" | custom-call | bytes 14680064 | tf_op jit(solution)/shard_map/pallas_call | solution.py:122
  31.1 1.3 %collective-permute-start.13 = (bf16[16,7168]{1,0:T(8,128)(2,1)S(1)}, bf16[16,7168]{1,0:T(8,128)(2,1)S(1)}, u32[]{:S(2)}, u32[]{:S(2)}) collective-permute-start(bf16[16,7168]{1,0:T(8,128)(2,1)S(1)} %pad_maximum_fusion.3.refs_2_.refs_3_), channel_id=1, source_target_pairs={{0,1},{1,0},{2,3},{3,2},{4,5},{5,4},{6,7},{7,6},{8,9},{9,8},{10,11... | collective-permute-start | bytes 688136 | tf_op jit(solution)/shard_map/blk_most_1/ppermute | solution.py:26
  33.2 7.4 %shard_map.67 = (bf16[64,1024]{1,0:T(8,128)(2,1)S(1)}, bf16[1,7168,1024]{2,1,0:T(8,128)(2,1)S(1)}) custom-call(bf16[24,7168]{1,0:T(8,128)(2,1)S(1)} %pad_maximum_fusion.2.refs_0_, bf16[16,7168]{1,0:T(8,128)(2,1)S(1)} %constant_dynamic-update-slice_fusion.refs_1_, bf16[24,7168]{1,0:T(8,128)(2,1)S(1)} %collective-permute-done.6.refs_2_.refs_4_, ...), custom_call_target="tpu_custom_call" | custom-call | flops 1879048192 | bytes 1048576 | tf_op jit(solution)/shard_map/pallas_call | solution.py:187
  40.6 1.3 %collective-permute-start.11 = (bf16[64,1024]{1,0:T(8,128)(2,1)S(1)}, bf16[64,1024]{1,0:T(8,128)(2,1)S(1)}, u32[]{:S(2)}, u32[]{:S(2)}) collective-permute-start(bf16[64,1024]{1,0:T(8,128)(2,1)S(1)} %get-tuple-element.57.refs_0_), channel_id=1, source_target_pairs={{0,1},{1,0},{2,3},{3,2},{4,5},{5,4},{6,7},{7,6},{8,9},{9,8},{10,11... | collective-permute-start | bytes 393224 | tf_op jit(solution)/shard_map/hidden_stay_1/ppermute | solution.py:26
  41.9 5.8 %shard_map.68.refs_2_ = bf16[64,1024]{1,0:T(8,128)(2,1)S(1)} custom-call(bf16[24,7168]{1,0:T(8,128)(2,1)S(1)} %pad_maximum_fusion.2.refs_0_, bf16[8,7168]{1,0:T(8,128)(2,1)S(1)} %collective-permute-done.7.refs_1_, bf16[16,7168]{1,0:T(8,128)(2,1)S(1)} %pad_maximum_fusion.3.refs_2_.refs_3_, bf16[16,7168]{1,0:T(8,128)(2,1)S(1)} %pad_maximum_fusion.3.refs_2_.refs_3_, ...), custom_call_target="tpu_custom_call" | custom-call | flops 1879048192 | bytes 1048576 | tf_op jit(solution)/shard_map/pallas_call | solution.py:187
  48.6 5.3 %shard_map.69.refs_4_ = bf16[1,2048,3584]{2,1,0:T(8,128)(2,1)S(1)} custom-call(bf16[1,2048,3584]{2,1,0:T(8,128)(2,1)} %refs_0_.1), custom_call_target="tpu_custom_call" | custom-call | bytes 14680064 | tf_op jit(solution)/shard_map/pallas_call | solution.py:122
  53.9 3.2 %shard_map.70 = bf16[128,3584]{1,0:T(8,128)(2,1)S(1)} custom-call(s32[1]{0:T(128)} %bitcast.place.refs_0_, bf16[64,1024]{1,0:T(8,128)(2,1)S(1)} %get-tuple-element.57.refs_0_, bf16[64,1024]{1,0:T(8,128)(2,1)S(1)} %collective-permute-done.11.refs_1_, bf16[64,1024]{1,0:T(8,128)(2,1)S(1)} %shard_map.68.refs_2_, ...), custom_call_target="tpu_custom_call" | custom-call | flops 1879048192 | bytes 1441792 | tf_op jit(solution)/shard_map/pallas_call | solution.py:226
  57.2 1.3 %collective-permute-start.15 = (bf16[32,3584]{1,0:T(8,128)(2,1)S(1)}, bf16[32,3584]{1,0:T(8,128)(2,1)S(1)}, u32[]{:S(2)}, u32[]{:S(2)}) collective-permute-start(bf16[32,3584]{1,0:T(8,128)(2,1)S(1)} %get-tuple-element.66), channel_id=1, source_target_pairs={{0,1},{1,0},{2,3},{3,2},{4,5},{5,4},{6,7},{7,6},{8,9},{9,8},{10,11... | collective-permute-start | bytes 688136 | tf_op jit(solution)/shard_map/own_stay_1/ppermute | solution.py:26
  58.6 1.6 %collective-permute-start.17 = (bf16[2,8,3584]{2,1,0:T(8,128)(2,1)S(1)}, bf16[2,8,3584]{2,1,0:T(8,128)(2,1)S(1)}, u32[]{:S(2)}, u32[]{:S(2)}) collective-permute-start(bf16[2,8,3584]{2,1,0:T(8,128)(2,1)S(1)} %get-tuple-element.80), channel_id=1, source_target_pairs={{0,4},{2,6},{4,0},{6,2},{8,12},{10,14},{12,8},{14,10},{16,20},{18,... | collective-permute-start | bytes 344072 | tf_op jit(solution)/shard_map/back_leave_2/ppermute | solution.py:20
  60.2 2.5 %collective-permute-start.19 = (bf16[2,8,3584]{2,1,0:T(8,128)(2,1)S(1)}, bf16[2,8,3584]{2,1,0:T(8,128)(2,1)S(1)}, u32[]{:S(2)}, u32[]{:S(2)}) collective-permute-start(bf16[2,8,3584]{2,1,0:T(8,128)(2,1)S(1)} %get-tuple-element.79), channel_id=1, source_target_pairs={{0,12},{2,14},{4,8},{6,10},{8,4},{10,6},{12,0},{14,2},{16,28},{18,... | collective-permute-start | bytes 344072 | tf_op jit(solution)/shard_map/back_leave_6/ppermute | solution.py:20
  62.7 1.4 %collective-permute-start.22 = (bf16[2,8,3584]{2,1,0:T(8,128)(2,1)S(1)}, bf16[2,8,3584]{2,1,0:T(8,128)(2,1)S(1)}, u32[]{:S(2)}, u32[]{:S(2)}) collective-permute-start(bf16[2,8,3584]{2,1,0:T(8,128)(2,1)S(1)} %get-tuple-element.78), channel_id=1, source_target_pairs={{0,20},{2,22},{4,16},{6,18},{8,28},{10,30},{12,24},{14,26},{16,4},... | collective-permute-start | bytes 344072 | tf_op jit(solution)/shard_map/back_leave_10/ppermute | solution.py:20
  64.1 1.3 %collective-permute-start.23 = (bf16[2,8,3584]{2,1,0:T(8,128)(2,1)S(1)}, bf16[2,8,3584]{2,1,0:T(8,128)(2,1)S(1)}, u32[]{:S(2)}, u32[]{:S(2)}) collective-permute-start(bf16[2,8,3584]{2,1,0:T(8,128)(2,1)S(1)} %get-tuple-element.77), channel_id=1, source_target_pairs={{0,28},{2,30},{4,24},{6,26},{8,20},{10,22},{12,16},{14,18},{16,12}... | collective-permute-start | bytes 344072 | tf_op jit(solution)/shard_map/back_leave_14/ppermute | solution.py:20
  65.5 1.6 %collective-permute-done.19 = bf16[2,8,3584]{2,1,0:T(8,128)(2,1)S(1)} collective-permute-done((bf16[2,8,3584]{2,1,0:T(8,128)(2,1)S(1)}, bf16[2,8,3584]{2,1,0:T(8,128)(2,1)S(1)}, u32[]{:S(2)}, u32[]{:S(2)}) %collective-permute-start.19) | collective-permute-done | bytes 114720 | tf_op jit(solution)/shard_map/back_leave_6/ppermute | solution.py:20
  67.1 2.4 %collective-permute-start.18 = (bf16[2,8,3584]{2,1,0:T(8,128)(2,1)S(1)}, bf16[2,8,3584]{2,1,0:T(8,128)(2,1)S(1)}, u32[]{:S(2)}, u32[]{:S(2)}) collective-permute-start(bf16[2,8,3584]{2,1,0:T(8,128)(2,1)S(1)} %get-tuple-element.61), channel_id=1, source_target_pairs={{0,16},{2,18},{4,20},{6,22},{8,24},{10,26},{12,28},{14,30},{16,0},... | collective-permute-start | bytes 344072 | tf_op jit(solution)/shard_map/back_stay_8/ppermute | solution.py:20
  69.5 3.0 %collective-permute-start.20 = (bf16[2,8,3584]{2,1,0:T(8,128)(2,1)S(1)}, bf16[2,8,3584]{2,1,0:T(8,128)(2,1)S(1)}, u32[]{:S(2)}, u32[]{:S(2)}) collective-permute-start(bf16[2,8,3584]{2,1,0:T(8,128)(2,1)S(1)} %get-tuple-element.62), channel_id=1, source_target_pairs={{0,24},{2,26},{4,28},{6,30},{8,16},{10,18},{12,20},{14,22},{16,8},... | collective-permute-start | bytes 344072 | tf_op jit(solution)/shard_map/back_stay_12/ppermute | solution.py:20
  72.5 5.8 %collective-permute-done.22 = bf16[2,8,3584]{2,1,0:T(8,128)(2,1)S(1)} collective-permute-done((bf16[2,8,3584]{2,1,0:T(8,128)(2,1)S(1)}, bf16[2,8,3584]{2,1,0:T(8,128)(2,1)S(1)}, u32[]{:S(2)}, u32[]{:S(2)}) %collective-permute-start.22) | collective-permute-done | bytes 114720 | tf_op jit(solution)/shard_map/back_leave_10/ppermute | solution.py:20
  78.4 0.9 %collective-permute-start.24 = (bf16[32,3584]{1,0:T(8,128)(2,1)S(1)}, bf16[32,3584]{1,0:T(8,128)(2,1)S(1)}, u32[]{:S(2)}, u32[]{:S(2)}) collective-permute-start(bf16[32,3584]{1,0:T(8,128)(2,1)S(1)} %get-tuple-element.76), channel_id=1, source_target_pairs={{0,1},{1,0},{2,3},{3,2},{4,5},{5,4},{6,7},{7,6},{8,9},{9,8},{10,11... | collective-permute-start | bytes 688136 | tf_op jit(solution)/shard_map/own_leave_1/ppermute | solution.py:26
  79.3 2.3 %collective-permute-done.18 = bf16[2,8,3584]{2,1,0:T(8,128)(2,1)S(1)} collective-permute-done((bf16[2,8,3584]{2,1,0:T(8,128)(2,1)S(1)}, bf16[2,8,3584]{2,1,0:T(8,128)(2,1)S(1)}, u32[]{:S(2)}, u32[]{:S(2)}) %collective-permute-start.18) | collective-permute-done | bytes 114720 | tf_op jit(solution)/shard_map/back_stay_8/ppermute | solution.py:20
  81.7 2.8 %collective-permute-done.24 = bf16[32,3584]{1,0:T(8,128)(2,1)S(1)} collective-permute-done((bf16[32,3584]{1,0:T(8,128)(2,1)S(1)}, bf16[32,3584]{1,0:T(8,128)(2,1)S(1)}, u32[]{:S(2)}, u32[]{:S(2)}) %collective-permute-start.24) | collective-permute-done | bytes 229408 | tf_op jit(solution)/shard_map/own_leave_1/ppermute | solution.py:26
  84.6 1.8 %collective-permute-done.25.refs_5_ = bf16[2,32,3584]{2,1,0:T(8,128)(2,1)S(1)} collective-permute-done((bf16[2,32,3584]{2,1,0:T(8,128)(2,1)S(1)}, bf16[2,32,3584]{2,1,0:T(8,128)(2,1)S(1)}, u32[]{:S(2)}, u32[]{:S(2)}) %collective-permute-start.25) | collective-permute-done | bytes 458784 | tf_op jit(solution)/shard_map/pair_leave_1/ppermute | solution.py:20
  86.4 1.4 %shard_map.71 = bf16[64,7168]{1,0:T(8,128)(2,1)} custom-call(s32[1]{0:T(128)} %bitcast.place.refs_0_, bf16[128,64]{1,0:T(8,128)(2,1)S(1)} %get-tuple-element.41.refs_1_, bf16[2,32,3584]{2,1,0:T(8,128)(2,1)S(1)} %pad_maximum_fusion.refs_2_, bf16[2,32,3584]{2,1,0:T(8,128)(2,1)S(1)} %collective-permute-done.21.refs_3_, ...), custom_call_target="tpu_custom_call" | custom-call | tf_op jit(solution)/shard_map/pallas_call | solution.py:258
  (44 shorter events, 5.1 us)
Async XLA Ops:
  0.0 2.8 %collective-permute-start.1 = (bf16[64,7168]{1,0:T(8,128)(2,1)}, bf16[64,7168]{1,0:T(8,128)(2,1)S(1)}, u32[]{:S(2)}, u32[]{:S(2)}) collective-permute-start(bf16[64,7168]{1,0:T(8,128)(2,1)} %refs_2_.1), channel_id=1, source_target_pairs={{0,2},{2,0},{4,6},{6,4},{8,10},{10,8},{12,14},{14,12},{16,18},{18,... | collective-permute-start | bytes 2752520 | tf_op jit(solution)/shard_map/tokens_1/ppermute | solution.py:20
  0.5 2.3 %collective-permute-start = (s32[8,64]{1,0:T(8,128)}, s32[8,64]{1,0:T(8,128)S(1)}, u32[]{:S(2)}, u32[]{:S(2)}) collective-permute-start(s32[8,64]{1,0:T(8,128)} %bitcast.14), channel_id=1, source_target_pairs={{0,2},{2,0},{4,6},{6,4},{8,10},{10,8},{12,14},{14,12},{16,18},{18,... | collective-permute-start | bytes 6152 | tf_op jit(solution)/shard_map/ids_1/ppermute | solution.py:20
  3.6 7.3 %collective-permute-start.2 = (bf16[8,7168]{1,0:T(8,128)(2,1)S(1)}, bf16[8,7168]{1,0:T(8,128)(2,1)S(1)}, u32[]{:S(2)}, u32[]{:S(2)}) collective-permute-start(bf16[8,7168]{1,0:T(8,128)(2,1)S(1)} %get-tuple-element.73), channel_id=1, source_target_pairs={{0,8},{2,10},{4,12},{6,14},{8,0},{10,2},{12,4},{14,6},{16,24},{18,... | collective-permute-start | bytes 344072 | tf_op jit(solution)/shard_map/go_stay_4/ppermute | solution.py:20
  6.6 4.9 %collective-permute-start.3 = (bf16[8,7168]{1,0:T(8,128)(2,1)S(1)}, bf16[8,7168]{1,0:T(8,128)(2,1)S(1)}, u32[]{:S(2)}, u32[]{:S(2)}) collective-permute-start(bf16[8,7168]{1,0:T(8,128)(2,1)S(1)} %get-tuple-element.72), channel_id=1, source_target_pairs={{0,4},{2,6},{4,0},{6,2},{8,12},{10,14},{12,8},{14,10},{16,20},{18,... | collective-permute-start | bytes 344072 | tf_op jit(solution)/shard_map/go_leave_2/ppermute | solution.py:20
  8.1 12.6 %collective-permute-start.4 = (bf16[8,7168]{1,0:T(8,128)(2,1)S(1)}, bf16[8,7168]{1,0:T(8,128)(2,1)S(1)}, u32[]{:S(2)}, u32[]{:S(2)}) collective-permute-start(bf16[8,7168]{1,0:T(8,128)(2,1)S(1)} %get-tuple-element.68), channel_id=1, source_target_pairs={{0,16},{2,18},{4,20},{6,22},{8,24},{10,26},{12,28},{14,30},{16,0},... | collective-permute-start | bytes 344072 | tf_op jit(solution)/shard_map/go_stay_8/ppermute | solution.py:20
  10.7 13.4 %collective-permute-start.5 = (bf16[8,7168]{1,0:T(8,128)(2,1)S(1)}, bf16[8,7168]{1,0:T(8,128)(2,1)S(1)}, u32[]{:S(2)}, u32[]{:S(2)}) collective-permute-start(bf16[8,7168]{1,0:T(8,128)(2,1)S(1)} %get-tuple-element.67), channel_id=1, source_target_pairs={{0,24},{2,26},{4,28},{6,30},{8,16},{10,18},{12,20},{14,22},{16,8},... | collective-permute-start | bytes 344072 | tf_op jit(solution)/shard_map/go_stay_12/ppermute | solution.py:20
  11.6 11.8 %collective-permute-start.6 = (bf16[24,7168]{1,0:T(8,128)(2,1)S(1)}, bf16[24,7168]{1,0:T(8,128)(2,1)S(1)}, u32[]{:S(2)}, u32[]{:S(2)}) collective-permute-start(bf16[24,7168]{1,0:T(8,128)(2,1)S(1)} %pad_maximum_fusion.2.refs_0_), channel_id=1, source_target_pairs={{0,1},{1,0},{2,3},{3,2},{4,5},{5,4},{6,7},{7,6},{8,9},{9,8},{10,11... | collective-permute-start | bytes 1032200 | tf_op jit(solution)/shard_map/blk_early_1/ppermute | solution.py:26
  13.1 10.2 %collective-permute-start.7 = (bf16[8,7168]{1,0:T(8,128)(2,1)S(1)}, bf16[8,7168]{1,0:T(8,128)(2,1)S(1)}, u32[]{:S(2)}, u32[]{:S(2)}) collective-permute-start(bf16[8,7168]{1,0:T(8,128)(2,1)S(1)} %get-tuple-element.46), channel_id=1, source_target_pairs={{0,12},{2,14},{4,8},{6,10},{8,4},{10,6},{12,0},{14,2},{16,28},{18,... | collective-permute-start | bytes 344072 | tf_op jit(solution)/shard_map/go_leave_6/ppermute | solution.py:20
  14.5 16.5 %collective-permute-start.9 = (bf16[8,7168]{1,0:T(8,128)(2,1)S(1)}, bf16[8,7168]{1,0:T(8,128)(2,1)S(1)}, u32[]{:S(2)}, u32[]{:S(2)}) collective-permute-start(bf16[8,7168]{1,0:T(8,128)(2,1)S(1)} %get-tuple-element.49), channel_id=1, source_target_pairs={{0,28},{2,30},{4,24},{6,26},{8,20},{10,22},{12,16},{14,18},{16,12}... | collective-permute-start | bytes 344072 | tf_op jit(solution)/shard_map/go_leave_14/ppermute | solution.py:20
  23.3 7.8 %collective-permute-start.10 = (bf16[8,7168]{1,0:T(8,128)(2,1)S(1)}, bf16[8,7168]{1,0:T(8,128)(2,1)S(1)}, u32[]{:S(2)}, u32[]{:S(2)}) collective-permute-start(bf16[8,7168]{1,0:T(8,128)(2,1)S(1)} %get-tuple-element.50), channel_id=1, source_target_pairs={{0,20},{2,22},{4,16},{6,18},{8,28},{10,30},{12,24},{14,26},{16,4},... | collective-permute-start | bytes 344072 | tf_op jit(solution)/shard_map/go_leave_10/ppermute | solution.py:20
  24.1 9.1 %collective-permute-start.8 = (bf16[16,7168]{1,0:T(8,128)(2,1)S(1)}, bf16[16,7168]{1,0:T(8,128)(2,1)S(1)}, u32[]{:S(2)}, u32[]{:S(2)}) collective-permute-start(bf16[16,7168]{1,0:T(8,128)(2,1)S(1)} %constant_dynamic-update-slice_fusion.refs_1_), channel_id=1, source_target_pairs={{0,1},{1,0},{2,3},{3,2},{4,5},{5,4},{6,7},{7,6},{8,9},{9,8},{10,11... | collective-permute-start | bytes 688136 | tf_op jit(solution)/shard_map/blk_late_1/ppermute | solution.py:26
  31.1 10.8 %collective-permute-start.13 = (bf16[16,7168]{1,0:T(8,128)(2,1)S(1)}, bf16[16,7168]{1,0:T(8,128)(2,1)S(1)}, u32[]{:S(2)}, u32[]{:S(2)}) collective-permute-start(bf16[16,7168]{1,0:T(8,128)(2,1)S(1)} %pad_maximum_fusion.3.refs_2_.refs_3_), channel_id=1, source_target_pairs={{0,1},{1,0},{2,3},{3,2},{4,5},{5,4},{6,7},{7,6},{8,9},{9,8},{10,11... | collective-permute-start | bytes 688136 | tf_op jit(solution)/shard_map/blk_most_1/ppermute | solution.py:26
  32.4 9.5 %collective-permute-start.12 = (bf16[8,7168]{1,0:T(8,128)(2,1)S(1)}, bf16[8,7168]{1,0:T(8,128)(2,1)S(1)}, u32[]{:S(2)}, u32[]{:S(2)}) collective-permute-start(bf16[8,7168]{1,0:T(8,128)(2,1)S(1)} %collective-permute-done.7.refs_1_), channel_id=1, source_target_pairs={{0,1},{1,0},{2,3},{3,2},{4,5},{5,4},{6,7},{7,6},{8,9},{9,8},{10,11... | collective-permute-start | bytes 344072 | tf_op jit(solution)/shard_map/blk_last_1/ppermute | solution.py:26
  40.6 7.2 %collective-permute-start.11 = (bf16[64,1024]{1,0:T(8,128)(2,1)S(1)}, bf16[64,1024]{1,0:T(8,128)(2,1)S(1)}, u32[]{:S(2)}, u32[]{:S(2)}) collective-permute-start(bf16[64,1024]{1,0:T(8,128)(2,1)S(1)} %get-tuple-element.57.refs_0_), channel_id=1, source_target_pairs={{0,1},{1,0},{2,3},{3,2},{4,5},{5,4},{6,7},{7,6},{8,9},{9,8},{10,11... | collective-permute-start | bytes 393224 | tf_op jit(solution)/shard_map/hidden_stay_1/ppermute | solution.py:26
  47.8 6.1 %collective-permute-start.14 = (bf16[64,1024]{1,0:T(8,128)(2,1)S(1)}, bf16[64,1024]{1,0:T(8,128)(2,1)S(1)}, u32[]{:S(2)}, u32[]{:S(2)}) collective-permute-start(bf16[64,1024]{1,0:T(8,128)(2,1)S(1)} %shard_map.68.refs_2_), channel_id=1, source_target_pairs={{0,1},{1,0},{2,3},{3,2},{4,5},{5,4},{6,7},{7,6},{8,9},{9,8},{10,11... | collective-permute-start | bytes 393224 | tf_op jit(solution)/shard_map/hidden_leave_1/ppermute | solution.py:26
  57.2 8.2 %collective-permute-start.15 = (bf16[32,3584]{1,0:T(8,128)(2,1)S(1)}, bf16[32,3584]{1,0:T(8,128)(2,1)S(1)}, u32[]{:S(2)}, u32[]{:S(2)}) collective-permute-start(bf16[32,3584]{1,0:T(8,128)(2,1)S(1)} %get-tuple-element.66), channel_id=1, source_target_pairs={{0,1},{1,0},{2,3},{3,2},{4,5},{5,4},{6,7},{7,6},{8,9},{9,8},{10,11... | collective-permute-start | bytes 688136 | tf_op jit(solution)/shard_map/own_stay_1/ppermute | solution.py:26
  58.6 6.9 %collective-permute-start.17 = (bf16[2,8,3584]{2,1,0:T(8,128)(2,1)S(1)}, bf16[2,8,3584]{2,1,0:T(8,128)(2,1)S(1)}, u32[]{:S(2)}, u32[]{:S(2)}) collective-permute-start(bf16[2,8,3584]{2,1,0:T(8,128)(2,1)S(1)} %get-tuple-element.80), channel_id=1, source_target_pairs={{0,4},{2,6},{4,0},{6,2},{8,12},{10,14},{12,8},{14,10},{16,20},{18,... | collective-permute-start | bytes 344072 | tf_op jit(solution)/shard_map/back_leave_2/ppermute | solution.py:20
  60.2 6.9 %collective-permute-start.19 = (bf16[2,8,3584]{2,1,0:T(8,128)(2,1)S(1)}, bf16[2,8,3584]{2,1,0:T(8,128)(2,1)S(1)}, u32[]{:S(2)}, u32[]{:S(2)}) collective-permute-start(bf16[2,8,3584]{2,1,0:T(8,128)(2,1)S(1)} %get-tuple-element.79), channel_id=1, source_target_pairs={{0,12},{2,14},{4,8},{6,10},{8,4},{10,6},{12,0},{14,2},{16,28},{18,... | collective-permute-start | bytes 344072 | tf_op jit(solution)/shard_map/back_leave_6/ppermute | solution.py:20
  62.7 15.5 %collective-permute-start.22 = (bf16[2,8,3584]{2,1,0:T(8,128)(2,1)S(1)}, bf16[2,8,3584]{2,1,0:T(8,128)(2,1)S(1)}, u32[]{:S(2)}, u32[]{:S(2)}) collective-permute-start(bf16[2,8,3584]{2,1,0:T(8,128)(2,1)S(1)} %get-tuple-element.78), channel_id=1, source_target_pairs={{0,20},{2,22},{4,16},{6,18},{8,28},{10,30},{12,24},{14,26},{16,4},... | collective-permute-start | bytes 344072 | tf_op jit(solution)/shard_map/back_leave_10/ppermute | solution.py:20
  64.1 14.2 %collective-permute-start.23 = (bf16[2,8,3584]{2,1,0:T(8,128)(2,1)S(1)}, bf16[2,8,3584]{2,1,0:T(8,128)(2,1)S(1)}, u32[]{:S(2)}, u32[]{:S(2)}) collective-permute-start(bf16[2,8,3584]{2,1,0:T(8,128)(2,1)S(1)} %get-tuple-element.77), channel_id=1, source_target_pairs={{0,28},{2,30},{4,24},{6,26},{8,20},{10,22},{12,16},{14,18},{16,12}... | collective-permute-start | bytes 344072 | tf_op jit(solution)/shard_map/back_leave_14/ppermute | solution.py:20
  67.1 14.5 %collective-permute-start.18 = (bf16[2,8,3584]{2,1,0:T(8,128)(2,1)S(1)}, bf16[2,8,3584]{2,1,0:T(8,128)(2,1)S(1)}, u32[]{:S(2)}, u32[]{:S(2)}) collective-permute-start(bf16[2,8,3584]{2,1,0:T(8,128)(2,1)S(1)} %get-tuple-element.61), channel_id=1, source_target_pairs={{0,16},{2,18},{4,20},{6,22},{8,24},{10,26},{12,28},{14,30},{16,0},... | collective-permute-start | bytes 344072 | tf_op jit(solution)/shard_map/back_stay_8/ppermute | solution.py:20
  69.5 12.0 %collective-permute-start.20 = (bf16[2,8,3584]{2,1,0:T(8,128)(2,1)S(1)}, bf16[2,8,3584]{2,1,0:T(8,128)(2,1)S(1)}, u32[]{:S(2)}, u32[]{:S(2)}) collective-permute-start(bf16[2,8,3584]{2,1,0:T(8,128)(2,1)S(1)} %get-tuple-element.62), channel_id=1, source_target_pairs={{0,24},{2,26},{4,28},{6,30},{8,16},{10,18},{12,20},{14,22},{16,8},... | collective-permute-start | bytes 344072 | tf_op jit(solution)/shard_map/back_stay_12/ppermute | solution.py:20
  72.5 9.0 %collective-permute-start.16 = (bf16[2,8,3584]{2,1,0:T(8,128)(2,1)S(1)}, bf16[2,8,3584]{2,1,0:T(8,128)(2,1)S(1)}, u32[]{:S(2)}, u32[]{:S(2)}) collective-permute-start(bf16[2,8,3584]{2,1,0:T(8,128)(2,1)S(1)} %get-tuple-element.82), channel_id=1, source_target_pairs={{0,8},{2,10},{4,12},{6,14},{8,0},{10,2},{12,4},{14,6},{16,24},{18,... | collective-permute-start | bytes 344072 | tf_op jit(solution)/shard_map/back_stay_4/ppermute | solution.py:20
  78.4 6.1 %collective-permute-start.24 = (bf16[32,3584]{1,0:T(8,128)(2,1)S(1)}, bf16[32,3584]{1,0:T(8,128)(2,1)S(1)}, u32[]{:S(2)}, u32[]{:S(2)}) collective-permute-start(bf16[32,3584]{1,0:T(8,128)(2,1)S(1)} %get-tuple-element.76), channel_id=1, source_target_pairs={{0,1},{1,0},{2,3},{3,2},{4,5},{5,4},{6,7},{7,6},{8,9},{9,8},{10,11... | collective-permute-start | bytes 688136 | tf_op jit(solution)/shard_map/own_leave_1/ppermute | solution.py:26
  81.6 3.0 %collective-permute-start.21 = (bf16[2,32,3584]{2,1,0:T(8,128)(2,1)S(1)}, bf16[2,32,3584]{2,1,0:T(8,128)(2,1)S(1)}, u32[]{:S(2)}, u32[]{:S(2)}) collective-permute-start(bf16[2,32,3584]{2,1,0:T(8,128)(2,1)S(1)} %pad_maximum_fusion.refs_2_), channel_id=1, source_target_pairs={{0,2},{2,0},{4,6},{6,4},{8,10},{10,8},{12,14},{14,12},{16,18},{18,... | collective-permute-start | bytes 1376264 | tf_op jit(solution)/shard_map/pair_stay_1/ppermute | solution.py:20
  84.5 1.9 %collective-permute-start.25 = (bf16[2,32,3584]{2,1,0:T(8,128)(2,1)S(1)}, bf16[2,32,3584]{2,1,0:T(8,128)(2,1)S(1)}, u32[]{:S(2)}, u32[]{:S(2)}) collective-permute-start(bf16[2,32,3584]{2,1,0:T(8,128)(2,1)S(1)} %pad_maximum_fusion.1.refs_4_), channel_id=1, source_target_pairs={{0,2},{2,0},{4,6},{6,4},{8,10},{10,8},{12,14},{14,12},{16,18},{18,... | collective-permute-start | bytes 1376264 | tf_op jit(solution)/shard_map/pair_leave_1/ppermute | solution.py:20

commit v4 on v2

--- a/solution.py
+++ b/solution.py
@@ -341,12 +341,23 @@
     def by_blk(output):
         return output.reshape(blocks, half, output.shape[1])
 
-    leave = to_owners(by_blk(leave), "own_leave")
-    stay = back(by_blk(stay), 0, "back_stay")
-    leave = back(leave, ROW, "back_leave")
-    stay = jnp.concatenate(stay, axis=1)
-    stay = to_owners(stay, "own_stay")
-    leave = jnp.concatenate(leave, axis=1)
+    stay, leave = by_blk(stay), by_blk(leave)
+    rear = [leave[:, z * unit:(z + 1) * unit] for z in range(2, levels)]
+    for z in range(levels - 1, 1, -1):
+        rear[z - 2] = exchanged(rear[z - 2], z * 2 * ROW + ROW, "back_leave")
+    front = to_owners(jnp.concatenate([stay, leave[:, :2 * unit]], axis=1), "own_front")
+    front = [front[:, z * unit:(z + 1) * unit] for z in range(levels + 2)]
+    light = [front[1], front[levels], front[levels + 1]]
+    light, rear[-1] = lax.optimization_barrier((light, rear[-1]))
+    front[1], front[levels:] = light[0], light[1:]
+    for z in range(levels - 1, 0, -1):
+        front[z] = exchanged(front[z], z * 2 * ROW, "back_stay")
+    for z in range(2):
+        front[levels + z] = exchanged(front[levels + z], z * 2 * ROW + ROW, "back_leave")
+    rear, front[2] = lax.optimization_barrier((rear, front[2]))
+    rear = to_owners(jnp.concatenate(rear, axis=1), "own_rear")
+    stay = jnp.concatenate(front[:levels], axis=1)
+    leave = jnp.concatenate([*front[levels:], rear], axis=1)
     returned = [stay, exchanged(stay, CORE, "pair_stay"), leave, exchanged(leave, CORE, "pair_leave")]
     return mixed_rows(weighting, returned, place)
 

time: 88.4 us -> 86.5 us (0.979)
  waiting for transfers between devices: 21.7 us -> 16.2 us
  starting transfers between devices: 35.4 us -> 39.1 us
    ppermute x18, waiting for transfers between devices: 21.7 us -> 14.4 us  [exchanged(): return lax.ppermute(block, 'expert', [(i, i ^ mask) for i in range(size)])]
    ppermute x18, starting transfers between devices: 26.1 us -> 29.1 us  [exchanged(): return lax.ppermute(block, 'expert', [(i, i ^ mask) for i in range(size)])]
    ppermute x8, waiting for transfers between devices: 0.02 us -> 1.77 us  [shifted(): lax.ppermute(block, 'blk', [(i, (i + steps) % size) for i in range(size)])]
  transfers between devices with their start and end apart: 26 -> 26, of which waited for: 9 -> 13; matrix products, arithmetic and copies ran while one was open for 0% -> 0% of each run, Pallas kernels for 28% -> 29%
where the time goes in v4:
time: 86.5 us; the launch traced here: 86.3 us
  starting transfers between devices  39.1 us (45%)
  Pallas kernels  30.5 us (35%)
  waiting for transfers between devices  16.2 us (19%)
    ppermute x18, starting transfers between devices, exchanged(): return lax.ppermute(block, 'expert', [(i, i ^ mask) for i in range(size)])  29.1 us
    ppermute x18, waiting for transfers between devices, exchanged(): return lax.ppermute(block, 'expert', [(i, i ^ mask) for i in range(size)])  14.4 us
    pallas_call x2, Pallas kernels, hidden_units(): pl.pallas_call(functools.partial(first_hidden_kernel if first else hidden...  13.2 us
    pallas_call x3, Pallas kernels, loaded(): pl.pallas_call(functools.partial(load_kernel, count), in_specs=[pl.BlockS...  11.9 us
    ppermute x8, starting transfers between devices, shifted(): lax.ppermute(block, 'blk', [(i, (i + steps) % size) for i in range(size)])  9.94 us
    pallas_call x1, Pallas kernels, down_slices(): pl.pallas_call(functools.partial(down_kernel, half, len(groups)), in_spec...  3.24 us
    ppermute x8, waiting for transfers between devices, shifted(): lax.ppermute(block, 'blk', [(i, (i + steps) % size) for i in range(size)])  1.77 us
  transfers between devices with their start and end apart: 26, of which 13 were waited for; matrix products, arithmetic and copies ran while one was open for 0% of the time, Pallas kernels for 29%

profile of v4, /device:TPU:0, one launch (start us, length us, event | category | flops | bytes accessed | tf_op | source)
XLA Modules:
  0.0 86.3 jit_solution(5768390420867453743)
XLA Ops:
  0.5 1.3 %shard_map.64 = (s32[8,64]{1,0:T(8,128)S(1)}, bf16[8,64]{1,0:T(8,128)(2,1)S(1)}, bf16[64,7168]{1,0:T(8,128)(2,1)S(1)}) custom-call(s32[8,64]{1,0:T(8,128)} %bitcast.18, bf16[8,64]{1,0:T(8,128)(2,1)} %bitcast.19, bf16[64,7168]{1,0:T(8,128)(2,1)} %refs_2_.1), custom_call_target="tpu_custom_call" | custom-call | bytes 920576 | tf_op jit(solution)/shard_map/pallas_call | solution.py:122
  1.8 0.9 %collective-permute-done.other_ids_ref = s32[8,64]{1,0:T(8,128)S(1)} collective-permute-done((s32[8,64]{1,0:T(8,128)}, s32[8,64]{1,0:T(8,128)S(1)}, u32[]{:S(2)}, u32[]{:S(2)}) %collective-permute-start) | collective-permute-done | bytes 2080 | tf_op jit(solution)/shard_map/ids_1/ppermute | solution.py:20
  3.6 3.0 %collective-permute-start.2 = (bf16[8,7168]{1,0:T(8,128)(2,1)S(1)}, bf16[8,7168]{1,0:T(8,128)(2,1)S(1)}, u32[]{:S(2)}, u32[]{:S(2)}) collective-permute-start(bf16[8,7168]{1,0:T(8,128)(2,1)S(1)} %get-tuple-element.79), channel_id=1, source_target_pairs={{0,8},{2,10},{4,12},{6,14},{8,0},{10,2},{12,4},{14,6},{16,24},{18,... | collective-permute-start | bytes 344072 | tf_op jit(solution)/shard_map/go_stay_4/ppermute | solution.py:20
  6.6 1.5 %collective-permute-start.3 = (bf16[8,7168]{1,0:T(8,128)(2,1)S(1)}, bf16[8,7168]{1,0:T(8,128)(2,1)S(1)}, u32[]{:S(2)}, u32[]{:S(2)}) collective-permute-start(bf16[8,7168]{1,0:T(8,128)(2,1)S(1)} %get-tuple-element.78), channel_id=1, source_target_pairs={{0,4},{2,6},{4,0},{6,2},{8,12},{10,14},{12,8},{14,10},{16,20},{18,... | collective-permute-start | bytes 344072 | tf_op jit(solution)/shard_map/go_leave_2/ppermute | solution.py:20
  8.1 2.6 %collective-permute-start.4 = (bf16[8,7168]{1,0:T(8,128)(2,1)S(1)}, bf16[8,7168]{1,0:T(8,128)(2,1)S(1)}, u32[]{:S(2)}, u32[]{:S(2)}) collective-permute-start(bf16[8,7168]{1,0:T(8,128)(2,1)S(1)} %get-tuple-element.74), channel_id=1, source_target_pairs={{0,16},{2,18},{4,20},{6,22},{8,24},{10,26},{12,28},{14,30},{16,0},... | collective-permute-start | bytes 344072 | tf_op jit(solution)/shard_map/go_stay_8/ppermute | solution.py:20
  11.6 1.6 %collective-permute-start.6 = (bf16[24,7168]{1,0:T(8,128)(2,1)S(1)}, bf16[24,7168]{1,0:T(8,128)(2,1)S(1)}, u32[]{:S(2)}, u32[]{:S(2)}) collective-permute-start(bf16[24,7168]{1,0:T(8,128)(2,1)S(1)} %pad_maximum_fusion.2.refs_0_), channel_id=1, source_target_pairs={{0,1},{1,0},{2,3},{3,2},{4,5},{5,4},{6,7},{7,6},{8,9},{9,8},{10,11... | collective-permute-start | bytes 1032200 | tf_op jit(solution)/shard_map/blk_early_1/ppermute | solution.py:26
  13.1 1.4 %collective-permute-start.7 = (bf16[8,7168]{1,0:T(8,128)(2,1)S(1)}, bf16[8,7168]{1,0:T(8,128)(2,1)S(1)}, u32[]{:S(2)}, u32[]{:S(2)}) collective-permute-start(bf16[8,7168]{1,0:T(8,128)(2,1)S(1)} %get-tuple-element.49), channel_id=1, source_target_pairs={{0,12},{2,14},{4,8},{6,10},{8,4},{10,6},{12,0},{14,2},{16,28},{18,... | collective-permute-start | bytes 344072 | tf_op jit(solution)/shard_map/go_leave_6/ppermute | solution.py:20
  14.5 3.5 %collective-permute-start.9 = (bf16[8,7168]{1,0:T(8,128)(2,1)S(1)}, bf16[8,7168]{1,0:T(8,128)(2,1)S(1)}, u32[]{:S(2)}, u32[]{:S(2)}) collective-permute-start(bf16[8,7168]{1,0:T(8,128)(2,1)S(1)} %get-tuple-element.52), channel_id=1, source_target_pairs={{0,28},{2,30},{4,24},{6,26},{8,20},{10,22},{12,16},{14,18},{16,12}... | collective-permute-start | bytes 344072 | tf_op jit(solution)/shard_map/go_leave_14/ppermute | solution.py:20
  18.1 2.7 %collective-permute-done.4 = bf16[8,7168]{1,0:T(8,128)(2,1)S(1)} collective-permute-done((bf16[8,7168]{1,0:T(8,128)(2,1)S(1)}, bf16[8,7168]{1,0:T(8,128)(2,1)S(1)}, u32[]{:S(2)}, u32[]{:S(2)}) %collective-permute-start.4) | collective-permute-done | bytes 114720 | tf_op jit(solution)/shard_map/go_stay_8/ppermute | solution.py:20
  20.7 2.6 %collective-permute-done.7.refs_1_ = bf16[8,7168]{1,0:T(8,128)(2,1)S(1)} collective-permute-done((bf16[8,7168]{1,0:T(8,128)(2,1)S(1)}, bf16[8,7168]{1,0:T(8,128)(2,1)S(1)}, u32[]{:S(2)}, u32[]{:S(2)}) %collective-permute-start.7) | collective-permute-done | bytes 114720 | tf_op jit(solution)/shard_map/go_leave_6/ppermute | solution.py:20
  24.1 1.6 %collective-permute-start.8 = (bf16[16,7168]{1,0:T(8,128)(2,1)S(1)}, bf16[16,7168]{1,0:T(8,128)(2,1)S(1)}, u32[]{:S(2)}, u32[]{:S(2)}) collective-permute-start(bf16[16,7168]{1,0:T(8,128)(2,1)S(1)} %constant_dynamic-update-slice_fusion.refs_1_), channel_id=1, source_target_pairs={{0,1},{1,0},{2,3},{3,2},{4,5},{5,4},{6,7},{7,6},{8,9},{9,8},{10,11... | collective-permute-start | bytes 688136 | tf_op jit(solution)/shard_map/blk_late_1/ppermute | solution.py:26
  25.7 5.3 %shard_map.66.refs_4_.refs_8_ = bf16[1,7168,1024]{2,1,0:T(8,128)(2,1)S(1)} custom-call(bf16[1,7168,1024]{2,1,0:T(8,128)(2,1)} %refs_0_), custom_call_target="tpu_custom_call" | custom-call | bytes 14680064 | tf_op jit(solution)/shard_map/pallas_call | solution.py:122
  31.1 1.3 %collective-permute-start.13 = (bf16[16,7168]{1,0:T(8,128)(2,1)S(1)}, bf16[16,7168]{1,0:T(8,128)(2,1)S(1)}, u32[]{:S(2)}, u32[]{:S(2)}) collective-permute-start(bf16[16,7168]{1,0:T(8,128)(2,1)S(1)} %pad_maximum_fusion.3.refs_2_.refs_3_), channel_id=1, source_target_pairs={{0,1},{1,0},{2,3},{3,2},{4,5},{5,4},{6,7},{7,6},{8,9},{9,8},{10,11... | collective-permute-start | bytes 688136 | tf_op jit(solution)/shard_map/blk_most_1/ppermute | solution.py:26
  33.2 7.4 %shard_map.67 = (bf16[64,1024]{1,0:T(8,128)(2,1)S(1)}, bf16[1,7168,1024]{2,1,0:T(8,128)(2,1)S(1)}) custom-call(bf16[24,7168]{1,0:T(8,128)(2,1)S(1)} %pad_maximum_fusion.2.refs_0_, bf16[16,7168]{1,0:T(8,128)(2,1)S(1)} %constant_dynamic-update-slice_fusion.refs_1_, bf16[24,7168]{1,0:T(8,128)(2,1)S(1)} %collective-permute-done.6.refs_2_.refs_4_, ...), custom_call_target="tpu_custom_call" | custom-call | flops 1879048192 | bytes 1048576 | tf_op jit(solution)/shard_map/pallas_call | solution.py:187
  40.6 1.3 %collective-permute-start.11 = (bf16[64,1024]{1,0:T(8,128)(2,1)S(1)}, bf16[64,1024]{1,0:T(8,128)(2,1)S(1)}, u32[]{:S(2)}, u32[]{:S(2)}) collective-permute-start(bf16[64,1024]{1,0:T(8,128)(2,1)S(1)} %get-tuple-element.60.refs_0_), channel_id=1, source_target_pairs={{0,1},{1,0},{2,3},{3,2},{4,5},{5,4},{6,7},{7,6},{8,9},{9,8},{10,11... | collective-permute-start | bytes 393224 | tf_op jit(solution)/shard_map/hidden_stay_1/ppermute | solution.py:26
  41.9 5.8 %shard_map.68.refs_2_ = bf16[64,1024]{1,0:T(8,128)(2,1)S(1)} custom-call(bf16[24,7168]{1,0:T(8,128)(2,1)S(1)} %pad_maximum_fusion.2.refs_0_, bf16[8,7168]{1,0:T(8,128)(2,1)S(1)} %collective-permute-done.7.refs_1_, bf16[16,7168]{1,0:T(8,128)(2,1)S(1)} %pad_maximum_fusion.3.refs_2_.refs_3_, bf16[16,7168]{1,0:T(8,128)(2,1)S(1)} %pad_maximum_fusion.3.refs_2_.refs_3_, ...), custom_call_target="tpu_custom_call" | custom-call | flops 1879048192 | bytes 1048576 | tf_op jit(solution)/shard_map/pallas_call | solution.py:187
  48.6 5.3 %shard_map.69.refs_4_ = bf16[1,2048,3584]{2,1,0:T(8,128)(2,1)S(1)} custom-call(bf16[1,2048,3584]{2,1,0:T(8,128)(2,1)} %refs_0_.1), custom_call_target="tpu_custom_call" | custom-call | bytes 14680064 | tf_op jit(solution)/shard_map/pallas_call | solution.py:122
  53.9 3.2 %shard_map.70 = bf16[128,3584]{1,0:T(8,128)(2,1)S(1)} custom-call(s32[1]{0:T(128)} %bitcast.place.refs_0_, bf16[64,1024]{1,0:T(8,128)(2,1)S(1)} %get-tuple-element.60.refs_0_, bf16[64,1024]{1,0:T(8,128)(2,1)S(1)} %collective-permute-done.11.refs_1_, bf16[64,1024]{1,0:T(8,128)(2,1)S(1)} %shard_map.68.refs_2_, ...), custom_call_target="tpu_custom_call" | custom-call | flops 1879048192 | bytes 1441792 | tf_op jit(solution)/shard_map/pallas_call | solution.py:226
  57.3 1.3 %collective-permute-start.15 = (bf16[48,3584]{1,0:T(8,128)(2,1)S(1)}, bf16[48,3584]{1,0:T(8,128)(2,1)S(1)}, u32[]{:S(2)}, u32[]{:S(2)}) collective-permute-start(bf16[48,3584]{1,0:T(8,128)(2,1)S(1)} %get-tuple-element.88), channel_id=1, source_target_pairs={{0,1},{1,0},{2,3},{3,2},{4,5},{5,4},{6,7},{7,6},{8,9},{9,8},{10,11... | collective-permute-start | bytes 1032200 | tf_op jit(solution)/shard_map/own_front_1/ppermute | solution.py:26
  58.7 3.5 %collective-permute-start.16 = (bf16[2,8,3584]{2,1,0:T(8,128)(2,1)S(1)}, bf16[2,8,3584]{2,1,0:T(8,128)(2,1)S(1)}, u32[]{:S(2)}, u32[]{:S(2)}) collective-permute-start(bf16[2,8,3584]{2,1,0:T(8,128)(2,1)S(1)} %get-tuple-element.89), channel_id=1, source_target_pairs={{0,28},{2,30},{4,24},{6,26},{8,20},{10,22},{12,16},{14,18},{16,12}... | collective-permute-start | bytes 344072 | tf_op jit(solution)/shard_map/back_leave_14/ppermute | solution.py:20
  62.2 1.5 %collective-permute-start.18 = (bf16[2,8,3584]{2,1,0:T(8,128)(2,1)S(1)}, bf16[2,8,3584]{2,1,0:T(8,128)(2,1)S(1)}, u32[]{:S(2)}, u32[]{:S(2)}) collective-permute-start(bf16[2,8,3584]{2,1,0:T(8,128)(2,1)S(1)} %get-tuple-element.90), channel_id=1, source_target_pairs={{0,20},{2,22},{4,16},{6,18},{8,28},{10,30},{12,24},{14,26},{16,4},... | collective-permute-start | bytes 344072 | tf_op jit(solution)/shard_map/back_leave_10/ppermute | solution.py:20
  63.7 0.9 %collective-permute-done.15 = bf16[48,3584]{1,0:T(8,128)(2,1)S(1)} collective-permute-done((bf16[48,3584]{1,0:T(8,128)(2,1)S(1)}, bf16[48,3584]{1,0:T(8,128)(2,1)S(1)}, u32[]{:S(2)}, u32[]{:S(2)}) %collective-permute-start.15) | collective-permute-done | bytes 344096 | tf_op jit(solution)/shard_map/own_front_1/ppermute | solution.py:26
  64.7 3.4 %collective-permute-start.19 = (bf16[2,8,3584]{2,1,0:T(8,128)(2,1)S(1)}, bf16[2,8,3584]{2,1,0:T(8,128)(2,1)S(1)}, u32[]{:S(2)}, u32[]{:S(2)}) collective-permute-start(bf16[2,8,3584]{2,1,0:T(8,128)(2,1)S(1)} %get-tuple-element.86), channel_id=1, source_target_pairs={{0,16},{2,18},{4,20},{6,22},{8,24},{10,26},{12,28},{14,30},{16,0},... | collective-permute-start | bytes 344072 | tf_op jit(solution)/shard_map/back_stay_8/ppermute | solution.py:20
  68.1 5.3 %collective-permute-start.23 = (bf16[2,8,3584]{2,1,0:T(8,128)(2,1)S(1)}, bf16[2,8,3584]{2,1,0:T(8,128)(2,1)S(1)}, u32[]{:S(2)}, u32[]{:S(2)}) collective-permute-start(bf16[2,8,3584]{2,1,0:T(8,128)(2,1)S(1)} %get-tuple-element.68), channel_id=1, source_target_pairs={{0,12},{2,14},{4,8},{6,10},{8,4},{10,6},{12,0},{14,2},{16,28},{18,... | collective-permute-start | bytes 344072 | tf_op jit(solution)/shard_map/back_leave_6/ppermute | solution.py:20
  73.4 1.7 %collective-permute-done.18 = bf16[2,8,3584]{2,1,0:T(8,128)(2,1)S(1)} collective-permute-done((bf16[2,8,3584]{2,1,0:T(8,128)(2,1)S(1)}, bf16[2,8,3584]{2,1,0:T(8,128)(2,1)S(1)}, u32[]{:S(2)}, u32[]{:S(2)}) %collective-permute-start.18) | collective-permute-done | bytes 114720 | tf_op jit(solution)/shard_map/back_leave_10/ppermute | solution.py:20
  75.1 1.7 %collective-permute-start.20 = (bf16[2,8,3584]{2,1,0:T(8,128)(2,1)S(1)}, bf16[2,8,3584]{2,1,0:T(8,128)(2,1)S(1)}, u32[]{:S(2)}, u32[]{:S(2)}) collective-permute-start(bf16[2,8,3584]{2,1,0:T(8,128)(2,1)S(1)} %get-tuple-element.85), channel_id=1, source_target_pairs={{0,24},{2,26},{4,28},{6,30},{8,16},{10,18},{12,20},{14,22},{16,8},... | collective-permute-start | bytes 344072 | tf_op jit(solution)/shard_map/back_stay_12/ppermute | solution.py:20
  76.8 1.4 %collective-permute-done.19 = bf16[2,8,3584]{2,1,0:T(8,128)(2,1)S(1)} collective-permute-done((bf16[2,8,3584]{2,1,0:T(8,128)(2,1)S(1)}, bf16[2,8,3584]{2,1,0:T(8,128)(2,1)S(1)}, u32[]{:S(2)}, u32[]{:S(2)}) %collective-permute-start.19) | collective-permute-done | bytes 114720 | tf_op jit(solution)/shard_map/back_stay_8/ppermute | solution.py:20
  78.2 1.2 %collective-permute-start.24 = (bf16[16,3584]{1,0:T(8,128)(2,1)S(1)}, bf16[16,3584]{1,0:T(8,128)(2,1)S(1)}, u32[]{:S(2)}, u32[]{:S(2)}) collective-permute-start(bf16[16,3584]{1,0:T(8,128)(2,1)S(1)} %get-tuple-element.92), channel_id=1, source_target_pairs={{0,1},{1,0},{2,3},{3,2},{4,5},{5,4},{6,7},{7,6},{8,9},{9,8},{10,11... | collective-permute-start | bytes 344072 | tf_op jit(solution)/shard_map/own_rear_1/ppermute | solution.py:26
  80.0 2.1 %collective-permute-done.20 = bf16[2,8,3584]{2,1,0:T(8,128)(2,1)S(1)} collective-permute-done((bf16[2,8,3584]{2,1,0:T(8,128)(2,1)S(1)}, bf16[2,8,3584]{2,1,0:T(8,128)(2,1)S(1)}, u32[]{:S(2)}, u32[]{:S(2)}) %collective-permute-start.20) | collective-permute-done | bytes 114720 | tf_op jit(solution)/shard_map/back_stay_12/ppermute | solution.py:20
  83.2 0.9 collective-permute-done.21.refs_3_
  84.0 1.0 %collective-permute-done.25.refs_5_ = bf16[2,32,3584]{2,1,0:T(8,128)(2,1)S(1)} collective-permute-done((bf16[2,32,3584]{2,1,0:T(8,128)(2,1)S(1)}, bf16[2,32,3584]{2,1,0:T(8,128)(2,1)S(1)}, u32[]{:S(2)}, u32[]{:S(2)}) %collective-permute-start.25) | collective-permute-done | bytes 458784 | tf_op jit(solution)/shard_map/pair_leave_1/ppermute | solution.py:20
  85.0 1.4 %shard_map.71 = bf16[64,7168]{1,0:T(8,128)(2,1)} custom-call(s32[1]{0:T(128)} %bitcast.place.refs_0_, bf16[128,64]{1,0:T(8,128)(2,1)S(1)} %get-tuple-element.44.refs_1_, bf16[2,32,3584]{2,1,0:T(8,128)(2,1)S(1)} %pad_maximum_fusion.refs_2_, bf16[2,32,3584]{2,1,0:T(8,128)(2,1)S(1)} %collective-permute-done.21.refs_3_, ...), custom_call_target="tpu_custom_call" | custom-call | tf_op jit(solution)/shard_map/pallas_call | solution.py:258
  (43 shorter events, 6.5 us)
Async XLA Ops:
  0.0 2.8 %collective-permute-start.1 = (bf16[64,7168]{1,0:T(8,128)(2,1)}, bf16[64,7168]{1,0:T(8,128)(2,1)S(1)}, u32[]{:S(2)}, u32[]{:S(2)}) collective-permute-start(bf16[64,7168]{1,0:T(8,128)(2,1)} %refs_2_.1), channel_id=1, source_target_pairs={{0,2},{2,0},{4,6},{6,4},{8,10},{10,8},{12,14},{14,12},{16,18},{18,... | collective-permute-start | bytes 2752520 | tf_op jit(solution)/shard_map/tokens_1/ppermute | solution.py:20
  0.5 2.3 %collective-permute-start = (s32[8,64]{1,0:T(8,128)}, s32[8,64]{1,0:T(8,128)S(1)}, u32[]{:S(2)}, u32[]{:S(2)}) collective-permute-start(s32[8,64]{1,0:T(8,128)} %bitcast.17), channel_id=1, source_target_pairs={{0,2},{2,0},{4,6},{6,4},{8,10},{10,8},{12,14},{14,12},{16,18},{18,... | collective-permute-start | bytes 6152 | tf_op jit(solution)/shard_map/ids_1/ppermute | solution.py:20
  3.6 7.3 %collective-permute-start.2 = (bf16[8,7168]{1,0:T(8,128)(2,1)S(1)}, bf16[8,7168]{1,0:T(8,128)(2,1)S(1)}, u32[]{:S(2)}, u32[]{:S(2)}) collective-permute-start(bf16[8,7168]{1,0:T(8,128)(2,1)S(1)} %get-tuple-element.79), channel_id=1, source_target_pairs={{0,8},{2,10},{4,12},{6,14},{8,0},{10,2},{12,4},{14,6},{16,24},{18,... | collective-permute-start | bytes 344072 | tf_op jit(solution)/shard_map/go_stay_4/ppermute | solution.py:20
  6.6 4.9 %collective-permute-start.3 = (bf16[8,7168]{1,0:T(8,128)(2,1)S(1)}, bf16[8,7168]{1,0:T(8,128)(2,1)S(1)}, u32[]{:S(2)}, u32[]{:S(2)}) collective-permute-start(bf16[8,7168]{1,0:T(8,128)(2,1)S(1)} %get-tuple-element.78), channel_id=1, source_target_pairs={{0,4},{2,6},{4,0},{6,2},{8,12},{10,14},{12,8},{14,10},{16,20},{18,... | collective-permute-start | bytes 344072 | tf_op jit(solution)/shard_map/go_leave_2/ppermute | solution.py:20
  8.1 12.6 %collective-permute-start.4 = (bf16[8,7168]{1,0:T(8,128)(2,1)S(1)}, bf16[8,7168]{1,0:T(8,128)(2,1)S(1)}, u32[]{:S(2)}, u32[]{:S(2)}) collective-permute-start(bf16[8,7168]{1,0:T(8,128)(2,1)S(1)} %get-tuple-element.74), channel_id=1, source_target_pairs={{0,16},{2,18},{4,20},{6,22},{8,24},{10,26},{12,28},{14,30},{16,0},... | collective-permute-start | bytes 344072 | tf_op jit(solution)/shard_map/go_stay_8/ppermute | solution.py:20
  10.7 13.4 %collective-permute-start.5 = (bf16[8,7168]{1,0:T(8,128)(2,1)S(1)}, bf16[8,7168]{1,0:T(8,128)(2,1)S(1)}, u32[]{:S(2)}, u32[]{:S(2)}) collective-permute-start(bf16[8,7168]{1,0:T(8,128)(2,1)S(1)} %get-tuple-element.73), channel_id=1, source_target_pairs={{0,24},{2,26},{4,28},{6,30},{8,16},{10,18},{12,20},{14,22},{16,8},... | collective-permute-start | bytes 344072 | tf_op jit(solution)/shard_map/go_stay_12/ppermute | solution.py:20
  11.6 11.8 %collective-permute-start.6 = (bf16[24,7168]{1,0:T(8,128)(2,1)S(1)}, bf16[24,7168]{1,0:T(8,128)(2,1)S(1)}, u32[]{:S(2)}, u32[]{:S(2)}) collective-permute-start(bf16[24,7168]{1,0:T(8,128)(2,1)S(1)} %pad_maximum_fusion.2.refs_0_), channel_id=1, source_target_pairs={{0,1},{1,0},{2,3},{3,2},{4,5},{5,4},{6,7},{7,6},{8,9},{9,8},{10,11... | collective-permute-start | bytes 1032200 | tf_op jit(solution)/shard_map/blk_early_1/ppermute | solution.py:26
  13.1 10.2 %collective-permute-start.7 = (bf16[8,7168]{1,0:T(8,128)(2,1)S(1)}, bf16[8,7168]{1,0:T(8,128)(2,1)S(1)}, u32[]{:S(2)}, u32[]{:S(2)}) collective-permute-start(bf16[8,7168]{1,0:T(8,128)(2,1)S(1)} %get-tuple-element.49), channel_id=1, source_target_pairs={{0,12},{2,14},{4,8},{6,10},{8,4},{10,6},{12,0},{14,2},{16,28},{18,... | collective-permute-start | bytes 344072 | tf_op jit(solution)/shard_map/go_leave_6/ppermute | solution.py:20
  14.5 16.5 %collective-permute-start.9 = (bf16[8,7168]{1,0:T(8,128)(2,1)S(1)}, bf16[8,7168]{1,0:T(8,128)(2,1)S(1)}, u32[]{:S(2)}, u32[]{:S(2)}) collective-permute-start(bf16[8,7168]{1,0:T(8,128)(2,1)S(1)} %get-tuple-element.52), channel_id=1, source_target_pairs={{0,28},{2,30},{4,24},{6,26},{8,20},{10,22},{12,16},{14,18},{16,12}... | collective-permute-start | bytes 344072 | tf_op jit(solution)/shard_map/go_leave_14/ppermute | solution.py:20
  23.3 7.8 %collective-permute-start.10 = (bf16[8,7168]{1,0:T(8,128)(2,1)S(1)}, bf16[8,7168]{1,0:T(8,128)(2,1)S(1)}, u32[]{:S(2)}, u32[]{:S(2)}) collective-permute-start(bf16[8,7168]{1,0:T(8,128)(2,1)S(1)} %get-tuple-element.53), channel_id=1, source_target_pairs={{0,20},{2,22},{4,16},{6,18},{8,28},{10,30},{12,24},{14,26},{16,4},... | collective-permute-start | bytes 344072 | tf_op jit(solution)/shard_map/go_leave_10/ppermute | solution.py:20
  24.1 9.1 %collective-permute-start.8 = (bf16[16,7168]{1,0:T(8,128)(2,1)S(1)}, bf16[16,7168]{1,0:T(8,128)(2,1)S(1)}, u32[]{:S(2)}, u32[]{:S(2)}) collective-permute-start(bf16[16,7168]{1,0:T(8,128)(2,1)S(1)} %constant_dynamic-update-slice_fusion.refs_1_), channel_id=1, source_target_pairs={{0,1},{1,0},{2,3},{3,2},{4,5},{5,4},{6,7},{7,6},{8,9},{9,8},{10,11... | collective-permute-start | bytes 688136 | tf_op jit(solution)/shard_map/blk_late_1/ppermute | solution.py:26
  31.1 10.8 %collective-permute-start.13 = (bf16[16,7168]{1,0:T(8,128)(2,1)S(1)}, bf16[16,7168]{1,0:T(8,128)(2,1)S(1)}, u32[]{:S(2)}, u32[]{:S(2)}) collective-permute-start(bf16[16,7168]{1,0:T(8,128)(2,1)S(1)} %pad_maximum_fusion.3.refs_2_.refs_3_), channel_id=1, source_target_pairs={{0,1},{1,0},{2,3},{3,2},{4,5},{5,4},{6,7},{7,6},{8,9},{9,8},{10,11... | collective-permute-start | bytes 688136 | tf_op jit(solution)/shard_map/blk_most_1/ppermute | solution.py:26
  32.4 9.5 %collective-permute-start.12 = (bf16[8,7168]{1,0:T(8,128)(2,1)S(1)}, bf16[8,7168]{1,0:T(8,128)(2,1)S(1)}, u32[]{:S(2)}, u32[]{:S(2)}) collective-permute-start(bf16[8,7168]{1,0:T(8,128)(2,1)S(1)} %collective-permute-done.7.refs_1_), channel_id=1, source_target_pairs={{0,1},{1,0},{2,3},{3,2},{4,5},{5,4},{6,7},{7,6},{8,9},{9,8},{10,11... | collective-permute-start | bytes 344072 | tf_op jit(solution)/shard_map/blk_last_1/ppermute | solution.py:26
  40.6 7.2 %collective-permute-start.11 = (bf16[64,1024]{1,0:T(8,128)(2,1)S(1)}, bf16[64,1024]{1,0:T(8,128)(2,1)S(1)}, u32[]{:S(2)}, u32[]{:S(2)}) collective-permute-start(bf16[64,1024]{1,0:T(8,128)(2,1)S(1)} %get-tuple-element.60.refs_0_), channel_id=1, source_target_pairs={{0,1},{1,0},{2,3},{3,2},{4,5},{5,4},{6,7},{7,6},{8,9},{9,8},{10,11... | collective-permute-start | bytes 393224 | tf_op jit(solution)/shard_map/hidden_stay_1/ppermute | solution.py:26
  47.8 6.1 %collective-permute-start.14 = (bf16[64,1024]{1,0:T(8,128)(2,1)S(1)}, bf16[64,1024]{1,0:T(8,128)(2,1)S(1)}, u32[]{:S(2)}, u32[]{:S(2)}) collective-permute-start(bf16[64,1024]{1,0:T(8,128)(2,1)S(1)} %shard_map.68.refs_2_), channel_id=1, source_target_pairs={{0,1},{1,0},{2,3},{3,2},{4,5},{5,4},{6,7},{7,6},{8,9},{9,8},{10,11... | collective-permute-start | bytes 393224 | tf_op jit(solution)/shard_map/hidden_leave_1/ppermute | solution.py:26
  57.3 7.3 %collective-permute-start.15 = (bf16[48,3584]{1,0:T(8,128)(2,1)S(1)}, bf16[48,3584]{1,0:T(8,128)(2,1)S(1)}, u32[]{:S(2)}, u32[]{:S(2)}) collective-permute-start(bf16[48,3584]{1,0:T(8,128)(2,1)S(1)} %get-tuple-element.88), channel_id=1, source_target_pairs={{0,1},{1,0},{2,3},{3,2},{4,5},{5,4},{6,7},{7,6},{8,9},{9,8},{10,11... | collective-permute-start | bytes 1032200 | tf_op jit(solution)/shard_map/own_front_1/ppermute | solution.py:26
  58.7 9.4 %collective-permute-start.16 = (bf16[2,8,3584]{2,1,0:T(8,128)(2,1)S(1)}, bf16[2,8,3584]{2,1,0:T(8,128)(2,1)S(1)}, u32[]{:S(2)}, u32[]{:S(2)}) collective-permute-start(bf16[2,8,3584]{2,1,0:T(8,128)(2,1)S(1)} %get-tuple-element.89), channel_id=1, source_target_pairs={{0,28},{2,30},{4,24},{6,26},{8,20},{10,22},{12,16},{14,18},{16,12}... | collective-permute-start | bytes 344072 | tf_op jit(solution)/shard_map/back_leave_14/ppermute | solution.py:20
  62.2 12.9 %collective-permute-start.18 = (bf16[2,8,3584]{2,1,0:T(8,128)(2,1)S(1)}, bf16[2,8,3584]{2,1,0:T(8,128)(2,1)S(1)}, u32[]{:S(2)}, u32[]{:S(2)}) collective-permute-start(bf16[2,8,3584]{2,1,0:T(8,128)(2,1)S(1)} %get-tuple-element.90), channel_id=1, source_target_pairs={{0,20},{2,22},{4,16},{6,18},{8,28},{10,30},{12,24},{14,26},{16,4},... | collective-permute-start | bytes 344072 | tf_op jit(solution)/shard_map/back_leave_10/ppermute | solution.py:20
  64.7 13.5 %collective-permute-start.19 = (bf16[2,8,3584]{2,1,0:T(8,128)(2,1)S(1)}, bf16[2,8,3584]{2,1,0:T(8,128)(2,1)S(1)}, u32[]{:S(2)}, u32[]{:S(2)}) collective-permute-start(bf16[2,8,3584]{2,1,0:T(8,128)(2,1)S(1)} %get-tuple-element.86), channel_id=1, source_target_pairs={{0,16},{2,18},{4,20},{6,22},{8,24},{10,26},{12,28},{14,30},{16,0},... | collective-permute-start | bytes 344072 | tf_op jit(solution)/shard_map/back_stay_8/ppermute | solution.py:20
  68.1 14.2 %collective-permute-start.22 = (bf16[2,8,3584]{2,1,0:T(8,128)(2,1)S(1)}, bf16[2,8,3584]{2,1,0:T(8,128)(2,1)S(1)}, u32[]{:S(2)}, u32[]{:S(2)}) collective-permute-start(bf16[2,8,3584]{2,1,0:T(8,128)(2,1)S(1)} %get-tuple-element.67), channel_id=1, source_target_pairs={{0,4},{2,6},{4,0},{6,2},{8,12},{10,14},{12,8},{14,10},{16,20},{18,... | collective-permute-start | bytes 344072 | tf_op jit(solution)/shard_map/back_leave_2/ppermute | solution.py:20
  68.1 14.2 %collective-permute-start.23 = (bf16[2,8,3584]{2,1,0:T(8,128)(2,1)S(1)}, bf16[2,8,3584]{2,1,0:T(8,128)(2,1)S(1)}, u32[]{:S(2)}, u32[]{:S(2)}) collective-permute-start(bf16[2,8,3584]{2,1,0:T(8,128)(2,1)S(1)} %get-tuple-element.68), channel_id=1, source_target_pairs={{0,12},{2,14},{4,8},{6,10},{8,4},{10,6},{12,0},{14,2},{16,28},{18,... | collective-permute-start | bytes 344072 | tf_op jit(solution)/shard_map/back_leave_6/ppermute | solution.py:20
  73.4 6.7 %collective-permute-start.17 = (bf16[2,8,3584]{2,1,0:T(8,128)(2,1)S(1)}, bf16[2,8,3584]{2,1,0:T(8,128)(2,1)S(1)}, u32[]{:S(2)}, u32[]{:S(2)}) collective-permute-start(bf16[2,8,3584]{2,1,0:T(8,128)(2,1)S(1)} %get-tuple-element.64), channel_id=1, source_target_pairs={{0,8},{2,10},{4,12},{6,14},{8,0},{10,2},{12,4},{14,6},{16,24},{18,... | collective-permute-start | bytes 344072 | tf_op jit(solution)/shard_map/back_stay_4/ppermute | solution.py:20
  75.1 7.0 %collective-permute-start.20 = (bf16[2,8,3584]{2,1,0:T(8,128)(2,1)S(1)}, bf16[2,8,3584]{2,1,0:T(8,128)(2,1)S(1)}, u32[]{:S(2)}, u32[]{:S(2)}) collective-permute-start(bf16[2,8,3584]{2,1,0:T(8,128)(2,1)S(1)} %get-tuple-element.85), channel_id=1, source_target_pairs={{0,24},{2,26},{4,28},{6,30},{8,16},{10,18},{12,20},{14,22},{16,8},... | collective-permute-start | bytes 344072 | tf_op jit(solution)/shard_map/back_stay_12/ppermute | solution.py:20
  78.2 4.9 %collective-permute-start.24 = (bf16[16,3584]{1,0:T(8,128)(2,1)S(1)}, bf16[16,3584]{1,0:T(8,128)(2,1)S(1)}, u32[]{:S(2)}, u32[]{:S(2)}) collective-permute-start(bf16[16,3584]{1,0:T(8,128)(2,1)S(1)} %get-tuple-element.92), channel_id=1, source_target_pairs={{0,1},{1,0},{2,3},{3,2},{4,5},{5,4},{6,7},{7,6},{8,9},{9,8},{10,11... | collective-permute-start | bytes 344072 | tf_op jit(solution)/shard_map/own_rear_1/ppermute | solution.py:26
  82.2 1.9 %collective-permute-start.21 = (bf16[2,32,3584]{2,1,0:T(8,128)(2,1)S(1)}, bf16[2,32,3584]{2,1,0:T(8,128)(2,1)S(1)}, u32[]{:S(2)}, u32[]{:S(2)}) collective-permute-start(bf16[2,32,3584]{2,1,0:T(8,128)(2,1)S(1)} %pad_maximum_fusion.refs_2_), channel_id=1, source_target_pairs={{0,2},{2,0},{4,6},{6,4},{8,10},{10,8},{12,14},{14,12},{16,18},{18,... | collective-permute-start | bytes 1376264 | tf_op jit(solution)/shard_map/pair_stay_1/ppermute | solution.py:20
  83.1 1.9 %collective-permute-start.25 = (bf16[2,32,3584]{2,1,0:T(8,128)(2,1)S(1)}, bf16[2,32,3584]{2,1,0:T(8,128)(2,1)S(1)}, u32[]{:S(2)}, u32[]{:S(2)}) collective-permute-start(bf16[2,32,3584]{2,1,0:T(8,128)(2,1)S(1)} %maximum_maximum_fusion.refs_4_), channel_id=1, source_target_pairs={{0,2},{2,0},{4,6},{6,4},{8,10},{10,8},{12,14},{14,12},{16,18},{18,... | collective-permute-start | bytes 1376264 | tf_op jit(solution)/shard_map/pair_leave_1/ppermute | solution.py:20

commit v5 on v4

--- a/solution.py
+++ b/solution.py
@@ -103,6 +103,49 @@
     return copies
 
 
+def column_copies(source, target, sem, start):
+    count = parts_of(source.shape[1], 128)
+    step = source.shape[1] // count
+    copies = []
+    for p in range(count):
+        rows = pl.ds(p * step, step)
+        part = source.at[0, rows, pl.ds(start, target.shape[2])]
+        copies.append(pltpu.make_async_copy(part, target.at[0, rows], sem.at[p]))
+    return copies
+
+
+def down_tile(width):
+    return tile_of(width, 512)
+
+
+def first_columns(width):
+    tile = down_tile(width)
+    return (width // tile + 1) // 2 * tile
+
+
+def first_kernel(source, target, sem):
+    copies = column_copies(source, target, sem, 0)
+    for copy in copies:
+        copy.start()
+    for copy in copies:
+        copy.wait()
+
+
+def first_loaded(weight):
+    shape = (1, weight.shape[1], first_columns(weight.shape[2]))
+    return pl.pallas_call(
+        first_kernel,
+        in_specs=[pl.BlockSpec(memory_space=pltpu.HBM)],
+        out_specs=pl.BlockSpec(memory_space=pltpu.VMEM),
+        out_shape=pltpu.VMEM(shape, weight.dtype),
+        scratch_shapes=[pltpu.SemaphoreType.DMA((PARTS,))],
+        compiler_params=pltpu.CompilerParams(vmem_limit_bytes=ROOM),
+        cost_estimate=pl.CostEstimate(
+            flops=0, bytes_accessed=shape[1] * shape[2] * weight.dtype.itemsize, transcendentals=0
+        ),
+    )(pltpu.with_memory_space_constraint(weight, pltpu.HBM))
+
+
 def load_kernel(count, *refs):
     sources, targets, sem = refs[:count], refs[count:-1], refs[-1]
     copies = []
@@ -200,41 +243,55 @@
 
 
 def down_kernel(half, groups, place, *refs):
-    parts, (weight_ref, out_ref) = refs[:-2], refs[-2:]
+    parts, (first_ref, weight_hbm, out_ref, rest_ref, sem) = refs[:-5], refs[-5:]
     size, units = len(parts) // groups, parts[0].shape[1]
-    tile = tile_of(out_ref.shape[1], 512)
-
-    @pl.loop(0, out_ref.shape[1] // tile)
-    def _(n):
-        columns = pl.ds(pl.multiple_of(n * tile, tile), tile)
-        total = jnp.zeros((out_ref.shape[0], tile), jnp.float32)
-        for k in range(size):
-            owner = lax.rem(place[0] + (size - k), size)
-            rows = pl.ds(pl.multiple_of(owner * units, units), units)
-            left = []
-            for part in parts[k::size]:
-                left += [part[-k * half:], part[:-k * half]] if k else [part[...]]
-            total += matmul(jnp.concatenate(left, axis=0), weight_ref[0, rows, columns])
-        out_ref[:, columns] = total.astype(out_ref.dtype)
-
-
-def down_slices(groups, half, place, w_down):
+    tile, first = down_tile(out_ref.shape[1]), first_ref.shape[2]
+    copies = column_copies(weight_hbm, rest_ref, sem, first)
+    for copy in copies:
+        copy.start()
+
+    def columns_of(weight_ref, start):
+        @pl.loop(0, weight_ref.shape[2] // tile)
+        def _(n):
+            columns = pl.ds(pl.multiple_of(n * tile, tile), tile)
+            total = jnp.zeros((out_ref.shape[0], tile), jnp.float32)
+            for k in range(size):
+                owner = lax.rem(place[0] + (size - k), size)
+                rows = pl.ds(pl.multiple_of(owner * units, units), units)
+                left = []
+                for part in parts[k::size]:
+                    left += [part[-k * half:], part[:-k * half]] if k else [part[...]]
+                total += matmul(jnp.concatenate(left, axis=0), weight_ref[0, rows, columns])
+            out_ref[:, pl.ds(pl.multiple_of(start + n * tile, tile), tile)] = total.astype(out_ref.dtype)
+
+    columns_of(first_ref, 0)
+    for copy in copies:
+        copy.wait()
+    columns_of(rest_ref, first)
+
+
+def down_slices(groups, half, place, first, w_down):
     units, width = w_down.shape[1:]
     parts = sum(groups, [])
     rows = sum(parts[0].shape[0] for parts in groups)
+    rest = (1, units, width - first.shape[2])
     vmem = pl.BlockSpec(memory_space=pltpu.VMEM)
+    limit = max(ROOM, 8 * rows * (units + width) + 2 * MIB) + 2 * rest[1] * rest[2]
     return pl.pallas_call(
         functools.partial(down_kernel, half, len(groups)),
-        in_specs=[pl.BlockSpec(memory_space=pltpu.SMEM)] + [vmem] * (len(parts) + 1),
+        in_specs=[pl.BlockSpec(memory_space=pltpu.SMEM)]
+        + [vmem] * (len(parts) + 1)
+        + [pl.BlockSpec(memory_space=pltpu.HBM)],
         out_specs=vmem,
         out_shape=jax.ShapeDtypeStruct((rows, width), jnp.bfloat16),
-        compiler_params=pltpu.CompilerParams(vmem_limit_bytes=max(ROOM, 8 * rows * (units + width) + 2 * MIB)),
+        scratch_shapes=[pltpu.VMEM(rest, w_down.dtype), pltpu.SemaphoreType.DMA((PARTS,))],
+        compiler_params=pltpu.CompilerParams(vmem_limit_bytes=limit),
         cost_estimate=pl.CostEstimate(
             flops=2 * rows * units * width,
             bytes_accessed=2 * rows * (units + width),
             transcendentals=0,
         ),
-    )(place, *parts, in_vmem(w_down))
+    )(place, *parts, in_vmem(first), pltpu.with_memory_space_constraint(w_down, pltpu.HBM))
 
 
 def mix_kernel(blocks, *refs):
@@ -324,7 +381,7 @@
     hidden, = hidden_units(leave, w_gate, w_up, False)
     stay, hidden, w_down = lax.optimization_barrier((stay, hidden, w_down))
     leave = [hidden] + over_blk(hidden, "hidden_leave")
-    output = down_slices([stay, leave], half, place, loaded(w_down)[0])
+    output = down_slices([stay, leave], half, place, first_loaded(w_down), w_down)
     stay, leave = output[:blocks * half], output[blocks * half:]
 
     def back(pieces, turn, name):

time: 86.5 us -> 86.3 us (level)
  starting transfers between devices: 39.1 us -> 40.1 us
    pallas_call x3 -> x2, Pallas kernels: 11.9 us -> 6.6 us  [loaded(): pl.pallas_call(functools.partial(load_kernel, count), in_specs=[pl.BlockS...]
    pallas_call x0 -> x1, Pallas kernels: none -> 3.5 us  [first_loaded(): pl.pallas_call(first_kernel, in_specs=[pl.BlockSpec(memory_space=pltpu.HB...]
    ppermute x18, waiting for transfers between devices: 14.4 us -> 12.3 us  [exchanged(): return lax.ppermute(block, 'expert', [(i, i ^ mask) for i in range(size)])]
    ppermute x18, starting transfers between devices: 29.1 us -> 31.1 us  [exchanged(): return lax.ppermute(block, 'expert', [(i, i ^ mask) for i in range(size)])]
    ppermute x8, waiting for transfers between devices: 1.77 us -> 3.42 us  [shifted(): lax.ppermute(block, 'blk', [(i, (i + steps) % size) for i in range(size)])]
    pallas_call x1, Pallas kernels: 3.24 us -> 4.26 us  [down_slices(): pl.pallas_call(functools.partial(down_kernel, half, len(groups)), in_spec...]
    ppermute x8, starting transfers between devices: 9.94 us -> 8.99 us  [shifted(): lax.ppermute(block, 'blk', [(i, (i + steps) % size) for i in range(size)])]
  transfers between devices with their start and end apart: 26 -> 26, of which waited for: 13 -> 12; matrix products, arithmetic and copies ran while one was open for 0% -> 0% of each run, Pallas kernels for 29% -> 27%
where the time goes in v5:
time: 86.3 us; the launch traced here: 86.1 us
  starting transfers between devices  40.1 us (46%)
  Pallas kernels  29.7 us (34%)
  waiting for transfers between devices  15.7 us (18%)
    ppermute x18, starting transfers between devices, exchanged(): return lax.ppermute(block, 'expert', [(i, i ^ mask) for i in range(size)])  31.1 us
    pallas_call x2, Pallas kernels, hidden_units(): pl.pallas_call(functools.partial(first_hidden_kernel if first else hidden...  13.2 us
    ppermute x18, waiting for transfers between devices, exchanged(): return lax.ppermute(block, 'expert', [(i, i ^ mask) for i in range(size)])  12.3 us
    ppermute x8, starting transfers between devices, shifted(): lax.ppermute(block, 'blk', [(i, (i + steps) % size) for i in range(size)])  8.99 us
    pallas_call x2, Pallas kernels, loaded(): pl.pallas_call(functools.partial(load_kernel, count), in_specs=[pl.BlockS...  6.6 us
    pallas_call x1, Pallas kernels, down_slices(): pl.pallas_call(functools.partial(down_kernel, half, len(groups)), in_spec...  4.26 us
    pallas_call x1, Pallas kernels, first_loaded(): pl.pallas_call(first_kernel, in_specs=[pl.BlockSpec(memory_space=pltpu.HB...  3.5 us
    ppermute x8, waiting for transfers between devices, shifted(): lax.ppermute(block, 'blk', [(i, (i + steps) % size) for i in range(size)])  3.42 us
  transfers between devices with their start and end apart: 26, of which 12 were waited for; matrix products, arithmetic and copies ran while one was open for 0% of the time, Pallas kernels for 27%

profile of v5, /device:TPU:0, one launch (start us, length us, event | category | flops | bytes accessed | tf_op | source)
XLA Modules:
  0.0 86.1 jit_solution(120359555915078791)
XLA Ops:
  0.5 1.3 %shard_map.64 = (s32[8,64]{1,0:T(8,128)S(1)}, bf16[8,64]{1,0:T(8,128)(2,1)S(1)}, bf16[64,7168]{1,0:T(8,128)(2,1)S(1)}) custom-call(s32[8,64]{1,0:T(8,128)} %bitcast.18, bf16[8,64]{1,0:T(8,128)(2,1)} %bitcast.19, bf16[64,7168]{1,0:T(8,128)(2,1)} %refs_2_.1), custom_call_target="tpu_custom_call" | custom-call | bytes 920576 | tf_op jit(solution)/shard_map/pallas_call | solution.py:165
  1.8 0.9 %collective-permute-done.other_ids_ref = s32[8,64]{1,0:T(8,128)S(1)} collective-permute-done((s32[8,64]{1,0:T(8,128)}, s32[8,64]{1,0:T(8,128)S(1)}, u32[]{:S(2)}, u32[]{:S(2)}) %collective-permute-start) | collective-permute-done | bytes 2080 | tf_op jit(solution)/shard_map/ids_1/ppermute | solution.py:20
  3.6 3.0 %collective-permute-start.2 = (bf16[8,7168]{1,0:T(8,128)(2,1)S(1)}, bf16[8,7168]{1,0:T(8,128)(2,1)S(1)}, u32[]{:S(2)}, u32[]{:S(2)}) collective-permute-start(bf16[8,7168]{1,0:T(8,128)(2,1)S(1)} %get-tuple-element.79), channel_id=1, source_target_pairs={{0,8},{2,10},{4,12},{6,14},{8,0},{10,2},{12,4},{14,6},{16,24},{18,... | collective-permute-start | bytes 344072 | tf_op jit(solution)/shard_map/go_stay_4/ppermute | solution.py:20
  6.6 1.5 %collective-permute-start.3 = (bf16[8,7168]{1,0:T(8,128)(2,1)S(1)}, bf16[8,7168]{1,0:T(8,128)(2,1)S(1)}, u32[]{:S(2)}, u32[]{:S(2)}) collective-permute-start(bf16[8,7168]{1,0:T(8,128)(2,1)S(1)} %get-tuple-element.78), channel_id=1, source_target_pairs={{0,4},{2,6},{4,0},{6,2},{8,12},{10,14},{12,8},{14,10},{16,20},{18,... | collective-permute-start | bytes 344072 | tf_op jit(solution)/shard_map/go_leave_2/ppermute | solution.py:20
  8.1 2.6 %collective-permute-start.4 = (bf16[8,7168]{1,0:T(8,128)(2,1)S(1)}, bf16[8,7168]{1,0:T(8,128)(2,1)S(1)}, u32[]{:S(2)}, u32[]{:S(2)}) collective-permute-start(bf16[8,7168]{1,0:T(8,128)(2,1)S(1)} %get-tuple-element.74), channel_id=1, source_target_pairs={{0,16},{2,18},{4,20},{6,22},{8,24},{10,26},{12,28},{14,30},{16,0},... | collective-permute-start | bytes 344072 | tf_op jit(solution)/shard_map/go_stay_8/ppermute | solution.py:20
  11.6 1.6 %collective-permute-start.6 = (bf16[24,7168]{1,0:T(8,128)(2,1)S(1)}, bf16[24,7168]{1,0:T(8,128)(2,1)S(1)}, u32[]{:S(2)}, u32[]{:S(2)}) collective-permute-start(bf16[24,7168]{1,0:T(8,128)(2,1)S(1)} %pad_maximum_fusion.2.refs_0_), channel_id=1, source_target_pairs={{0,1},{1,0},{2,3},{3,2},{4,5},{5,4},{6,7},{7,6},{8,9},{9,8},{10,11... | collective-permute-start | bytes 1032200 | tf_op jit(solution)/shard_map/blk_early_1/ppermute | solution.py:26
  13.1 1.4 %collective-permute-start.7 = (bf16[8,7168]{1,0:T(8,128)(2,1)S(1)}, bf16[8,7168]{1,0:T(8,128)(2,1)S(1)}, u32[]{:S(2)}, u32[]{:S(2)}) collective-permute-start(bf16[8,7168]{1,0:T(8,128)(2,1)S(1)} %get-tuple-element.49), channel_id=1, source_target_pairs={{0,12},{2,14},{4,8},{6,10},{8,4},{10,6},{12,0},{14,2},{16,28},{18,... | collective-permute-start | bytes 344072 | tf_op jit(solution)/shard_map/go_leave_6/ppermute | solution.py:20
  14.5 3.5 %collective-permute-start.9 = (bf16[8,7168]{1,0:T(8,128)(2,1)S(1)}, bf16[8,7168]{1,0:T(8,128)(2,1)S(1)}, u32[]{:S(2)}, u32[]{:S(2)}) collective-permute-start(bf16[8,7168]{1,0:T(8,128)(2,1)S(1)} %get-tuple-element.52), channel_id=1, source_target_pairs={{0,28},{2,30},{4,24},{6,26},{8,20},{10,22},{12,16},{14,18},{16,12}... | collective-permute-start | bytes 344072 | tf_op jit(solution)/shard_map/go_leave_14/ppermute | solution.py:20
  18.1 2.7 %collective-permute-done.4 = bf16[8,7168]{1,0:T(8,128)(2,1)S(1)} collective-permute-done((bf16[8,7168]{1,0:T(8,128)(2,1)S(1)}, bf16[8,7168]{1,0:T(8,128)(2,1)S(1)}, u32[]{:S(2)}, u32[]{:S(2)}) %collective-permute-start.4) | collective-permute-done | bytes 114720 | tf_op jit(solution)/shard_map/go_stay_8/ppermute | solution.py:20
  20.7 2.6 %collective-permute-done.7.refs_1_ = bf16[8,7168]{1,0:T(8,128)(2,1)S(1)} collective-permute-done((bf16[8,7168]{1,0:T(8,128)(2,1)S(1)}, bf16[8,7168]{1,0:T(8,128)(2,1)S(1)}, u32[]{:S(2)}, u32[]{:S(2)}) %collective-permute-start.7) | collective-permute-done | bytes 114720 | tf_op jit(solution)/shard_map/go_leave_6/ppermute | solution.py:20
  24.1 1.6 %collective-permute-start.8 = (bf16[16,7168]{1,0:T(8,128)(2,1)S(1)}, bf16[16,7168]{1,0:T(8,128)(2,1)S(1)}, u32[]{:S(2)}, u32[]{:S(2)}) collective-permute-start(bf16[16,7168]{1,0:T(8,128)(2,1)S(1)} %constant_dynamic-update-slice_fusion.refs_1_), channel_id=1, source_target_pairs={{0,1},{1,0},{2,3},{3,2},{4,5},{5,4},{6,7},{7,6},{8,9},{9,8},{10,11... | collective-permute-start | bytes 688136 | tf_op jit(solution)/shard_map/blk_late_1/ppermute | solution.py:26
  25.7 5.3 %shard_map.66.refs_4_.refs_8_ = bf16[1,7168,1024]{2,1,0:T(8,128)(2,1)S(1)} custom-call(bf16[1,7168,1024]{2,1,0:T(8,128)(2,1)} %refs_0_), custom_call_target="tpu_custom_call" | custom-call | bytes 14680064 | tf_op jit(solution)/shard_map/pallas_call | solution.py:165
  31.1 1.3 %collective-permute-start.13 = (bf16[16,7168]{1,0:T(8,128)(2,1)S(1)}, bf16[16,7168]{1,0:T(8,128)(2,1)S(1)}, u32[]{:S(2)}, u32[]{:S(2)}) collective-permute-start(bf16[16,7168]{1,0:T(8,128)(2,1)S(1)} %pad_maximum_fusion.3.refs_2_.refs_3_), channel_id=1, source_target_pairs={{0,1},{1,0},{2,3},{3,2},{4,5},{5,4},{6,7},{7,6},{8,9},{9,8},{10,11... | collective-permute-start | bytes 688136 | tf_op jit(solution)/shard_map/blk_most_1/ppermute | solution.py:26
  33.2 7.4 %shard_map.67 = (bf16[64,1024]{1,0:T(8,128)(2,1)S(1)}, bf16[1,7168,1024]{2,1,0:T(8,128)(2,1)S(1)}) custom-call(bf16[24,7168]{1,0:T(8,128)(2,1)S(1)} %pad_maximum_fusion.2.refs_0_, bf16[16,7168]{1,0:T(8,128)(2,1)S(1)} %constant_dynamic-update-slice_fusion.refs_1_, bf16[24,7168]{1,0:T(8,128)(2,1)S(1)} %collective-permute-done.6.refs_2_.refs_4_, ...), custom_call_target="tpu_custom_call" | custom-call | flops 1879048192 | bytes 1048576 | tf_op jit(solution)/shard_map/pallas_call | solution.py:230
  40.6 1.3 %collective-permute-start.11 = (bf16[64,1024]{1,0:T(8,128)(2,1)S(1)}, bf16[64,1024]{1,0:T(8,128)(2,1)S(1)}, u32[]{:S(2)}, u32[]{:S(2)}) collective-permute-start(bf16[64,1024]{1,0:T(8,128)(2,1)S(1)} %get-tuple-element.60.refs_0_), channel_id=1, source_target_pairs={{0,1},{1,0},{2,3},{3,2},{4,5},{5,4},{6,7},{7,6},{8,9},{9,8},{10,11... | collective-permute-start | bytes 393224 | tf_op jit(solution)/shard_map/hidden_stay_1/ppermute | solution.py:26
  41.9 5.8 %shard_map.68.refs_2_ = bf16[64,1024]{1,0:T(8,128)(2,1)S(1)} custom-call(bf16[24,7168]{1,0:T(8,128)(2,1)S(1)} %pad_maximum_fusion.2.refs_0_, bf16[8,7168]{1,0:T(8,128)(2,1)S(1)} %collective-permute-done.7.refs_1_, bf16[16,7168]{1,0:T(8,128)(2,1)S(1)} %pad_maximum_fusion.3.refs_2_.refs_3_, bf16[16,7168]{1,0:T(8,128)(2,1)S(1)} %pad_maximum_fusion.3.refs_2_.refs_3_, ...), custom_call_target="tpu_custom_call" | custom-call | flops 1879048192 | bytes 1048576 | tf_op jit(solution)/shard_map/pallas_call | solution.py:230
  47.8 0.8 collective-permute-start.14
  48.6 3.5 %shard_map.69.refs_4_ = bf16[1,2048,2048]{2,1,0:T(8,128)(2,1)S(1)} custom-call(bf16[1,2048,3584]{2,1,0:T(8,128)(2,1)} %refs_5_.2), custom_call_target="tpu_custom_call" | custom-call | bytes 8388608 | tf_op jit(solution)/shard_map/pallas_call | solution.py:136
  52.8 4.3 %shard_map.70 = bf16[128,3584]{1,0:T(8,128)(2,1)S(1)} custom-call(s32[1]{0:T(128)} %bitcast.place.refs_0_, bf16[64,1024]{1,0:T(8,128)(2,1)S(1)} %get-tuple-element.60.refs_0_, bf16[64,1024]{1,0:T(8,128)(2,1)S(1)} %collective-permute-done.11.refs_1_, bf16[64,1024]{1,0:T(8,128)(2,1)S(1)} %shard_map.68.refs_2_, ...), custom_call_target="tpu_custom_call" | custom-call | flops 1879048192 | bytes 1441792 | tf_op jit(solution)/shard_map/pallas_call | solution.py:280
  57.3 0.8 collective-permute-start.15
  58.1 3.3 %collective-permute-start.16 = (bf16[2,8,3584]{2,1,0:T(8,128)(2,1)S(1)}, bf16[2,8,3584]{2,1,0:T(8,128)(2,1)S(1)}, u32[]{:S(2)}, u32[]{:S(2)}) collective-permute-start(bf16[2,8,3584]{2,1,0:T(8,128)(2,1)S(1)} %get-tuple-element.89), channel_id=1, source_target_pairs={{0,28},{2,30},{4,24},{6,26},{8,20},{10,22},{12,16},{14,18},{16,12}... | collective-permute-start | bytes 344072 | tf_op jit(solution)/shard_map/back_leave_14/ppermute | solution.py:20
  61.4 2.1 %collective-permute-start.18 = (bf16[2,8,3584]{2,1,0:T(8,128)(2,1)S(1)}, bf16[2,8,3584]{2,1,0:T(8,128)(2,1)S(1)}, u32[]{:S(2)}, u32[]{:S(2)}) collective-permute-start(bf16[2,8,3584]{2,1,0:T(8,128)(2,1)S(1)} %get-tuple-element.90), channel_id=1, source_target_pairs={{0,20},{2,22},{4,16},{6,18},{8,28},{10,30},{12,24},{14,26},{16,4},... | collective-permute-start | bytes 344072 | tf_op jit(solution)/shard_map/back_leave_10/ppermute | solution.py:20
  63.5 1.0 %collective-permute-done.15 = bf16[48,3584]{1,0:T(8,128)(2,1)S(1)} collective-permute-done((bf16[48,3584]{1,0:T(8,128)(2,1)S(1)}, bf16[48,3584]{1,0:T(8,128)(2,1)S(1)}, u32[]{:S(2)}, u32[]{:S(2)}) %collective-permute-start.15) | collective-permute-done | bytes 344096 | tf_op jit(solution)/shard_map/own_front_1/ppermute | solution.py:26
  64.6 2.7 %collective-permute-start.19 = (bf16[2,8,3584]{2,1,0:T(8,128)(2,1)S(1)}, bf16[2,8,3584]{2,1,0:T(8,128)(2,1)S(1)}, u32[]{:S(2)}, u32[]{:S(2)}) collective-permute-start(bf16[2,8,3584]{2,1,0:T(8,128)(2,1)S(1)} %get-tuple-element.86), channel_id=1, source_target_pairs={{0,16},{2,18},{4,20},{6,22},{8,24},{10,26},{12,28},{14,30},{16,0},... | collective-permute-start | bytes 344072 | tf_op jit(solution)/shard_map/back_stay_8/ppermute | solution.py:20
  67.5 5.6 %collective-permute-start.23 = (bf16[2,8,3584]{2,1,0:T(8,128)(2,1)S(1)}, bf16[2,8,3584]{2,1,0:T(8,128)(2,1)S(1)}, u32[]{:S(2)}, u32[]{:S(2)}) collective-permute-start(bf16[2,8,3584]{2,1,0:T(8,128)(2,1)S(1)} %get-tuple-element.68), channel_id=1, source_target_pairs={{0,12},{2,14},{4,8},{6,10},{8,4},{10,6},{12,0},{14,2},{16,28},{18,... | collective-permute-start | bytes 344072 | tf_op jit(solution)/shard_map/back_leave_6/ppermute | solution.py:20
  73.0 1.4 %collective-permute-done.18 = bf16[2,8,3584]{2,1,0:T(8,128)(2,1)S(1)} collective-permute-done((bf16[2,8,3584]{2,1,0:T(8,128)(2,1)S(1)}, bf16[2,8,3584]{2,1,0:T(8,128)(2,1)S(1)}, u32[]{:S(2)}, u32[]{:S(2)}) %collective-permute-start.18) | collective-permute-done | bytes 114720 | tf_op jit(solution)/shard_map/back_leave_10/ppermute | solution.py:20
  74.4 3.5 %collective-permute-start.20 = (bf16[2,8,3584]{2,1,0:T(8,128)(2,1)S(1)}, bf16[2,8,3584]{2,1,0:T(8,128)(2,1)S(1)}, u32[]{:S(2)}, u32[]{:S(2)}) collective-permute-start(bf16[2,8,3584]{2,1,0:T(8,128)(2,1)S(1)} %get-tuple-element.85), channel_id=1, source_target_pairs={{0,24},{2,26},{4,28},{6,30},{8,16},{10,18},{12,20},{14,22},{16,8},... | collective-permute-start | bytes 344072 | tf_op jit(solution)/shard_map/back_stay_12/ppermute | solution.py:20
  78.0 0.8 collective-permute-start.24
  79.1 1.9 %collective-permute-done.20 = bf16[2,8,3584]{2,1,0:T(8,128)(2,1)S(1)} collective-permute-done((bf16[2,8,3584]{2,1,0:T(8,128)(2,1)S(1)}, bf16[2,8,3584]{2,1,0:T(8,128)(2,1)S(1)}, u32[]{:S(2)}, u32[]{:S(2)}) %collective-permute-start.20) | collective-permute-done | bytes 114720 | tf_op jit(solution)/shard_map/back_stay_12/ppermute | solution.py:20
  81.1 1.7 %collective-permute-done.24 = bf16[16,3584]{1,0:T(8,128)(2,1)S(1)} collective-permute-done((bf16[16,3584]{1,0:T(8,128)(2,1)S(1)}, bf16[16,3584]{1,0:T(8,128)(2,1)S(1)}, u32[]{:S(2)}, u32[]{:S(2)}) %collective-permute-start.24) | collective-permute-done | bytes 114720 | tf_op jit(solution)/shard_map/own_rear_1/ppermute | solution.py:26
  82.9 1.8 %collective-permute-done.25.refs_5_ = bf16[2,32,3584]{2,1,0:T(8,128)(2,1)S(1)} collective-permute-done((bf16[2,32,3584]{2,1,0:T(8,128)(2,1)S(1)}, bf16[2,32,3584]{2,1,0:T(8,128)(2,1)S(1)}, u32[]{:S(2)}, u32[]{:S(2)}) %collective-permute-start.25) | collective-permute-done | bytes 458784 | tf_op jit(solution)/shard_map/pair_leave_1/ppermute | solution.py:20
  84.7 1.4 %shard_map.71 = bf16[64,7168]{1,0:T(8,128)(2,1)} custom-call(s32[1]{0:T(128)} %bitcast.place.refs_0_, bf16[128,64]{1,0:T(8,128)(2,1)S(1)} %get-tuple-element.44.refs_1_, bf16[2,32,3584]{2,1,0:T(8,128)(2,1)S(1)} %pad_maximum_fusion.refs_2_, bf16[2,32,3584]{2,1,0:T(8,128)(2,1)S(1)} %collective-permute-done.21.refs_3_, ...), custom_call_target="tpu_custom_call" | custom-call | tf_op jit(solution)/shard_map/pallas_call | solution.py:315
  (43 shorter events, 5.5 us)
Async XLA Ops:
  0.0 2.8 %collective-permute-start.1 = (bf16[64,7168]{1,0:T(8,128)(2,1)}, bf16[64,7168]{1,0:T(8,128)(2,1)S(1)}, u32[]{:S(2)}, u32[]{:S(2)}) collective-permute-start(bf16[64,7168]{1,0:T(8,128)(2,1)} %refs_2_.1), channel_id=1, source_target_pairs={{0,2},{2,0},{4,6},{6,4},{8,10},{10,8},{12,14},{14,12},{16,18},{18,... | collective-permute-start | bytes 2752520 | tf_op jit(solution)/shard_map/tokens_1/ppermute | solution.py:20
  0.5 2.3 %collective-permute-start = (s32[8,64]{1,0:T(8,128)}, s32[8,64]{1,0:T(8,128)S(1)}, u32[]{:S(2)}, u32[]{:S(2)}) collective-permute-start(s32[8,64]{1,0:T(8,128)} %bitcast.17), channel_id=1, source_target_pairs={{0,2},{2,0},{4,6},{6,4},{8,10},{10,8},{12,14},{14,12},{16,18},{18,... | collective-permute-start | bytes 6152 | tf_op jit(solution)/shard_map/ids_1/ppermute | solution.py:20
  3.6 7.3 %collective-permute-start.2 = (bf16[8,7168]{1,0:T(8,128)(2,1)S(1)}, bf16[8,7168]{1,0:T(8,128)(2,1)S(1)}, u32[]{:S(2)}, u32[]{:S(2)}) collective-permute-start(bf16[8,7168]{1,0:T(8,128)(2,1)S(1)} %get-tuple-element.79), channel_id=1, source_target_pairs={{0,8},{2,10},{4,12},{6,14},{8,0},{10,2},{12,4},{14,6},{16,24},{18,... | collective-permute-start | bytes 344072 | tf_op jit(solution)/shard_map/go_stay_4/ppermute | solution.py:20
  6.6 4.9 %collective-permute-start.3 = (bf16[8,7168]{1,0:T(8,128)(2,1)S(1)}, bf16[8,7168]{1,0:T(8,128)(2,1)S(1)}, u32[]{:S(2)}, u32[]{:S(2)}) collective-permute-start(bf16[8,7168]{1,0:T(8,128)(2,1)S(1)} %get-tuple-element.78), channel_id=1, source_target_pairs={{0,4},{2,6},{4,0},{6,2},{8,12},{10,14},{12,8},{14,10},{16,20},{18,... | collective-permute-start | bytes 344072 | tf_op jit(solution)/shard_map/go_leave_2/ppermute | solution.py:20
  8.1 12.6 %collective-permute-start.4 = (bf16[8,7168]{1,0:T(8,128)(2,1)S(1)}, bf16[8,7168]{1,0:T(8,128)(2,1)S(1)}, u32[]{:S(2)}, u32[]{:S(2)}) collective-permute-start(bf16[8,7168]{1,0:T(8,128)(2,1)S(1)} %get-tuple-element.74), channel_id=1, source_target_pairs={{0,16},{2,18},{4,20},{6,22},{8,24},{10,26},{12,28},{14,30},{16,0},... | collective-permute-start | bytes 344072 | tf_op jit(solution)/shard_map/go_stay_8/ppermute | solution.py:20
  10.7 13.4 %collective-permute-start.5 = (bf16[8,7168]{1,0:T(8,128)(2,1)S(1)}, bf16[8,7168]{1,0:T(8,128)(2,1)S(1)}, u32[]{:S(2)}, u32[]{:S(2)}) collective-permute-start(bf16[8,7168]{1,0:T(8,128)(2,1)S(1)} %get-tuple-element.73), channel_id=1, source_target_pairs={{0,24},{2,26},{4,28},{6,30},{8,16},{10,18},{12,20},{14,22},{16,8},... | collective-permute-start | bytes 344072 | tf_op jit(solution)/shard_map/go_stay_12/ppermute | solution.py:20
  11.6 11.8 %collective-permute-start.6 = (bf16[24,7168]{1,0:T(8,128)(2,1)S(1)}, bf16[24,7168]{1,0:T(8,128)(2,1)S(1)}, u32[]{:S(2)}, u32[]{:S(2)}) collective-permute-start(bf16[24,7168]{1,0:T(8,128)(2,1)S(1)} %pad_maximum_fusion.2.refs_0_), channel_id=1, source_target_pairs={{0,1},{1,0},{2,3},{3,2},{4,5},{5,4},{6,7},{7,6},{8,9},{9,8},{10,11... | collective-permute-start | bytes 1032200 | tf_op jit(solution)/shard_map/blk_early_1/ppermute | solution.py:26
  13.1 10.2 %collective-permute-start.7 = (bf16[8,7168]{1,0:T(8,128)(2,1)S(1)}, bf16[8,7168]{1,0:T(8,128)(2,1)S(1)}, u32[]{:S(2)}, u32[]{:S(2)}) collective-permute-start(bf16[8,7168]{1,0:T(8,128)(2,1)S(1)} %get-tuple-element.49), channel_id=1, source_target_pairs={{0,12},{2,14},{4,8},{6,10},{8,4},{10,6},{12,0},{14,2},{16,28},{18,... | collective-permute-start | bytes 344072 | tf_op jit(solution)/shard_map/go_leave_6/ppermute | solution.py:20
  14.5 16.5 %collective-permute-start.9 = (bf16[8,7168]{1,0:T(8,128)(2,1)S(1)}, bf16[8,7168]{1,0:T(8,128)(2,1)S(1)}, u32[]{:S(2)}, u32[]{:S(2)}) collective-permute-start(bf16[8,7168]{1,0:T(8,128)(2,1)S(1)} %get-tuple-element.52), channel_id=1, source_target_pairs={{0,28},{2,30},{4,24},{6,26},{8,20},{10,22},{12,16},{14,18},{16,12}... | collective-permute-start | bytes 344072 | tf_op jit(solution)/shard_map/go_leave_14/ppermute | solution.py:20
  23.3 7.8 %collective-permute-start.10 = (bf16[8,7168]{1,0:T(8,128)(2,1)S(1)}, bf16[8,7168]{1,0:T(8,128)(2,1)S(1)}, u32[]{:S(2)}, u32[]{:S(2)}) collective-permute-start(bf16[8,7168]{1,0:T(8,128)(2,1)S(1)} %get-tuple-element.53), channel_id=1, source_target_pairs={{0,20},{2,22},{4,16},{6,18},{8,28},{10,30},{12,24},{14,26},{16,4},... | collective-permute-start | bytes 344072 | tf_op jit(solution)/shard_map/go_leave_10/ppermute | solution.py:20
  24.1 9.1 %collective-permute-start.8 = (bf16[16,7168]{1,0:T(8,128)(2,1)S(1)}, bf16[16,7168]{1,0:T(8,128)(2,1)S(1)}, u32[]{:S(2)}, u32[]{:S(2)}) collective-permute-start(bf16[16,7168]{1,0:T(8,128)(2,1)S(1)} %constant_dynamic-update-slice_fusion.refs_1_), channel_id=1, source_target_pairs={{0,1},{1,0},{2,3},{3,2},{4,5},{5,4},{6,7},{7,6},{8,9},{9,8},{10,11... | collective-permute-start | bytes 688136 | tf_op jit(solution)/shard_map/blk_late_1/ppermute | solution.py:26
  31.1 10.8 %collective-permute-start.13 = (bf16[16,7168]{1,0:T(8,128)(2,1)S(1)}, bf16[16,7168]{1,0:T(8,128)(2,1)S(1)}, u32[]{:S(2)}, u32[]{:S(2)}) collective-permute-start(bf16[16,7168]{1,0:T(8,128)(2,1)S(1)} %pad_maximum_fusion.3.refs_2_.refs_3_), channel_id=1, source_target_pairs={{0,1},{1,0},{2,3},{3,2},{4,5},{5,4},{6,7},{7,6},{8,9},{9,8},{10,11... | collective-permute-start | bytes 688136 | tf_op jit(solution)/shard_map/blk_most_1/ppermute | solution.py:26
  32.4 9.5 %collective-permute-start.12 = (bf16[8,7168]{1,0:T(8,128)(2,1)S(1)}, bf16[8,7168]{1,0:T(8,128)(2,1)S(1)}, u32[]{:S(2)}, u32[]{:S(2)}) collective-permute-start(bf16[8,7168]{1,0:T(8,128)(2,1)S(1)} %collective-permute-done.7.refs_1_), channel_id=1, source_target_pairs={{0,1},{1,0},{2,3},{3,2},{4,5},{5,4},{6,7},{7,6},{8,9},{9,8},{10,11... | collective-permute-start | bytes 344072 | tf_op jit(solution)/shard_map/blk_last_1/ppermute | solution.py:26
  40.6 7.2 %collective-permute-start.11 = (bf16[64,1024]{1,0:T(8,128)(2,1)S(1)}, bf16[64,1024]{1,0:T(8,128)(2,1)S(1)}, u32[]{:S(2)}, u32[]{:S(2)}) collective-permute-start(bf16[64,1024]{1,0:T(8,128)(2,1)S(1)} %get-tuple-element.60.refs_0_), channel_id=1, source_target_pairs={{0,1},{1,0},{2,3},{3,2},{4,5},{5,4},{6,7},{7,6},{8,9},{9,8},{10,11... | collective-permute-start | bytes 393224 | tf_op jit(solution)/shard_map/hidden_stay_1/ppermute | solution.py:26
  47.8 5.0 %collective-permute-start.14 = (bf16[64,1024]{1,0:T(8,128)(2,1)S(1)}, bf16[64,1024]{1,0:T(8,128)(2,1)S(1)}, u32[]{:S(2)}, u32[]{:S(2)}) collective-permute-start(bf16[64,1024]{1,0:T(8,128)(2,1)S(1)} %shard_map.68.refs_2_), channel_id=1, source_target_pairs={{0,1},{1,0},{2,3},{3,2},{4,5},{5,4},{6,7},{7,6},{8,9},{9,8},{10,11... | collective-permute-start | bytes 393224 | tf_op jit(solution)/shard_map/hidden_leave_1/ppermute | solution.py:26
  57.3 7.3 %collective-permute-start.15 = (bf16[48,3584]{1,0:T(8,128)(2,1)S(1)}, bf16[48,3584]{1,0:T(8,128)(2,1)S(1)}, u32[]{:S(2)}, u32[]{:S(2)}) collective-permute-start(bf16[48,3584]{1,0:T(8,128)(2,1)S(1)} %get-tuple-element.88), channel_id=1, source_target_pairs={{0,1},{1,0},{2,3},{3,2},{4,5},{5,4},{6,7},{7,6},{8,9},{9,8},{10,11... | collective-permute-start | bytes 1032200 | tf_op jit(solution)/shard_map/own_front_1/ppermute | solution.py:26
  58.1 9.2 %collective-permute-start.16 = (bf16[2,8,3584]{2,1,0:T(8,128)(2,1)S(1)}, bf16[2,8,3584]{2,1,0:T(8,128)(2,1)S(1)}, u32[]{:S(2)}, u32[]{:S(2)}) collective-permute-start(bf16[2,8,3584]{2,1,0:T(8,128)(2,1)S(1)} %get-tuple-element.89), channel_id=1, source_target_pairs={{0,28},{2,30},{4,24},{6,26},{8,20},{10,22},{12,16},{14,18},{16,12}... | collective-permute-start | bytes 344072 | tf_op jit(solution)/shard_map/back_leave_14/ppermute | solution.py:20
  61.4 13.0 %collective-permute-start.18 = (bf16[2,8,3584]{2,1,0:T(8,128)(2,1)S(1)}, bf16[2,8,3584]{2,1,0:T(8,128)(2,1)S(1)}, u32[]{:S(2)}, u32[]{:S(2)}) collective-permute-start(bf16[2,8,3584]{2,1,0:T(8,128)(2,1)S(1)} %get-tuple-element.90), channel_id=1, source_target_pairs={{0,20},{2,22},{4,16},{6,18},{8,28},{10,30},{12,24},{14,26},{16,4},... | collective-permute-start | bytes 344072 | tf_op jit(solution)/shard_map/back_leave_10/ppermute | solution.py:20
  64.6 13.3 %collective-permute-start.19 = (bf16[2,8,3584]{2,1,0:T(8,128)(2,1)S(1)}, bf16[2,8,3584]{2,1,0:T(8,128)(2,1)S(1)}, u32[]{:S(2)}, u32[]{:S(2)}) collective-permute-start(bf16[2,8,3584]{2,1,0:T(8,128)(2,1)S(1)} %get-tuple-element.86), channel_id=1, source_target_pairs={{0,16},{2,18},{4,20},{6,22},{8,24},{10,26},{12,28},{14,30},{16,0},... | collective-permute-start | bytes 344072 | tf_op jit(solution)/shard_map/back_stay_8/ppermute | solution.py:20
  67.3 13.8 %collective-permute-start.22 = (bf16[2,8,3584]{2,1,0:T(8,128)(2,1)S(1)}, bf16[2,8,3584]{2,1,0:T(8,128)(2,1)S(1)}, u32[]{:S(2)}, u32[]{:S(2)}) collective-permute-start(bf16[2,8,3584]{2,1,0:T(8,128)(2,1)S(1)} %get-tuple-element.67), channel_id=1, source_target_pairs={{0,4},{2,6},{4,0},{6,2},{8,12},{10,14},{12,8},{14,10},{16,20},{18,... | collective-permute-start | bytes 344072 | tf_op jit(solution)/shard_map/back_leave_2/ppermute | solution.py:20
  67.5 13.7 %collective-permute-start.23 = (bf16[2,8,3584]{2,1,0:T(8,128)(2,1)S(1)}, bf16[2,8,3584]{2,1,0:T(8,128)(2,1)S(1)}, u32[]{:S(2)}, u32[]{:S(2)}) collective-permute-start(bf16[2,8,3584]{2,1,0:T(8,128)(2,1)S(1)} %get-tuple-element.68), channel_id=1, source_target_pairs={{0,12},{2,14},{4,8},{6,10},{8,4},{10,6},{12,0},{14,2},{16,28},{18,... | collective-permute-start | bytes 344072 | tf_op jit(solution)/shard_map/back_leave_6/ppermute | solution.py:20
  73.0 6.1 %collective-permute-start.17 = (bf16[2,8,3584]{2,1,0:T(8,128)(2,1)S(1)}, bf16[2,8,3584]{2,1,0:T(8,128)(2,1)S(1)}, u32[]{:S(2)}, u32[]{:S(2)}) collective-permute-start(bf16[2,8,3584]{2,1,0:T(8,128)(2,1)S(1)} %get-tuple-element.64), channel_id=1, source_target_pairs={{0,8},{2,10},{4,12},{6,14},{8,0},{10,2},{12,4},{14,6},{16,24},{18,... | collective-permute-start | bytes 344072 | tf_op jit(solution)/shard_map/back_stay_4/ppermute | solution.py:20
  74.4 6.6 %collective-permute-start.20 = (bf16[2,8,3584]{2,1,0:T(8,128)(2,1)S(1)}, bf16[2,8,3584]{2,1,0:T(8,128)(2,1)S(1)}, u32[]{:S(2)}, u32[]{:S(2)}) collective-permute-start(bf16[2,8,3584]{2,1,0:T(8,128)(2,1)S(1)} %get-tuple-element.85), channel_id=1, source_target_pairs={{0,24},{2,26},{4,28},{6,30},{8,16},{10,18},{12,20},{14,22},{16,8},... | collective-permute-start | bytes 344072 | tf_op jit(solution)/shard_map/back_stay_12/ppermute | solution.py:20
  78.0 4.9 %collective-permute-start.24 = (bf16[16,3584]{1,0:T(8,128)(2,1)S(1)}, bf16[16,3584]{1,0:T(8,128)(2,1)S(1)}, u32[]{:S(2)}, u32[]{:S(2)}) collective-permute-start(bf16[16,3584]{1,0:T(8,128)(2,1)S(1)} %get-tuple-element.92), channel_id=1, source_target_pairs={{0,1},{1,0},{2,3},{3,2},{4,5},{5,4},{6,7},{7,6},{8,9},{9,8},{10,11... | collective-permute-start | bytes 344072 | tf_op jit(solution)/shard_map/own_rear_1/ppermute | solution.py:26
  81.0 1.9 %collective-permute-start.21 = (bf16[2,32,3584]{2,1,0:T(8,128)(2,1)S(1)}, bf16[2,32,3584]{2,1,0:T(8,128)(2,1)S(1)}, u32[]{:S(2)}, u32[]{:S(2)}) collective-permute-start(bf16[2,32,3584]{2,1,0:T(8,128)(2,1)S(1)} %pad_maximum_fusion.refs_2_), channel_id=1, source_target_pairs={{0,2},{2,0},{4,6},{6,4},{8,10},{10,8},{12,14},{14,12},{16,18},{18,... | collective-permute-start | bytes 1376264 | tf_op jit(solution)/shard_map/pair_stay_1/ppermute | solution.py:20
  82.8 1.9 %collective-permute-start.25 = (bf16[2,32,3584]{2,1,0:T(8,128)(2,1)S(1)}, bf16[2,32,3584]{2,1,0:T(8,128)(2,1)S(1)}, u32[]{:S(2)}, u32[]{:S(2)}) collective-permute-start(bf16[2,32,3584]{2,1,0:T(8,128)(2,1)S(1)} %maximum_maximum_fusion.refs_4_), channel_id=1, source_target_pairs={{0,2},{2,0},{4,6},{6,4},{8,10},{10,8},{12,14},{14,12},{16,18},{18,... | collective-permute-start | bytes 1376264 | tf_op jit(solution)/shard_map/pair_leave_1/ppermute | solution.py:20

commit v6 on v5

--- a/solution.py
+++ b/solution.py
@@ -120,7 +120,7 @@
 
 def first_columns(width):
     tile = down_tile(width)
-    return (width // tile + 1) // 2 * tile
+    return (2 * (width // tile) + 2) // 3 * tile
 
 
 def first_kernel(source, target, sem):

time: 86.3 us -> 85.9 us (level)
  waiting for transfers between devices: 15.7 us -> 17.1 us
  starting transfers between devices: 40.1 us -> 38.7 us
    ppermute x18, waiting for transfers between devices: 12.3 us -> 14.4 us  [exchanged(): return lax.ppermute(block, 'expert', [(i, i ^ mask) for i in range(size)])]
    ppermute x18, starting transfers between devices: 31.1 us -> 29.3 us  [exchanged(): return lax.ppermute(block, 'expert', [(i, i ^ mask) for i in range(size)])]
    pallas_call x1, Pallas kernels: 4.26 us -> 3.29 us  [down_slices(): pl.pallas_call(functools.partial(down_kernel, half, len(groups)), in_spec...]
  transfers between devices with their start and end apart: 26 -> 26, of which waited for: 12 -> 13; matrix products, arithmetic and copies ran while one was open for 0% -> 0% of each run, Pallas kernels for 27% -> 28%
where the time goes in v6:
time: 85.9 us; the launch traced here: 85.7 us
  starting transfers between devices  38.7 us (45%)
  Pallas kernels  29.3 us (34%)
  waiting for transfers between devices  17.1 us (20%)
    ppermute x18, starting transfers between devices, exchanged(): return lax.ppermute(block, 'expert', [(i, i ^ mask) for i in range(size)])  29.3 us
    ppermute x18, waiting for transfers between devices, exchanged(): return lax.ppermute(block, 'expert', [(i, i ^ mask) for i in range(size)])  14.4 us
    pallas_call x2, Pallas kernels, hidden_units(): pl.pallas_call(functools.partial(first_hidden_kernel if first else hidden...  13.2 us
    ppermute x8, starting transfers between devices, shifted(): lax.ppermute(block, 'blk', [(i, (i + steps) % size) for i in range(size)])  9.37 us
    pallas_call x2, Pallas kernels, loaded(): pl.pallas_call(functools.partial(load_kernel, count), in_specs=[pl.BlockS...  6.6 us
    pallas_call x1, Pallas kernels, first_loaded(): pl.pallas_call(first_kernel, in_specs=[pl.BlockSpec(memory_space=pltpu.HB...  4.1 us
    pallas_call x1, Pallas kernels, down_slices(): pl.pallas_call(functools.partial(down_kernel, half, len(groups)), in_spec...  3.29 us
    ppermute x8, waiting for transfers between devices, shifted(): lax.ppermute(block, 'blk', [(i, (i + steps) % size) for i in range(size)])  2.65 us
  transfers between devices with their start and end apart: 26, of which 13 were waited for; matrix products, arithmetic and copies ran while one was open for 0% of the time, Pallas kernels for 28%

profile of v6, /device:TPU:0, one launch (start us, length us, event | category | flops | bytes accessed | tf_op | source)
XLA Modules:
  0.0 85.7 jit_solution(14919808561312113758)
XLA Ops:
  0.5 1.3 %shard_map.64 = (s32[8,64]{1,0:T(8,128)S(1)}, bf16[8,64]{1,0:T(8,128)(2,1)S(1)}, bf16[64,7168]{1,0:T(8,128)(2,1)S(1)}) custom-call(s32[8,64]{1,0:T(8,128)} %bitcast.18, bf16[8,64]{1,0:T(8,128)(2,1)} %bitcast.19, bf16[64,7168]{1,0:T(8,128)(2,1)} %refs_2_.1), custom_call_target="tpu_custom_call" | custom-call | bytes 920576 | tf_op jit(solution)/shard_map/pallas_call | solution.py:165
  1.8 0.9 %collective-permute-done.other_ids_ref = s32[8,64]{1,0:T(8,128)S(1)} collective-permute-done((s32[8,64]{1,0:T(8,128)}, s32[8,64]{1,0:T(8,128)S(1)}, u32[]{:S(2)}, u32[]{:S(2)}) %collective-permute-start) | collective-permute-done | bytes 2080 | tf_op jit(solution)/shard_map/ids_1/ppermute | solution.py:20
  3.6 3.0 %collective-permute-start.2 = (bf16[8,7168]{1,0:T(8,128)(2,1)S(1)}, bf16[8,7168]{1,0:T(8,128)(2,1)S(1)}, u32[]{:S(2)}, u32[]{:S(2)}) collective-permute-start(bf16[8,7168]{1,0:T(8,128)(2,1)S(1)} %get-tuple-element.79), channel_id=1, source_target_pairs={{0,8},{2,10},{4,12},{6,14},{8,0},{10,2},{12,4},{14,6},{16,24},{18,... | collective-permute-start | bytes 344072 | tf_op jit(solution)/shard_map/go_stay_4/ppermute | solution.py:20
  6.6 1.5 %collective-permute-start.3 = (bf16[8,7168]{1,0:T(8,128)(2,1)S(1)}, bf16[8,7168]{1,0:T(8,128)(2,1)S(1)}, u32[]{:S(2)}, u32[]{:S(2)}) collective-permute-start(bf16[8,7168]{1,0:T(8,128)(2,1)S(1)} %get-tuple-element.78), channel_id=1, source_target_pairs={{0,4},{2,6},{4,0},{6,2},{8,12},{10,14},{12,8},{14,10},{16,20},{18,... | collective-permute-start | bytes 344072 | tf_op jit(solution)/shard_map/go_leave_2/ppermute | solution.py:20
  8.1 2.6 %collective-permute-start.4 = (bf16[8,7168]{1,0:T(8,128)(2,1)S(1)}, bf16[8,7168]{1,0:T(8,128)(2,1)S(1)}, u32[]{:S(2)}, u32[]{:S(2)}) collective-permute-start(bf16[8,7168]{1,0:T(8,128)(2,1)S(1)} %get-tuple-element.74), channel_id=1, source_target_pairs={{0,16},{2,18},{4,20},{6,22},{8,24},{10,26},{12,28},{14,30},{16,0},... | collective-permute-start | bytes 344072 | tf_op jit(solution)/shard_map/go_stay_8/ppermute | solution.py:20
  11.6 1.6 %collective-permute-start.6 = (bf16[24,7168]{1,0:T(8,128)(2,1)S(1)}, bf16[24,7168]{1,0:T(8,128)(2,1)S(1)}, u32[]{:S(2)}, u32[]{:S(2)}) collective-permute-start(bf16[24,7168]{1,0:T(8,128)(2,1)S(1)} %pad_maximum_fusion.2.refs_0_), channel_id=1, source_target_pairs={{0,1},{1,0},{2,3},{3,2},{4,5},{5,4},{6,7},{7,6},{8,9},{9,8},{10,11... | collective-permute-start | bytes 1032200 | tf_op jit(solution)/shard_map/blk_early_1/ppermute | solution.py:26
  13.1 1.4 %collective-permute-start.7 = (bf16[8,7168]{1,0:T(8,128)(2,1)S(1)}, bf16[8,7168]{1,0:T(8,128)(2,1)S(1)}, u32[]{:S(2)}, u32[]{:S(2)}) collective-permute-start(bf16[8,7168]{1,0:T(8,128)(2,1)S(1)} %get-tuple-element.49), channel_id=1, source_target_pairs={{0,12},{2,14},{4,8},{6,10},{8,4},{10,6},{12,0},{14,2},{16,28},{18,... | collective-permute-start | bytes 344072 | tf_op jit(solution)/shard_map/go_leave_6/ppermute | solution.py:20
  14.5 3.5 %collective-permute-start.9 = (bf16[8,7168]{1,0:T(8,128)(2,1)S(1)}, bf16[8,7168]{1,0:T(8,128)(2,1)S(1)}, u32[]{:S(2)}, u32[]{:S(2)}) collective-permute-start(bf16[8,7168]{1,0:T(8,128)(2,1)S(1)} %get-tuple-element.52), channel_id=1, source_target_pairs={{0,28},{2,30},{4,24},{6,26},{8,20},{10,22},{12,16},{14,18},{16,12}... | collective-permute-start | bytes 344072 | tf_op jit(solution)/shard_map/go_leave_14/ppermute | solution.py:20
  18.1 2.7 %collective-permute-done.4 = bf16[8,7168]{1,0:T(8,128)(2,1)S(1)} collective-permute-done((bf16[8,7168]{1,0:T(8,128)(2,1)S(1)}, bf16[8,7168]{1,0:T(8,128)(2,1)S(1)}, u32[]{:S(2)}, u32[]{:S(2)}) %collective-permute-start.4) | collective-permute-done | bytes 114720 | tf_op jit(solution)/shard_map/go_stay_8/ppermute | solution.py:20
  20.7 2.6 %collective-permute-done.7.refs_1_ = bf16[8,7168]{1,0:T(8,128)(2,1)S(1)} collective-permute-done((bf16[8,7168]{1,0:T(8,128)(2,1)S(1)}, bf16[8,7168]{1,0:T(8,128)(2,1)S(1)}, u32[]{:S(2)}, u32[]{:S(2)}) %collective-permute-start.7) | collective-permute-done | bytes 114720 | tf_op jit(solution)/shard_map/go_leave_6/ppermute | solution.py:20
  24.1 1.6 %collective-permute-start.8 = (bf16[16,7168]{1,0:T(8,128)(2,1)S(1)}, bf16[16,7168]{1,0:T(8,128)(2,1)S(1)}, u32[]{:S(2)}, u32[]{:S(2)}) collective-permute-start(bf16[16,7168]{1,0:T(8,128)(2,1)S(1)} %constant_dynamic-update-slice_fusion.refs_1_), channel_id=1, source_target_pairs={{0,1},{1,0},{2,3},{3,2},{4,5},{5,4},{6,7},{7,6},{8,9},{9,8},{10,11... | collective-permute-start | bytes 688136 | tf_op jit(solution)/shard_map/blk_late_1/ppermute | solution.py:26
  25.7 5.3 %shard_map.66.refs_4_.refs_8_ = bf16[1,7168,1024]{2,1,0:T(8,128)(2,1)S(1)} custom-call(bf16[1,7168,1024]{2,1,0:T(8,128)(2,1)} %refs_0_), custom_call_target="tpu_custom_call" | custom-call | bytes 14680064 | tf_op jit(solution)/shard_map/pallas_call | solution.py:165
  31.1 1.3 %collective-permute-start.13 = (bf16[16,7168]{1,0:T(8,128)(2,1)S(1)}, bf16[16,7168]{1,0:T(8,128)(2,1)S(1)}, u32[]{:S(2)}, u32[]{:S(2)}) collective-permute-start(bf16[16,7168]{1,0:T(8,128)(2,1)S(1)} %pad_maximum_fusion.3.refs_2_.refs_3_), channel_id=1, source_target_pairs={{0,1},{1,0},{2,3},{3,2},{4,5},{5,4},{6,7},{7,6},{8,9},{9,8},{10,11... | collective-permute-start | bytes 688136 | tf_op jit(solution)/shard_map/blk_most_1/ppermute | solution.py:26
  33.2 7.4 %shard_map.67 = (bf16[64,1024]{1,0:T(8,128)(2,1)S(1)}, bf16[1,7168,1024]{2,1,0:T(8,128)(2,1)S(1)}) custom-call(bf16[24,7168]{1,0:T(8,128)(2,1)S(1)} %pad_maximum_fusion.2.refs_0_, bf16[16,7168]{1,0:T(8,128)(2,1)S(1)} %constant_dynamic-update-slice_fusion.refs_1_, bf16[24,7168]{1,0:T(8,128)(2,1)S(1)} %collective-permute-done.6.refs_2_.refs_4_, ...), custom_call_target="tpu_custom_call" | custom-call | flops 1879048192 | bytes 1048576 | tf_op jit(solution)/shard_map/pallas_call | solution.py:230
  40.6 1.3 %collective-permute-start.11 = (bf16[64,1024]{1,0:T(8,128)(2,1)S(1)}, bf16[64,1024]{1,0:T(8,128)(2,1)S(1)}, u32[]{:S(2)}, u32[]{:S(2)}) collective-permute-start(bf16[64,1024]{1,0:T(8,128)(2,1)S(1)} %get-tuple-element.60.refs_0_), channel_id=1, source_target_pairs={{0,1},{1,0},{2,3},{3,2},{4,5},{5,4},{6,7},{7,6},{8,9},{9,8},{10,11... | collective-permute-start | bytes 393224 | tf_op jit(solution)/shard_map/hidden_stay_1/ppermute | solution.py:26
  41.9 5.8 %shard_map.68.refs_2_ = bf16[64,1024]{1,0:T(8,128)(2,1)S(1)} custom-call(bf16[24,7168]{1,0:T(8,128)(2,1)S(1)} %pad_maximum_fusion.2.refs_0_, bf16[8,7168]{1,0:T(8,128)(2,1)S(1)} %collective-permute-done.7.refs_1_, bf16[16,7168]{1,0:T(8,128)(2,1)S(1)} %pad_maximum_fusion.3.refs_2_.refs_3_, bf16[16,7168]{1,0:T(8,128)(2,1)S(1)} %pad_maximum_fusion.3.refs_2_.refs_3_, ...), custom_call_target="tpu_custom_call" | custom-call | flops 1879048192 | bytes 1048576 | tf_op jit(solution)/shard_map/pallas_call | solution.py:230
  47.8 0.8 collective-permute-start.14
  48.6 4.1 %shard_map.69.refs_4_ = bf16[1,2048,2560]{2,1,0:T(8,128)(2,1)S(1)} custom-call(bf16[1,2048,3584]{2,1,0:T(8,128)(2,1)} %refs_5_.2), custom_call_target="tpu_custom_call" | custom-call | bytes 10485760 | tf_op jit(solution)/shard_map/pallas_call | solution.py:136
  52.8 3.3 %shard_map.70 = bf16[128,3584]{1,0:T(8,128)(2,1)S(1)} custom-call(s32[1]{0:T(128)} %bitcast.place.refs_0_, bf16[64,1024]{1,0:T(8,128)(2,1)S(1)} %get-tuple-element.60.refs_0_, bf16[64,1024]{1,0:T(8,128)(2,1)S(1)} %collective-permute-done.11.refs_1_, bf16[64,1024]{1,0:T(8,128)(2,1)S(1)} %shard_map.68.refs_2_, ...), custom_call_target="tpu_custom_call" | custom-call | flops 1879048192 | bytes 1441792 | tf_op jit(solution)/shard_map/pallas_call | solution.py:280
  56.3 1.3 %collective-permute-start.15 = (bf16[48,3584]{1,0:T(8,128)(2,1)S(1)}, bf16[48,3584]{1,0:T(8,128)(2,1)S(1)}, u32[]{:S(2)}, u32[]{:S(2)}) collective-permute-start(bf16[48,3584]{1,0:T(8,128)(2,1)S(1)} %get-tuple-element.88), channel_id=1, source_target_pairs={{0,1},{1,0},{2,3},{3,2},{4,5},{5,4},{6,7},{7,6},{8,9},{9,8},{10,11... | collective-permute-start | bytes 1032200 | tf_op jit(solution)/shard_map/own_front_1/ppermute | solution.py:26
  57.6 3.5 %collective-permute-start.16 = (bf16[2,8,3584]{2,1,0:T(8,128)(2,1)S(1)}, bf16[2,8,3584]{2,1,0:T(8,128)(2,1)S(1)}, u32[]{:S(2)}, u32[]{:S(2)}) collective-permute-start(bf16[2,8,3584]{2,1,0:T(8,128)(2,1)S(1)} %get-tuple-element.89), channel_id=1, source_target_pairs={{0,28},{2,30},{4,24},{6,26},{8,20},{10,22},{12,16},{14,18},{16,12}... | collective-permute-start | bytes 344072 | tf_op jit(solution)/shard_map/back_leave_14/ppermute | solution.py:20
  61.1 1.5 %collective-permute-start.18 = (bf16[2,8,3584]{2,1,0:T(8,128)(2,1)S(1)}, bf16[2,8,3584]{2,1,0:T(8,128)(2,1)S(1)}, u32[]{:S(2)}, u32[]{:S(2)}) collective-permute-start(bf16[2,8,3584]{2,1,0:T(8,128)(2,1)S(1)} %get-tuple-element.90), channel_id=1, source_target_pairs={{0,20},{2,22},{4,16},{6,18},{8,28},{10,30},{12,24},{14,26},{16,4},... | collective-permute-start | bytes 344072 | tf_op jit(solution)/shard_map/back_leave_10/ppermute | solution.py:20
  62.6 1.0 %collective-permute-done.15 = bf16[48,3584]{1,0:T(8,128)(2,1)S(1)} collective-permute-done((bf16[48,3584]{1,0:T(8,128)(2,1)S(1)}, bf16[48,3584]{1,0:T(8,128)(2,1)S(1)}, u32[]{:S(2)}, u32[]{:S(2)}) %collective-permute-start.15) | collective-permute-done | bytes 344096 | tf_op jit(solution)/shard_map/own_front_1/ppermute | solution.py:26
  63.6 3.3 %collective-permute-start.19 = (bf16[2,8,3584]{2,1,0:T(8,128)(2,1)S(1)}, bf16[2,8,3584]{2,1,0:T(8,128)(2,1)S(1)}, u32[]{:S(2)}, u32[]{:S(2)}) collective-permute-start(bf16[2,8,3584]{2,1,0:T(8,128)(2,1)S(1)} %get-tuple-element.86), channel_id=1, source_target_pairs={{0,16},{2,18},{4,20},{6,22},{8,24},{10,26},{12,28},{14,30},{16,0},... | collective-permute-start | bytes 344072 | tf_op jit(solution)/shard_map/back_stay_8/ppermute | solution.py:20
  66.9 5.3 %collective-permute-start.23 = (bf16[2,8,3584]{2,1,0:T(8,128)(2,1)S(1)}, bf16[2,8,3584]{2,1,0:T(8,128)(2,1)S(1)}, u32[]{:S(2)}, u32[]{:S(2)}) collective-permute-start(bf16[2,8,3584]{2,1,0:T(8,128)(2,1)S(1)} %get-tuple-element.68), channel_id=1, source_target_pairs={{0,12},{2,14},{4,8},{6,10},{8,4},{10,6},{12,0},{14,2},{16,28},{18,... | collective-permute-start | bytes 344072 | tf_op jit(solution)/shard_map/back_leave_6/ppermute | solution.py:20
  72.3 1.7 %collective-permute-done.18 = bf16[2,8,3584]{2,1,0:T(8,128)(2,1)S(1)} collective-permute-done((bf16[2,8,3584]{2,1,0:T(8,128)(2,1)S(1)}, bf16[2,8,3584]{2,1,0:T(8,128)(2,1)S(1)}, u32[]{:S(2)}, u32[]{:S(2)}) %collective-permute-start.18) | collective-permute-done | bytes 114720 | tf_op jit(solution)/shard_map/back_leave_10/ppermute | solution.py:20
  74.0 2.0 %collective-permute-start.20 = (bf16[2,8,3584]{2,1,0:T(8,128)(2,1)S(1)}, bf16[2,8,3584]{2,1,0:T(8,128)(2,1)S(1)}, u32[]{:S(2)}, u32[]{:S(2)}) collective-permute-start(bf16[2,8,3584]{2,1,0:T(8,128)(2,1)S(1)} %get-tuple-element.85), channel_id=1, source_target_pairs={{0,24},{2,26},{4,28},{6,30},{8,16},{10,18},{12,20},{14,22},{16,8},... | collective-permute-start | bytes 344072 | tf_op jit(solution)/shard_map/back_stay_12/ppermute | solution.py:20
  76.0 1.6 %collective-permute-done.19 = bf16[2,8,3584]{2,1,0:T(8,128)(2,1)S(1)} collective-permute-done((bf16[2,8,3584]{2,1,0:T(8,128)(2,1)S(1)}, bf16[2,8,3584]{2,1,0:T(8,128)(2,1)S(1)}, u32[]{:S(2)}, u32[]{:S(2)}) %collective-permute-start.19) | collective-permute-done | bytes 114720 | tf_op jit(solution)/shard_map/back_stay_8/ppermute | solution.py:20
  78.3 2.4 %collective-permute-done.17 = bf16[2,8,3584]{2,1,0:T(8,128)(2,1)S(1)} collective-permute-done((bf16[2,8,3584]{2,1,0:T(8,128)(2,1)S(1)}, bf16[2,8,3584]{2,1,0:T(8,128)(2,1)S(1)}, u32[]{:S(2)}, u32[]{:S(2)}) %collective-permute-start.17) | collective-permute-done | bytes 114720 | tf_op jit(solution)/shard_map/back_stay_4/ppermute | solution.py:20
  80.9 1.5 %collective-permute-done.24 = bf16[16,3584]{1,0:T(8,128)(2,1)S(1)} collective-permute-done((bf16[16,3584]{1,0:T(8,128)(2,1)S(1)}, bf16[16,3584]{1,0:T(8,128)(2,1)S(1)}, u32[]{:S(2)}, u32[]{:S(2)}) %collective-permute-start.24) | collective-permute-done | bytes 114720 | tf_op jit(solution)/shard_map/own_rear_1/ppermute | solution.py:26
  82.7 1.6 %collective-permute-done.25.refs_5_ = bf16[2,32,3584]{2,1,0:T(8,128)(2,1)S(1)} collective-permute-done((bf16[2,32,3584]{2,1,0:T(8,128)(2,1)S(1)}, bf16[2,32,3584]{2,1,0:T(8,128)(2,1)S(1)}, u32[]{:S(2)}, u32[]{:S(2)}) %collective-permute-start.25) | collective-permute-done | bytes 458784 | tf_op jit(solution)/shard_map/pair_leave_1/ppermute | solution.py:20
  84.4 1.4 %shard_map.71 = bf16[64,7168]{1,0:T(8,128)(2,1)} custom-call(s32[1]{0:T(128)} %bitcast.place.refs_0_, bf16[128,64]{1,0:T(8,128)(2,1)S(1)} %get-tuple-element.44.refs_1_, bf16[2,32,3584]{2,1,0:T(8,128)(2,1)S(1)} %pad_maximum_fusion.refs_2_, bf16[2,32,3584]{2,1,0:T(8,128)(2,1)S(1)} %collective-permute-done.21.refs_3_, ...), custom_call_target="tpu_custom_call" | custom-call | tf_op jit(solution)/shard_map/pallas_call | solution.py:315
  (43 shorter events, 5.4 us)
Async XLA Ops:
  0.0 2.8 %collective-permute-start.1 = (bf16[64,7168]{1,0:T(8,128)(2,1)}, bf16[64,7168]{1,0:T(8,128)(2,1)S(1)}, u32[]{:S(2)}, u32[]{:S(2)}) collective-permute-start(bf16[64,7168]{1,0:T(8,128)(2,1)} %refs_2_.1), channel_id=1, source_target_pairs={{0,2},{2,0},{4,6},{6,4},{8,10},{10,8},{12,14},{14,12},{16,18},{18,... | collective-permute-start | bytes 2752520 | tf_op jit(solution)/shard_map/tokens_1/ppermute | solution.py:20
  0.5 2.3 %collective-permute-start = (s32[8,64]{1,0:T(8,128)}, s32[8,64]{1,0:T(8,128)S(1)}, u32[]{:S(2)}, u32[]{:S(2)}) collective-permute-start(s32[8,64]{1,0:T(8,128)} %bitcast.17), channel_id=1, source_target_pairs={{0,2},{2,0},{4,6},{6,4},{8,10},{10,8},{12,14},{14,12},{16,18},{18,... | collective-permute-start | bytes 6152 | tf_op jit(solution)/shard_map/ids_1/ppermute | solution.py:20
  3.6 7.3 %collective-permute-start.2 = (bf16[8,7168]{1,0:T(8,128)(2,1)S(1)}, bf16[8,7168]{1,0:T(8,128)(2,1)S(1)}, u32[]{:S(2)}, u32[]{:S(2)}) collective-permute-start(bf16[8,7168]{1,0:T(8,128)(2,1)S(1)} %get-tuple-element.79), channel_id=1, source_target_pairs={{0,8},{2,10},{4,12},{6,14},{8,0},{10,2},{12,4},{14,6},{16,24},{18,... | collective-permute-start | bytes 344072 | tf_op jit(solution)/shard_map/go_stay_4/ppermute | solution.py:20
  6.6 4.9 %collective-permute-start.3 = (bf16[8,7168]{1,0:T(8,128)(2,1)S(1)}, bf16[8,7168]{1,0:T(8,128)(2,1)S(1)}, u32[]{:S(2)}, u32[]{:S(2)}) collective-permute-start(bf16[8,7168]{1,0:T(8,128)(2,1)S(1)} %get-tuple-element.78), channel_id=1, source_target_pairs={{0,4},{2,6},{4,0},{6,2},{8,12},{10,14},{12,8},{14,10},{16,20},{18,... | collective-permute-start | bytes 344072 | tf_op jit(solution)/shard_map/go_leave_2/ppermute | solution.py:20
  8.1 12.6 %collective-permute-start.4 = (bf16[8,7168]{1,0:T(8,128)(2,1)S(1)}, bf16[8,7168]{1,0:T(8,128)(2,1)S(1)}, u32[]{:S(2)}, u32[]{:S(2)}) collective-permute-start(bf16[8,7168]{1,0:T(8,128)(2,1)S(1)} %get-tuple-element.74), channel_id=1, source_target_pairs={{0,16},{2,18},{4,20},{6,22},{8,24},{10,26},{12,28},{14,30},{16,0},... | collective-permute-start | bytes 344072 | tf_op jit(solution)/shard_map/go_stay_8/ppermute | solution.py:20
  10.7 13.4 %collective-permute-start.5 = (bf16[8,7168]{1,0:T(8,128)(2,1)S(1)}, bf16[8,7168]{1,0:T(8,128)(2,1)S(1)}, u32[]{:S(2)}, u32[]{:S(2)}) collective-permute-start(bf16[8,7168]{1,0:T(8,128)(2,1)S(1)} %get-tuple-element.73), channel_id=1, source_target_pairs={{0,24},{2,26},{4,28},{6,30},{8,16},{10,18},{12,20},{14,22},{16,8},... | collective-permute-start | bytes 344072 | tf_op jit(solution)/shard_map/go_stay_12/ppermute | solution.py:20
  11.6 11.8 %collective-permute-start.6 = (bf16[24,7168]{1,0:T(8,128)(2,1)S(1)}, bf16[24,7168]{1,0:T(8,128)(2,1)S(1)}, u32[]{:S(2)}, u32[]{:S(2)}) collective-permute-start(bf16[24,7168]{1,0:T(8,128)(2,1)S(1)} %pad_maximum_fusion.2.refs_0_), channel_id=1, source_target_pairs={{0,1},{1,0},{2,3},{3,2},{4,5},{5,4},{6,7},{7,6},{8,9},{9,8},{10,11... | collective-permute-start | bytes 1032200 | tf_op jit(solution)/shard_map/blk_early_1/ppermute | solution.py:26
  13.1 10.2 %collective-permute-start.7 = (bf16[8,7168]{1,0:T(8,128)(2,1)S(1)}, bf16[8,7168]{1,0:T(8,128)(2,1)S(1)}, u32[]{:S(2)}, u32[]{:S(2)}) collective-permute-start(bf16[8,7168]{1,0:T(8,128)(2,1)S(1)} %get-tuple-element.49), channel_id=1, source_target_pairs={{0,12},{2,14},{4,8},{6,10},{8,4},{10,6},{12,0},{14,2},{16,28},{18,... | collective-permute-start | bytes 344072 | tf_op jit(solution)/shard_map/go_leave_6/ppermute | solution.py:20
  14.5 16.5 %collective-permute-start.9 = (bf16[8,7168]{1,0:T(8,128)(2,1)S(1)}, bf16[8,7168]{1,0:T(8,128)(2,1)S(1)}, u32[]{:S(2)}, u32[]{:S(2)}) collective-permute-start(bf16[8,7168]{1,0:T(8,128)(2,1)S(1)} %get-tuple-element.52), channel_id=1, source_target_pairs={{0,28},{2,30},{4,24},{6,26},{8,20},{10,22},{12,16},{14,18},{16,12}... | collective-permute-start | bytes 344072 | tf_op jit(solution)/shard_map/go_leave_14/ppermute | solution.py:20
  23.3 7.8 %collective-permute-start.10 = (bf16[8,7168]{1,0:T(8,128)(2,1)S(1)}, bf16[8,7168]{1,0:T(8,128)(2,1)S(1)}, u32[]{:S(2)}, u32[]{:S(2)}) collective-permute-start(bf16[8,7168]{1,0:T(8,128)(2,1)S(1)} %get-tuple-element.53), channel_id=1, source_target_pairs={{0,20},{2,22},{4,16},{6,18},{8,28},{10,30},{12,24},{14,26},{16,4},... | collective-permute-start | bytes 344072 | tf_op jit(solution)/shard_map/go_leave_10/ppermute | solution.py:20
  24.1 9.1 %collective-permute-start.8 = (bf16[16,7168]{1,0:T(8,128)(2,1)S(1)}, bf16[16,7168]{1,0:T(8,128)(2,1)S(1)}, u32[]{:S(2)}, u32[]{:S(2)}) collective-permute-start(bf16[16,7168]{1,0:T(8,128)(2,1)S(1)} %constant_dynamic-update-slice_fusion.refs_1_), channel_id=1, source_target_pairs={{0,1},{1,0},{2,3},{3,2},{4,5},{5,4},{6,7},{7,6},{8,9},{9,8},{10,11... | collective-permute-start | bytes 688136 | tf_op jit(solution)/shard_map/blk_late_1/ppermute | solution.py:26
  31.1 10.8 %collective-permute-start.13 = (bf16[16,7168]{1,0:T(8,128)(2,1)S(1)}, bf16[16,7168]{1,0:T(8,128)(2,1)S(1)}, u32[]{:S(2)}, u32[]{:S(2)}) collective-permute-start(bf16[16,7168]{1,0:T(8,128)(2,1)S(1)} %pad_maximum_fusion.3.refs_2_.refs_3_), channel_id=1, source_target_pairs={{0,1},{1,0},{2,3},{3,2},{4,5},{5,4},{6,7},{7,6},{8,9},{9,8},{10,11... | collective-permute-start | bytes 688136 | tf_op jit(solution)/shard_map/blk_most_1/ppermute | solution.py:26
  32.4 9.5 %collective-permute-start.12 = (bf16[8,7168]{1,0:T(8,128)(2,1)S(1)}, bf16[8,7168]{1,0:T(8,128)(2,1)S(1)}, u32[]{:S(2)}, u32[]{:S(2)}) collective-permute-start(bf16[8,7168]{1,0:T(8,128)(2,1)S(1)} %collective-permute-done.7.refs_1_), channel_id=1, source_target_pairs={{0,1},{1,0},{2,3},{3,2},{4,5},{5,4},{6,7},{7,6},{8,9},{9,8},{10,11... | collective-permute-start | bytes 344072 | tf_op jit(solution)/shard_map/blk_last_1/ppermute | solution.py:26
  40.6 7.2 %collective-permute-start.11 = (bf16[64,1024]{1,0:T(8,128)(2,1)S(1)}, bf16[64,1024]{1,0:T(8,128)(2,1)S(1)}, u32[]{:S(2)}, u32[]{:S(2)}) collective-permute-start(bf16[64,1024]{1,0:T(8,128)(2,1)S(1)} %get-tuple-element.60.refs_0_), channel_id=1, source_target_pairs={{0,1},{1,0},{2,3},{3,2},{4,5},{5,4},{6,7},{7,6},{8,9},{9,8},{10,11... | collective-permute-start | bytes 393224 | tf_op jit(solution)/shard_map/hidden_stay_1/ppermute | solution.py:26
  47.8 5.0 %collective-permute-start.14 = (bf16[64,1024]{1,0:T(8,128)(2,1)S(1)}, bf16[64,1024]{1,0:T(8,128)(2,1)S(1)}, u32[]{:S(2)}, u32[]{:S(2)}) collective-permute-start(bf16[64,1024]{1,0:T(8,128)(2,1)S(1)} %shard_map.68.refs_2_), channel_id=1, source_target_pairs={{0,1},{1,0},{2,3},{3,2},{4,5},{5,4},{6,7},{7,6},{8,9},{9,8},{10,11... | collective-permute-start | bytes 393224 | tf_op jit(solution)/shard_map/hidden_leave_1/ppermute | solution.py:26
  56.3 7.3 %collective-permute-start.15 = (bf16[48,3584]{1,0:T(8,128)(2,1)S(1)}, bf16[48,3584]{1,0:T(8,128)(2,1)S(1)}, u32[]{:S(2)}, u32[]{:S(2)}) collective-permute-start(bf16[48,3584]{1,0:T(8,128)(2,1)S(1)} %get-tuple-element.88), channel_id=1, source_target_pairs={{0,1},{1,0},{2,3},{3,2},{4,5},{5,4},{6,7},{7,6},{8,9},{9,8},{10,11... | collective-permute-start | bytes 1032200 | tf_op jit(solution)/shard_map/own_front_1/ppermute | solution.py:26
  57.6 9.4 %collective-permute-start.16 = (bf16[2,8,3584]{2,1,0:T(8,128)(2,1)S(1)}, bf16[2,8,3584]{2,1,0:T(8,128)(2,1)S(1)}, u32[]{:S(2)}, u32[]{:S(2)}) collective-permute-start(bf16[2,8,3584]{2,1,0:T(8,128)(2,1)S(1)} %get-tuple-element.89), channel_id=1, source_target_pairs={{0,28},{2,30},{4,24},{6,26},{8,20},{10,22},{12,16},{14,18},{16,12}... | collective-permute-start | bytes 344072 | tf_op jit(solution)/shard_map/back_leave_14/ppermute | solution.py:20
  61.1 12.9 %collective-permute-start.18 = (bf16[2,8,3584]{2,1,0:T(8,128)(2,1)S(1)}, bf16[2,8,3584]{2,1,0:T(8,128)(2,1)S(1)}, u32[]{:S(2)}, u32[]{:S(2)}) collective-permute-start(bf16[2,8,3584]{2,1,0:T(8,128)(2,1)S(1)} %get-tuple-element.90), channel_id=1, source_target_pairs={{0,20},{2,22},{4,16},{6,18},{8,28},{10,30},{12,24},{14,26},{16,4},... | collective-permute-start | bytes 344072 | tf_op jit(solution)/shard_map/back_leave_10/ppermute | solution.py:20
  63.6 13.9 %collective-permute-start.19 = (bf16[2,8,3584]{2,1,0:T(8,128)(2,1)S(1)}, bf16[2,8,3584]{2,1,0:T(8,128)(2,1)S(1)}, u32[]{:S(2)}, u32[]{:S(2)}) collective-permute-start(bf16[2,8,3584]{2,1,0:T(8,128)(2,1)S(1)} %get-tuple-element.86), channel_id=1, source_target_pairs={{0,16},{2,18},{4,20},{6,22},{8,24},{10,26},{12,28},{14,30},{16,0},... | collective-permute-start | bytes 344072 | tf_op jit(solution)/shard_map/back_stay_8/ppermute | solution.py:20
  66.9 14.0 %collective-permute-start.22 = (bf16[2,8,3584]{2,1,0:T(8,128)(2,1)S(1)}, bf16[2,8,3584]{2,1,0:T(8,128)(2,1)S(1)}, u32[]{:S(2)}, u32[]{:S(2)}) collective-permute-start(bf16[2,8,3584]{2,1,0:T(8,128)(2,1)S(1)} %get-tuple-element.67), channel_id=1, source_target_pairs={{0,4},{2,6},{4,0},{6,2},{8,12},{10,14},{12,8},{14,10},{16,20},{18,... | collective-permute-start | bytes 344072 | tf_op jit(solution)/shard_map/back_leave_2/ppermute | solution.py:20
  66.9 14.0 %collective-permute-start.23 = (bf16[2,8,3584]{2,1,0:T(8,128)(2,1)S(1)}, bf16[2,8,3584]{2,1,0:T(8,128)(2,1)S(1)}, u32[]{:S(2)}, u32[]{:S(2)}) collective-permute-start(bf16[2,8,3584]{2,1,0:T(8,128)(2,1)S(1)} %get-tuple-element.68), channel_id=1, source_target_pairs={{0,12},{2,14},{4,8},{6,10},{8,4},{10,6},{12,0},{14,2},{16,28},{18,... | collective-permute-start | bytes 344072 | tf_op jit(solution)/shard_map/back_leave_6/ppermute | solution.py:20
  72.2 8.6 %collective-permute-start.17 = (bf16[2,8,3584]{2,1,0:T(8,128)(2,1)S(1)}, bf16[2,8,3584]{2,1,0:T(8,128)(2,1)S(1)}, u32[]{:S(2)}, u32[]{:S(2)}) collective-permute-start(bf16[2,8,3584]{2,1,0:T(8,128)(2,1)S(1)} %get-tuple-element.64), channel_id=1, source_target_pairs={{0,8},{2,10},{4,12},{6,14},{8,0},{10,2},{12,4},{14,6},{16,24},{18,... | collective-permute-start | bytes 344072 | tf_op jit(solution)/shard_map/back_stay_4/ppermute | solution.py:20
  74.0 6.8 %collective-permute-start.20 = (bf16[2,8,3584]{2,1,0:T(8,128)(2,1)S(1)}, bf16[2,8,3584]{2,1,0:T(8,128)(2,1)S(1)}, u32[]{:S(2)}, u32[]{:S(2)}) collective-permute-start(bf16[2,8,3584]{2,1,0:T(8,128)(2,1)S(1)} %get-tuple-element.85), channel_id=1, source_target_pairs={{0,24},{2,26},{4,28},{6,30},{8,16},{10,18},{12,20},{14,22},{16,8},... | collective-permute-start | bytes 344072 | tf_op jit(solution)/shard_map/back_stay_12/ppermute | solution.py:20
  77.6 4.9 %collective-permute-start.24 = (bf16[16,3584]{1,0:T(8,128)(2,1)S(1)}, bf16[16,3584]{1,0:T(8,128)(2,1)S(1)}, u32[]{:S(2)}, u32[]{:S(2)}) collective-permute-start(bf16[16,3584]{1,0:T(8,128)(2,1)S(1)} %get-tuple-element.92), channel_id=1, source_target_pairs={{0,1},{1,0},{2,3},{3,2},{4,5},{5,4},{6,7},{7,6},{8,9},{9,8},{10,11... | collective-permute-start | bytes 344072 | tf_op jit(solution)/shard_map/own_rear_1/ppermute | solution.py:26
  80.8 1.9 %collective-permute-start.21 = (bf16[2,32,3584]{2,1,0:T(8,128)(2,1)S(1)}, bf16[2,32,3584]{2,1,0:T(8,128)(2,1)S(1)}, u32[]{:S(2)}, u32[]{:S(2)}) collective-permute-start(bf16[2,32,3584]{2,1,0:T(8,128)(2,1)S(1)} %pad_maximum_fusion.refs_2_), channel_id=1, source_target_pairs={{0,2},{2,0},{4,6},{6,4},{8,10},{10,8},{12,14},{14,12},{16,18},{18,... | collective-permute-start | bytes 1376264 | tf_op jit(solution)/shard_map/pair_stay_1/ppermute | solution.py:20
  82.5 1.9 %collective-permute-start.25 = (bf16[2,32,3584]{2,1,0:T(8,128)(2,1)S(1)}, bf16[2,32,3584]{2,1,0:T(8,128)(2,1)S(1)}, u32[]{:S(2)}, u32[]{:S(2)}) collective-permute-start(bf16[2,32,3584]{2,1,0:T(8,128)(2,1)S(1)} %maximum_maximum_fusion.refs_4_), channel_id=1, source_target_pairs={{0,2},{2,0},{4,6},{6,4},{8,10},{10,8},{12,14},{14,12},{16,18},{18,... | collective-permute-start | bytes 1376264 | tf_op jit(solution)/shard_map/pair_leave_1/ppermute | solution.py:20
